TPU v7x, 256 devices: a whole 4x4x8 slice. The times are simulated.
256 devices in a mesh: dp: 2 (over x_lo), mp: 128 (over z, x_hi, y, core).
Axes of the slice: x: 4 (x_hi: 2, x_lo: 2; x = x_hi * 2 + x_lo), y: 4, z: 8, core: 2. Of those that a mesh axis runs over, the one named last changes fastest.
Arguments:
- tokens: bfloat16 [512, 4608], P('dp', 'mp'), may hold values from -6 to 6
- teacher: bfloat16 [512, 4608], P('dp', 'mp'), may hold values from -4 to 4
- gate_weight: bfloat16 [4608, 36864], P(None, 'mp'), may hold values from -0.09375 to 0.09375
- up_weight: bfloat16 [4608, 36864], P(None, 'mp'), may hold values from -0.09375 to 0.09375
- down_weight: bfloat16 [36864, 4608], P('mp'), may hold values from -0.125 to 0.125
Outputs:
- student: bfloat16 [512, 4608], P('dp', 'mp')
- grad_gate: bfloat16 [4608, 36864], P('dp', 'mp')
- grad_up: bfloat16 [4608, 36864], P('dp', 'mp')
- grad_down: bfloat16 [36864, 4608], P('mp', 'dp')
All inputs are finite; a program needn't handle non-finite values.
Results may differ from a plain program's by a relative error of at most 0.0085.
Values may be sent and summed in bfloat16 or wider, within the bound.
No kernel may reach another device: no remote copies, remote signals or barrier semaphores. Data moves between devices by JAX's collectives and lax.ppermute only.
A program may use at most 128 MiB of HBM per device.

v0:
```python
import math

import jax
import jax.numpy as jnp
from jax import lax
from jax.sharding import PartitionSpec as P


def shards(tokens, teacher, gate_weight, up_weight, down_weight):
    gathered = lax.all_gather(tokens, "mp", axis=1, tiled=True)
    gate = jnp.dot(gathered, gate_weight, preferred_element_type=jnp.float32)
    upper = jnp.dot(gathered, up_weight, preferred_element_type=jnp.float32)
    sigma = jax.nn.sigmoid(gate)
    hidden = (gate * sigma * upper).astype(jnp.bfloat16)
    partial_terms = jnp.dot(hidden, down_weight, preferred_element_type=jnp.float32)
    summed = lax.psum_scatter(partial_terms, "mp", scatter_dimension=1, tiled=True)
    student = summed.astype(jnp.bfloat16)
    factor = 1.0 / math.sqrt(tokens.shape[0] * lax.axis_size("dp"))
    errors = ((summed - teacher.astype(jnp.float32)) * factor).astype(jnp.bfloat16)
    all_errors = lax.all_gather(errors, "mp", axis=1, tiled=True)
    back = lax.dot_general(
        all_errors, down_weight, (((1,), (1,)), ((), ())), preferred_element_type=jnp.float32
    )
    up_back = (back * gate * sigma).astype(jnp.bfloat16)
    gate_back = (back * upper * sigma * (1.0 + gate * (1.0 - sigma))).astype(jnp.bfloat16)
    contract = (((0,), (0,)), ((), ()))
    gate_terms = lax.dot_general(gathered, gate_back, contract, preferred_element_type=jnp.float32)
    up_terms = lax.dot_general(gathered, up_back, contract, preferred_element_type=jnp.float32)
    down_terms = lax.dot_general(all_errors, hidden, contract, preferred_element_type=jnp.float32)
    grad_gate, grad_up, down_turned = (
        lax.psum_scatter(gate_terms, "dp", scatter_dimension=0, tiled=True),
        lax.psum_scatter(up_terms, "dp", scatter_dimension=0, tiled=True),
        lax.psum_scatter(down_terms, "dp", scatter_dimension=0, tiled=True),
    )
    grad_down = down_turned.T
    return (
        student,
        grad_gate.astype(jnp.bfloat16),
        grad_up.astype(jnp.bfloat16),
        grad_down.astype(jnp.bfloat16),
    )


def solution(mesh):
    return jax.shard_map(
        shards,
        mesh=mesh,
        in_specs=(P("dp", "mp"), P("dp", "mp"), P(None, "mp"), P(None, "mp"), P("mp", None)),
        out_specs=(P("dp", "mp"), P("dp", "mp"), P("dp", "mp"), P("mp", "dp")),
        check_vma=False,
    )
```

profile of v0, /device:TPU:1, one launch (start us, length us, event | category | flops | bytes accessed | tf_op | source)
XLA Modules:
  0.0 913.1 jit_solution(12888101198113061915)
XLA Ops:
  8.0 124.2 %all-gather.5.cloned.1.call-done = bf16[128,36,256]{2,1,0:T(8,128)(2,1)} async-done(((bf16[1,36,256]{2,1,0:T(8,128)(2,1)}), bf16[128,36,256]{2,1,0:T(8,128)(2,1)}) %all-gather.5.cloned.1.call-update) | async-done | bytes 2359312 | tf_op jit(solution)/shard_map/all_gather | solution.py:10
  132.1 4.7 reshape.9
  136.8 3.5 fusion.8
  140.8 1.6 multiply_convert_fusion.2
  143.0 3.8 fusion.6
  146.8 351.4 %fusion = f32[256,40]{0,1:T(8,128)S(1)} fusion(f32[256,4608]{0,1:T(8,128)} %fusion.6), kind=kCustom, calls=%all-reduce-scatter | all-reduce-scatter fusion | flops 1310721 | bytes 4760576
  498.2 1.3 collective-permute-start.11
  499.5 1.3 collective-permute-start.10
  500.8 1.9 collective-permute-start.12
  504.0 1.3 collective-permute-start.8
  505.3 22.6 %collective-permute-start.7 = (f32[256,40]{0,1:T(8,128)S(1)}, f32[256,40]{0,1:T(8,128)S(1)}, u32[]{:S(2)}, u32[]{:S(2)}) collective-permute-start(f32[256,40]{0,1:T(8,128)S(1)} %fusion), channel_id=1, source_target_pairs={{0,8},{1,9},{2,10},{3,11},{4,12},{5,13},{6,14},{7,15},{8,16},{9,17... | collective-permute-start | bytes 122888
  529.3 3.2 collective-permute-start.5
  532.5 3.4 collective-permute-start.4
  535.9 3.2 collective-permute-start.3
  539.0 3.6 collective-permute-start.2
  542.7 1.9 collective-permute-start.1
  544.7 2.5 collective-permute-start
  549.7 10.8 %concatenate = f32[256,548]{0,1:T(8,128)S(1)} concatenate(f32[256,28]{0,1:T(8,128)} %collective-permute-done.12, f32[256,40]{0,1:T(8,128)} %copy-done.7, f32[256,40]{0,1:T(8,128)} %copy-done.8, f32[256,40]{0,1:T(8,128)} %copy-done.9, f32[256,40]{0,1:T(8,128)} %copy-done.10, f32[256,40]{0,1:T(8,128)} %copy-done.11, f32[256,40]{0,1:T(8,128)} %copy-done.12, f32[256,40]{0,1:T(8,128)} %copy-done.13, ...), dimensions={1} | concatenate | bytes 1122304
  560.6 1.4 fusion.3
  562.0 113.6 %all-gather.7.cloned.1.call-done = bf16[128,36,256]{2,1,0:T(8,128)(2,1)} async-done(((bf16[1,36,256]{2,1,0:T(8,128)(2,1)}), bf16[128,36,256]{2,1,0:T(8,128)(2,1)}) %all-gather.7.cloned.1.call-update) | async-done | bytes 2359312 | tf_op jit(solution)/shard_map/all_gather | solution.py:20
  675.6 4.7 reshape.11
  680.3 2.7 fusion.9
  683.0 3.2 convolution_bitcast_fusion.1
  687.2 5.0 fusion.7
  692.2 4.9 convolution_bitcast_fusion
  697.2 1.4 dynamic-slice_convert_fusion
  698.6 55.2 %reduce-scatter.6.cloned.1.call-done = f32[2304,288]{0,1:T(8,128)} async-done(((f32[4608,288]{0,1:T(8,128)}), f32[2304,288]{0,1:T(8,128)}) %reduce-scatter.6.cloned.1.call-update) | async-done | bytes 2654224 | tf_op jit(solution)/shard_map/reduce_scatter | solution.py:31
  753.8 2.9 convert_element_type.35
  756.8 72.0 %reduce-scatter.10.cloned.1.call-done = f32[2304,288]{0,1:T(8,128)} async-done(((f32[4608,288]{0,1:T(8,128)}), f32[2304,288]{0,1:T(8,128)}) %reduce-scatter.10.cloned.1.call-update) | async-done | bytes 2654224 | tf_op jit(solution)/shard_map/reduce_scatter | solution.py:33
  828.7 2.9 convert_bitcast_fusion
  831.7 72.0 %reduce-scatter.8.cloned.1.call-done = f32[2304,288]{0,1:T(8,128)} async-done(((f32[4608,288]{0,1:T(8,128)}), f32[2304,288]{0,1:T(8,128)}) %reduce-scatter.8.cloned.1.call-update) | async-done | bytes 2654224 | tf_op jit(solution)/shard_map/reduce_scatter | solution.py:32
  903.6 2.9 convert_element_type.37
  (67 shorter events, 7.3 us)
Async XLA Ops:
  7.2 135.9 %copy-start = (bf16[288,4608]{1,0:T(8,128)(2,1)S(1)}, bf16[288,4608]{1,0:T(8,128)(2,1)}, u32[]{:S(2)}) copy-start(bf16[288,4608]{1,0:T(8,128)(2,1)} %param.9) | copy-start | bytes 7962628
  7.2 124.9 %all-gather.5.cloned.1.call-start = ((), (), s32[]{:S(2)}) async-start(), calls=%async_computation.6 | async-start | bytes 2641920 | tf_op jit(solution)/shard_map/all_gather | solution.py:10
  7.9 667.7 %all-gather.7.cloned.1.call-start = ((), (), s32[]{:S(2)}) async-start(), calls=%async_computation.7 | async-start | bytes 2641920 | tf_op jit(solution)/shard_map/all_gather | solution.py:20
  136.8 3.5 copy-start.1
  136.8 4.0 copy-start.19
  146.8 400.4 %copy-start.18 = (u32[256]{0:T(256)S(1)}, u32[256]{0:T(256)}, u32[]{:S(2)}) copy-start(u32[256]{0:T(256)} %constant.11) | copy-start | bytes 3076
  498.2 29.8 %collective-permute-start.11 = (f32[256,40]{0,1:T(8,128)S(1)}, f32[256,40]{0,1:T(8,128)S(1)}, u32[]{:S(2)}, u32[]{:S(2)}) collective-permute-start(f32[256,40]{0,1:T(8,128)S(1)} %fusion), channel_id=1, source_target_pairs={{0,12},{1,13},{2,14},{3,15},{4,16},{5,17},{6,18},{7,19},{8,20},{9,... | collective-permute-start | bytes 122888
  499.5 29.8 %collective-permute-start.10 = (f32[256,40]{0,1:T(8,128)S(1)}, f32[256,40]{0,1:T(8,128)S(1)}, u32[]{:S(2)}, u32[]{:S(2)}) collective-permute-start(f32[256,40]{0,1:T(8,128)S(1)} %fusion), channel_id=1, source_target_pairs={{0,11},{1,12},{2,13},{3,14},{4,15},{5,16},{6,17},{7,18},{8,19},{9,... | collective-permute-start | bytes 122888
  500.8 4.5 collective-permute-start.12
  502.7 29.8 %collective-permute-start.9 = (f32[256,40]{0,1:T(8,128)S(1)}, f32[256,40]{0,1:T(8,128)S(1)}, u32[]{:S(2)}, u32[]{:S(2)}) collective-permute-start(f32[256,40]{0,1:T(8,128)S(1)} %fusion), channel_id=1, source_target_pairs={{0,10},{1,11},{2,12},{3,13},{4,14},{5,15},{6,16},{7,17},{8,18},{9,... | collective-permute-start | bytes 122888
  504.0 31.9 %collective-permute-start.8 = (f32[256,40]{0,1:T(8,128)S(1)}, f32[256,40]{0,1:T(8,128)S(1)}, u32[]{:S(2)}, u32[]{:S(2)}) collective-permute-start(f32[256,40]{0,1:T(8,128)S(1)} %fusion), channel_id=1, source_target_pairs={{0,9},{1,10},{2,11},{3,12},{4,13},{5,14},{6,15},{7,16},{8,17},{9,1... | collective-permute-start | bytes 122888
  505.3 33.7 %collective-permute-start.7 = (f32[256,40]{0,1:T(8,128)S(1)}, f32[256,40]{0,1:T(8,128)S(1)}, u32[]{:S(2)}, u32[]{:S(2)}) collective-permute-start(f32[256,40]{0,1:T(8,128)S(1)} %fusion), channel_id=1, source_target_pairs={{0,8},{1,9},{2,10},{3,11},{4,12},{5,13},{6,14},{7,15},{8,16},{9,17... | collective-permute-start | bytes 122888
  528.0 20.5 %copy-start.7 = (f32[256,40]{0,1:T(8,128)}, f32[256,40]{0,1:T(8,128)S(1)}, u32[]{:S(2)}) copy-start(f32[256,40]{0,1:T(8,128)S(1)} %collective-permute-done.11) | copy-start | bytes 122884
  528.0 14.7 %collective-permute-start.6 = (f32[256,40]{0,1:T(8,128)S(1)}, f32[256,40]{0,1:T(8,128)S(1)}, u32[]{:S(2)}, u32[]{:S(2)}) collective-permute-start(f32[256,40]{0,1:T(8,128)S(1)} %fusion), channel_id=1, source_target_pairs={{0,7},{1,8},{2,9},{3,10},{4,11},{5,12},{6,13},{7,14},{8,15},{9,16}... | collective-permute-start | bytes 122888
  529.3 19.2 %copy-start.8 = (f32[256,40]{0,1:T(8,128)}, f32[256,40]{0,1:T(8,128)S(1)}, u32[]{:S(2)}) copy-start(f32[256,40]{0,1:T(8,128)S(1)} %collective-permute-done.10) | copy-start | bytes 122884
  529.3 15.4 %collective-permute-start.5 = (f32[256,40]{0,1:T(8,128)S(1)}, f32[256,40]{0,1:T(8,128)S(1)}, u32[]{:S(2)}, u32[]{:S(2)}) collective-permute-start(f32[256,40]{0,1:T(8,128)S(1)} %fusion), channel_id=1, source_target_pairs={{0,6},{1,7},{2,8},{3,9},{4,10},{5,11},{6,12},{7,13},{8,14},{9,15},... | collective-permute-start | bytes 122888
  532.5 16.1 %copy-start.9 = (f32[256,40]{0,1:T(8,128)}, f32[256,40]{0,1:T(8,128)S(1)}, u32[]{:S(2)}) copy-start(f32[256,40]{0,1:T(8,128)S(1)} %collective-permute-done.9) | copy-start | bytes 122884
  532.5 15.9 %collective-permute-start.4 = (f32[256,40]{0,1:T(8,128)S(1)}, f32[256,40]{0,1:T(8,128)S(1)}, u32[]{:S(2)}, u32[]{:S(2)}) collective-permute-start(f32[256,40]{0,1:T(8,128)S(1)} %fusion), channel_id=1, source_target_pairs={{0,5},{1,6},{2,7},{3,8},{4,9},{5,10},{6,11},{7,12},{8,13},{9,14},{... | collective-permute-start | bytes 122888
  535.9 12.7 %copy-start.10 = (f32[256,40]{0,1:T(8,128)}, f32[256,40]{0,1:T(8,128)S(1)}, u32[]{:S(2)}) copy-start(f32[256,40]{0,1:T(8,128)S(1)} %collective-permute-done.8) | copy-start | bytes 122884
  535.9 12.6 %collective-permute-start.3 = (f32[256,40]{0,1:T(8,128)S(1)}, f32[256,40]{0,1:T(8,128)S(1)}, u32[]{:S(2)}, u32[]{:S(2)}) collective-permute-start(f32[256,40]{0,1:T(8,128)S(1)} %fusion), channel_id=1, source_target_pairs={{0,4},{1,5},{2,6},{3,7},{4,8},{5,9},{6,10},{7,11},{8,12},{9,13},{1... | collective-permute-start | bytes 122888
  539.0 9.5 %copy-start.11 = (f32[256,40]{0,1:T(8,128)}, f32[256,40]{0,1:T(8,128)S(1)}, u32[]{:S(2)}) copy-start(f32[256,40]{0,1:T(8,128)S(1)} %collective-permute-done.7) | copy-start | bytes 122884
  539.0 9.4 %collective-permute-start.2 = (f32[256,40]{0,1:T(8,128)S(1)}, f32[256,40]{0,1:T(8,128)S(1)}, u32[]{:S(2)}, u32[]{:S(2)}) collective-permute-start(f32[256,40]{0,1:T(8,128)S(1)} %fusion), channel_id=1, source_target_pairs={{0,3},{1,4},{2,5},{3,6},{4,7},{5,8},{6,9},{7,10},{8,11},{9,12},{10... | collective-permute-start | bytes 122888
  542.7 5.8 copy-start.12
  542.7 5.8 collective-permute-start.1
  544.6 3.9 copy-start.13
  544.7 5.0 collective-permute-start
  560.5 115.1 %copy-start.3 = (f32[256,548]{0,1:T(8,128)}, f32[256,548]{0,1:T(8,128)S(1)}, u32[]{:S(2)}) copy-start(f32[256,548]{0,1:T(8,128)S(1)} %concatenate) | copy-start | bytes 1683460
  562.0 191.9 %reduce-scatter.6.cloned.1.call-start = ((), (), s32[]{:S(2)}) async-start(), calls=%async_computation.3 | async-start | bytes 7962624 | tf_op jit(solution)/shard_map/reduce_scatter | solution.py:31
  680.3 2.7 copy-start.2
  680.3 2.7 copy-start.6
  686.3 142.4 %reduce-scatter.10.cloned.1.call-start = ((), (), s32[]{:S(2)}) async-start(), calls=%async_computation.5 | async-start | bytes 7962624 | tf_op jit(solution)/shard_map/reduce_scatter | solution.py:33
  692.2 211.5 %reduce-scatter.8.cloned.1.call-start = ((), (), s32[]{:S(2)}) async-start(), calls=%async_computation.4 | async-start | bytes 7962624 | tf_op jit(solution)/shard_map/reduce_scatter | solution.py:32
  (6 other events, 4.0 us)
Sparse Core Ops, SparseCore 0:
  11.6 120.4 all-gather.4
  562.1 113.5 all-gather.6
  686.4 67.3 reduce-scatter.5
  756.2 72.4 reduce-scatter.9
  831.1 72.4 reduce-scatter.7
where the time goes:
time: 915 us; the launch traced here: 913 us
  waiting for transfers between devices  438 us (48%)
  blocking collectives  351 us (38%)
  starting transfers between devices  48.9 us (5%)
  local copies, waits for them, and re-layouts  25.5 us (3%)
  matrix products  24.6 us (3%)
  between operations  14.9 us (2%)
  other arithmetic  10.2 us (1%)
    unnamed x1, blocking collectives  351 us
    all_gather x1, waiting for transfers between devices, shards(): gathered = lax.all_gather(tokens, 'mp', axis=1, tiled=True)  124 us
    all_gather x1, waiting for transfers between devices, shards(): all_errors = lax.all_gather(errors, 'mp', axis=1, tiled=True)  114 us
    reduce_scatter x1, waiting for transfers between devices, shards(): lax.psum_scatter(up_terms, 'dp', scatter_dimension=0, tiled=True)  72 us
    reduce_scatter x1, waiting for transfers between devices, shards(): lax.psum_scatter(down_terms, 'dp', scatter_dimension=0, tiled=True)  72 us
    reduce_scatter x1, waiting for transfers between devices, shards(): lax.psum_scatter(gate_terms, 'dp', scatter_dimension=0, tiled=True)  55.2 us
    unnamed x13, starting transfers between devices  48.7 us
    unnamed x45, local copies, waits for them, and re-layouts  24 us
  transfers between devices with their start and end apart: 18, of which 5 were waited for; matrix products, arithmetic and copies ran while one was open for 2% of the time, Pallas kernels for 0%

commit v1 on v0

v1 whole, which is shorter than its diff:
```python
import math

import jax
import jax.numpy as jnp
from jax import lax
from jax.sharding import Mesh, PartitionSpec as P

BF = jnp.bfloat16
F32 = jnp.float32
ZX = ("z", "xh")


def swap(x, axis):
    return lax.ppermute(x, axis, [(0, 1), (1, 0)])


def shift(x, axis, k):
    n = lax.axis_size(axis)
    return lax.ppermute(x, axis, [(i, (i + k) % n) for i in range(n)])


def pair_block(x, c):
    xt = x.T
    half = xt.shape[1] // 2
    first, second = xt[:, :half], xt[:, half:]
    mine = jnp.where(c == 0, first, second)
    theirs = swap(jnp.where(c == 0, second, first), "c")
    low = jnp.where(c == 0, mine, theirs)
    high = jnp.where(c == 0, theirs, mine)
    return jnp.concatenate([low, high], axis=0)


def unpair_block(block, c):
    rows = block.shape[0] // 2
    low, high = block[:rows], block[rows:]
    mine = jnp.where(c == 0, low, high)
    theirs = swap(jnp.where(c == 0, high, low), "c")
    first = jnp.where(c == 0, mine, theirs)
    second = jnp.where(c == 0, theirs, mine)
    return jnp.concatenate([first, second], axis=1).T


def gather_half(block, y):
    groups = lax.axis_size("z") * lax.axis_size("xh")
    ny = lax.axis_size("y")
    copies = jnp.broadcast_to(block[None], (groups,) + block.shape)
    part = lax.all_to_all(copies, ZX, 0, 0)
    whole = jnp.zeros((groups, ny) + block.shape, block.dtype)
    whole = lax.dynamic_update_slice_in_dim(whole, part[:, None], y, 1)
    for k in range(1, ny):
        piece = shift(part, "y", k)
        whole = lax.dynamic_update_slice_in_dim(whole, piece[:, None], lax.rem(y - k + ny, ny), 1)
    return whole


def scatter_half(terms, y):
    ny = lax.axis_size("y")
    narrow = terms.astype(BF)
    total = lax.dynamic_index_in_dim(terms, y, 1, keepdims=False)
    for k in range(1, ny):
        sent = lax.dynamic_index_in_dim(narrow, lax.rem(y + k, ny), 1, keepdims=False)
        total = total + shift(sent, "y", k).astype(F32)
    pieces = lax.all_to_all(total.astype(BF), ZX, 0, 0)
    return jnp.sum(pieces.astype(F32), axis=0)


def shards(tokens, teacher, gate_weight, up_weight, down_weight):
    c, y, d = lax.axis_index("c"), lax.axis_index("y"), lax.axis_index("dp")
    features = gate_weight.shape[0]
    half = features // 2
    factor = 1.0 / math.sqrt(tokens.shape[0] * lax.axis_size("dp"))

    x_mine = gather_half(pair_block(tokens, c), y)
    teach = pair_block(teacher, c).astype(F32)
    shape4 = x_mine.shape
    x_mine = x_mine.reshape(features, -1)
    x_other = swap(x_mine, "c")
    x = jnp.concatenate([x_mine, x_other], axis=1)

    first = (((0,), (0,)), ((), ()))
    gate = lax.dot_general(x, gate_weight, first, preferred_element_type=F32)
    upper = lax.dot_general(x, up_weight, first, preferred_element_type=F32)
    sigma = jax.nn.sigmoid(gate)
    hidden = (gate * sigma * upper).astype(BF)

    terms = lax.dot_general(down_weight, hidden, (((0,), (1,)), ((), ())), preferred_element_type=F32)
    count = shape4[-1]
    received = swap(terms[:, count:].astype(BF), "c")
    pair = (terms[:, :count] + received.astype(F32)).reshape(shape4)
    summed = scatter_half(pair, y)
    student = unpair_block(summed.astype(BF), c)
    errors = ((summed - teach) * factor).astype(BF)

    e_mine = gather_half(errors, y).reshape(features, -1)
    e_other = swap(e_mine, "c")
    e = jnp.concatenate([e_mine, e_other], axis=1)
    back = lax.dot_general(e, down_weight, (((0,), (1,)), ((), ())), preferred_element_type=F32)
    up_back = (back * gate * sigma).astype(BF)
    gate_back = (back * upper * sigma * (1.0 + gate * (1.0 - sigma))).astype(BF)

    def other_half(z):
        return lax.dynamic_slice_in_dim(z, (1 - d) * half, half, 0)

    def own_half(z):
        return lax.dynamic_slice_in_dim(z, d * half, half, 0)

    xp_mine = swap(other_half(x_mine), "dp")
    xp = jnp.concatenate([xp_mine, swap(xp_mine, "c")], axis=1)
    ep_mine = swap(other_half(e_mine), "dp")
    ep = jnp.concatenate([ep_mine, swap(ep_mine, "c")], axis=1)
    xo, eo = own_half(x), own_half(e)
    hidden_p = swap(hidden, "dp")
    up_back_p = swap(up_back, "dp")
    gate_back_p = swap(gate_back, "dp")

    def dot(a, b, dims):
        return lax.dot_general(a, b, (dims, ((), ())), preferred_element_type=F32)

    grad_gate = dot(xo, gate_back, ((1,), (0,))) + dot(xp, gate_back_p, ((1,), (0,)))
    grad_up = dot(xo, up_back, ((1,), (0,))) + dot(xp, up_back_p, ((1,), (0,)))
    grad_down = dot(hidden, eo, ((0,), (1,))) + dot(hidden_p, ep, ((0,), (1,)))
    return student, grad_gate.astype(BF), grad_up.astype(BF), grad_down.astype(BF)


def solution(mesh):
    mp = ("z", "xh", "y", "c")
    fine = Mesh(mesh.devices.reshape(2, 8, 2, 4, 2), ("dp",) + mp)
    return jax.shard_map(
        shards,
        mesh=fine,
        in_specs=(P("dp", mp), P("dp", mp), P(None, mp), P(None, mp), P(mp, None)),
        out_specs=(P("dp", mp), P("dp", mp), P("dp", mp), P(mp, "dp")),
        check_vma=False,
    )
```

time: 915 us -> 166 us (0.18)
  waiting for transfers between devices: 438 us -> 66 us
  blocking collectives: 351 us -> 22 us
  local copies, waits for them, and re-layouts: 25.5 us -> 10.3 us
  between operations: 14.9 us -> 0.92 us
  matrix products: 24.6 us -> 12.3 us
    unnamed x1 -> x0, blocking collectives: 351 us -> none
    all_gather x2 -> x0, waiting for transfers between devices: 238 us -> none  [the longest x1 124 us: shards(): gathered = lax.all_gather(tokens, 'mp', axis=1, tiled=True)]
    reduce_scatter x3 -> x0, waiting for transfers between devices: 199 us -> none  [the longest x1 72 us: shards(): lax.psum_scatter(up_terms, 'dp', scatter_dimension=0, tiled=True)]
    unnamed x13 -> x0, starting transfers between devices: 48.7 us -> none
    ppermute x0 -> x22, waiting for transfers between devices: none -> 45.7 us  [the longest x9 31.8 us: shift(): return lax.ppermute(x, axis, [(i, (i + k) % n) for i in range(n)])]
    ppermute x0 -> x22, starting transfers between devices: none -> 37.8 us  [the longest x13 22.7 us: swap(): return lax.ppermute(x, axis, [(0, 1), (1, 0)])]
    all_to_all x0 -> x1, blocking collectives: none -> 22 us  [gather_half(): part = lax.all_to_all(copies, ZX, 0, 0)]
    unnamed x45 -> x23, local copies, waits for them, and re-layouts: 24 us -> 2.46 us
  transfers between devices with their start and end apart: 18 -> 24, of which waited for: 5 -> 18; matrix products, arithmetic and copies ran while one was open for 2% -> 7% of each run, Pallas kernels for 0% -> 0%
where the time goes in v1:
time: 166 us; the launch traced here: 165 us
  waiting for transfers between devices  66 us (40%)
  starting transfers between devices  45.4 us (27%)
  blocking collectives  22 us (13%)
  matrix products  12.3 us (7%)
  local copies, waits for them, and re-layouts  10.3 us (6%)
  other arithmetic  7.7 us (5%)
    ppermute x9, waiting for transfers between devices, shift(): return lax.ppermute(x, axis, [(i, (i + k) % n) for i in range(n)])  31.8 us
    ppermute x13, starting transfers between devices, swap(): return lax.ppermute(x, axis, [(0, 1), (1, 0)])  22.7 us
    all_to_all x1, blocking collectives, gather_half(): part = lax.all_to_all(copies, ZX, 0, 0)  22 us
    ppermute x9, starting transfers between devices, shift(): return lax.ppermute(x, axis, [(i, (i + k) % n) for i in range(n)])  15.1 us
    ppermute x13, waiting for transfers between devices, swap(): return lax.ppermute(x, axis, [(0, 1), (1, 0)])  13.9 us
    all_to_all x1, waiting for transfers between devices, gather_half(): part = lax.all_to_all(copies, ZX, 0, 0)  11.4 us
    all_to_all x1, waiting for transfers between devices, scatter_half(): pieces = lax.all_to_all(total.astype(BF), ZX, 0, 0)  8.86 us
    dot_general x6, matrix products, dot(): return lax.dot_general(a, b, (dims, ((), ())), preferred_element_type=F32)  7.63 us
  transfers between devices with their start and end apart: 24, of which 18 were waited for; matrix products, arithmetic and copies ran while one was open for 7% of the time, Pallas kernels for 0%

profile of v1, /device:TPU:1, one launch (start us, length us, event | category | flops | bytes accessed | tf_op | source)
XLA Modules:
  0.0 164.7 jit_solution(4865707975160035980)
XLA Ops:
  1.5 3.2 %collective-permute-start = (bf16[36,128]{1,0:T(8,128)(2,1)S(1)}, bf16[36,128]{1,0:T(8,128)(2,1)S(1)}, u32[]{:S(2)}, u32[]{:S(2)}) collective-permute-start(bf16[36,128]{1,0:T(8,128)(2,1)S(1)} %broadcast_select_fusion.10), channel_id=1, source_target_pairs={{0,1},{1,0},{2,3},{3,2},{4,5},{5,4},{6,7},{7,6},{8,9},{9,8},{10,11... | collective-permute-start | bytes 27656 | tf_op jit(solution)/shard_map/ppermute | solution.py:14
  6.4 22.0 %all_to_all.15 = bf16[16,72,128]{2,1,0:T(8,128)(2,1)S(1)} all-to-all(bf16[16,72,128]{2,1,0:T(8,128)(2,1)S(1)} %broadcast_in_dim.36), channel_id=1, replica_groups=mesh['dp'=2,'z'=8,'xh'=2,'y'=4,'c'=2] {'z','xh'}, dimensions={0} | all-to-all | bytes 589824 | tf_op jit(solution)/shard_map/all_to_all | solution.py:47
  29.7 2.6 %collective-permute-start.2 = (bf16[16,72,128]{2,1,0:T(8,128)(2,1)S(1)}, bf16[16,72,128]{2,1,0:T(8,128)(2,1)S(1)}, u32[]{:S(2)}, u32[]{:S(2)}) collective-permute-start(bf16[16,72,128]{2,1,0:T(8,128)(2,1)S(1)} %all_to_all.15), channel_id=1, source_target_pairs={{0,4},{2,6},{4,0},{6,2},{1,5},{3,7},{5,1},{7,3},{8,12},{10,14},{12... | collective-permute-start | bytes 884744 | tf_op jit(solution)/shard_map/ppermute | solution.py:19
  33.6 2.7 %collective-permute-done.1 = bf16[16,72,128]{2,1,0:T(8,128)(2,1)S(1)} collective-permute-done((bf16[16,72,128]{2,1,0:T(8,128)(2,1)S(1)}, bf16[16,72,128]{2,1,0:T(8,128)(2,1)S(1)}, u32[]{:S(2)}, u32[]{:S(2)}) %collective-permute-start.1) | collective-permute-done | bytes 294944 | tf_op jit(solution)/shard_map/ppermute | solution.py:19
  36.4 7.4 %collective-permute-done.2 = bf16[16,72,128]{2,1,0:T(8,128)(2,1)S(1)} collective-permute-done((bf16[16,72,128]{2,1,0:T(8,128)(2,1)S(1)}, bf16[16,72,128]{2,1,0:T(8,128)(2,1)S(1)}, u32[]{:S(2)}, u32[]{:S(2)}) %collective-permute-start.2) | collective-permute-done | bytes 294944 | tf_op jit(solution)/shard_map/ppermute | solution.py:19
  44.0 2.8 %collective-permute-start.4 = (bf16[4608,128]{1,0:T(8,128)(2,1)S(1)}, bf16[4608,128]{1,0:T(8,128)(2,1)S(1)}, u32[]{:S(2)}, u32[]{:S(2)}) collective-permute-start(bf16[4608,128]{1,0:T(8,128)(2,1)S(1)} %bitcast.64), channel_id=1, source_target_pairs={{0,1},{1,0},{2,3},{3,2},{4,5},{5,4},{6,7},{7,6},{8,9},{9,8},{10,11... | collective-permute-start | bytes 3538952 | tf_op jit(solution)/shard_map/ppermute | solution.py:14
  46.8 2.5 %collective-permute-done.4 = bf16[4608,128]{1,0:T(8,128)(2,1)S(1)} collective-permute-done((bf16[4608,128]{1,0:T(8,128)(2,1)S(1)}, bf16[4608,128]{1,0:T(8,128)(2,1)S(1)}, u32[]{:S(2)}, u32[]{:S(2)}) %collective-permute-start.4) | collective-permute-done | bytes 1179680 | tf_op jit(solution)/shard_map/ppermute | solution.py:14
  53.9 2.5 %collective-permute-done.5 = bf16[4608,128]{0,1:T(8,128)(2,1)S(1)} collective-permute-done((bf16[4608,128]{0,1:T(8,128)(2,1)S(1)}, bf16[4608,128]{0,1:T(8,128)(2,1)S(1)}, u32[]{:S(2)}, u32[]{:S(2)}) %collective-permute-start.5) | collective-permute-done | bytes 1179680 | tf_op jit(solution)/shard_map/ppermute | solution.py:14
  56.3 1.6 slice_add_fusion
  58.0 3.1 %copy.18 = f32[4608,128]{1,0:T(8,128)} copy(f32[4608,128]{0,1:T(8,128)} %slice_add_fusion) | data formatting | bytes 4718592 | tf_op jit(solution)/shard_map/add | solution.py:89
  61.0 1.8 %convert_element_type.59 = bf16[16,4,72,128]{3,2,1,0:T(8,128)(2,1)S(1)} convert(f32[16,4,72,128]{3,2,1,0:T(8,128)} %bitcast.70) | non-fusion elementwise | flops 589824 | bytes 3538944 | tf_op jit(solution)/shard_map/convert_element_type | solution.py:58
  63.8 2.1 %collective-permute-start.7 = (bf16[16,72,128]{2,1,0:T(8,128)(2,1)S(1)}, bf16[16,72,128]{2,1,0:T(8,128)(2,1)S(1)}, u32[]{:S(2)}, u32[]{:S(2)}) collective-permute-start(bf16[16,72,128]{2,1,0:T(8,128)(2,1)S(1)} %get-tuple-element.6), channel_id=1, source_target_pairs={{0,4},{2,6},{4,0},{6,2},{1,5},{3,7},{5,1},{7,3},{8,12},{10,14},{12... | collective-permute-start | bytes 884744 | tf_op jit(solution)/shard_map/ppermute | solution.py:19
  67.3 5.1 %collective-permute-done.6 = bf16[16,72,128]{2,1,0:T(8,128)(2,1)S(1)} collective-permute-done((bf16[16,72,128]{2,1,0:T(8,128)(2,1)S(1)}, bf16[16,72,128]{2,1,0:T(8,128)(2,1)S(1)}, u32[]{:S(2)}, u32[]{:S(2)}) %collective-permute-start.6) | collective-permute-done | bytes 294944 | tf_op jit(solution)/shard_map/ppermute | solution.py:19
  72.5 6.5 %collective-permute-done.7 = bf16[16,72,128]{2,1,0:T(8,128)(2,1)S(1)} collective-permute-done((bf16[16,72,128]{2,1,0:T(8,128)(2,1)S(1)}, bf16[16,72,128]{2,1,0:T(8,128)(2,1)S(1)}, u32[]{:S(2)}, u32[]{:S(2)}) %collective-permute-start.7) | collective-permute-done | bytes 294944 | tf_op jit(solution)/shard_map/ppermute | solution.py:19
  79.1 1.9 %fusion.15 = bf16[16,72,128]{2,1,0:T(8,128)(2,1)} fusion(bf16[16,72,128]{2,1,0:T(8,128)(2,1)S(1)} %collective-permute-done.8, bf16[16,72,128]{2,1,0:T(8,128)(2,1)S(1)} %collective-permute-done.7, bf16[16,72,128]{2,1,0:T(8,128)(2,1)S(1)} %collective-permute-done.6, f32[16,4,72,128]{3,2,1,0:T(8,128)} %bitcast.71, s32[]{:T(128)S(6)} %select_n.87), kind=kLoop, calls=%fused_computation.27 | loop fusion | flops 1032192 | bytes 1769476 | tf_op jit(solution)/shard_map/convert_element_type | solution.py:63
  81.0 3.6 %all-to-all-start.1 = ((bf16[16,72,128]{2,1,0:T(8,128)(2,1)}), bf16[16,72,128]{2,1,0:T(8,128)(2,1)S(1)}, u32[]{:S(2)}, u32[]{:S(2)}) async-start(bf16[16,72,128]{2,1,0:T(8,128)(2,1)} %fusion.15), calls=%async_computation.1 | async-start | bytes 589824 | tf_op jit(solution)/shard_map/all_to_all | solution.py:63
  84.6 1.9 %collective-permute-start.10 = (bf16[36,128]{1,0:T(8,128)(2,1)S(1)}, bf16[36,128]{1,0:T(8,128)(2,1)S(1)}, u32[]{:S(2)}, u32[]{:S(2)}) collective-permute-start(bf16[36,128]{1,0:T(8,128)(2,1)S(1)} %broadcast_select_fusion.2), channel_id=1, source_target_pairs={{0,1},{1,0},{2,3},{3,2},{4,5},{5,4},{6,7},{7,6},{8,9},{9,8},{10,11... | collective-permute-start | bytes 27656 | tf_op jit(solution)/shard_map/ppermute | solution.py:14
  87.4 8.9 %all-to-all-done.1 = bf16[16,72,128]{2,1,0:T(8,128)(2,1)S(1)} async-done(((bf16[16,72,128]{2,1,0:T(8,128)(2,1)}), bf16[16,72,128]{2,1,0:T(8,128)(2,1)S(1)}, u32[]{:S(2)}, u32[]{:S(2)}) %all-to-all-start.1) | async-done | bytes 294944 | tf_op jit(solution)/shard_map/all_to_all | solution.py:63
  97.0 4.1 %all-to-all-start.2 = ((bf16[16,72,128]{2,1,0:T(8,128)(2,1)}), bf16[16,72,128]{2,1,0:T(8,128)(2,1)S(1)}, u32[]{:S(2)}, u32[]{:S(2)}) async-start(bf16[16,72,128]{2,1,0:T(8,128)(2,1)} %broadcast_in_dim.41), calls=%async_computation.2 | async-start | bytes 589824 | tf_op jit(solution)/shard_map/all_to_all | solution.py:47
  101.1 11.4 %all-to-all-done.2 = bf16[16,72,128]{2,1,0:T(8,128)(2,1)S(1)} async-done(((bf16[16,72,128]{2,1,0:T(8,128)(2,1)}), bf16[16,72,128]{2,1,0:T(8,128)(2,1)S(1)}, u32[]{:S(2)}, u32[]{:S(2)}) %all-to-all-start.2) | async-done | bytes 294944 | tf_op jit(solution)/shard_map/all_to_all | solution.py:47
  112.5 2.9 %collective-permute-start.11 = (bf16[16,72,128]{2,1,0:T(8,128)(2,1)S(1)}, bf16[16,72,128]{2,1,0:T(8,128)(2,1)S(1)}, u32[]{:S(2)}, u32[]{:S(2)}) collective-permute-start(bf16[16,72,128]{2,1,0:T(8,128)(2,1)S(1)} %all-to-all-done.2), channel_id=1, source_target_pairs={{0,2},{2,4},{4,6},{6,0},{1,3},{3,5},{5,7},{7,1},{8,10},{10,12},{12... | collective-permute-start | bytes 884744 | tf_op jit(solution)/shard_map/ppermute | solution.py:19
  117.1 2.8 %collective-permute-start.12 = (bf16[16,72,128]{2,1,0:T(8,128)(2,1)S(1)}, bf16[16,72,128]{2,1,0:T(8,128)(2,1)S(1)}, u32[]{:S(2)}, u32[]{:S(2)}) collective-permute-start(bf16[16,72,128]{2,1,0:T(8,128)(2,1)S(1)} %all-to-all-done.2), channel_id=1, source_target_pairs={{0,4},{2,6},{4,0},{6,2},{1,5},{3,7},{5,1},{7,3},{8,12},{10,14},{12... | collective-permute-start | bytes 884744 | tf_op jit(solution)/shard_map/ppermute | solution.py:19
  121.2 6.5 %collective-permute-done.12 = bf16[16,72,128]{2,1,0:T(8,128)(2,1)S(1)} collective-permute-done((bf16[16,72,128]{2,1,0:T(8,128)(2,1)S(1)}, bf16[16,72,128]{2,1,0:T(8,128)(2,1)S(1)}, u32[]{:S(2)}, u32[]{:S(2)}) %collective-permute-start.12) | collective-permute-done | bytes 294944 | tf_op jit(solution)/shard_map/ppermute | solution.py:19
  127.8 2.4 %collective-permute-done.13 = bf16[16,72,128]{2,1,0:T(8,128)(2,1)S(1)} collective-permute-done((bf16[16,72,128]{2,1,0:T(8,128)(2,1)S(1)}, bf16[16,72,128]{2,1,0:T(8,128)(2,1)S(1)}, u32[]{:S(2)}, u32[]{:S(2)}) %collective-permute-start.13) | collective-permute-done | bytes 294944 | tf_op jit(solution)/shard_map/ppermute | solution.py:19
  133.2 3.9 %collective-permute-start.16 = (bf16[2304,128]{1,0:T(8,128)(2,1)}, bf16[2304,128]{1,0:T(8,128)(2,1)}, u32[]{:S(2)}, u32[]{:S(2)}) collective-permute-start(bf16[2304,128]{1,0:T(8,128)(2,1)} %collective-permute-done.15), channel_id=1, source_target_pairs={{0,1},{1,0},{2,3},{3,2},{4,5},{5,4},{6,7},{7,6},{8,9},{9,8},{10,11... | collective-permute-start | bytes 1769480 | tf_op jit(solution)/shard_map/ppermute | solution.py:14
  139.3 4.3 %collective-permute-done.20 = bf16[2304,128]{1,0:T(8,128)(2,1)} collective-permute-done((bf16[2304,128]{1,0:T(8,128)(2,1)}, bf16[2304,128]{1,0:T(8,128)(2,1)}, u32[]{:S(2)}, u32[]{:S(2)}) %collective-permute-start.20) | collective-permute-done | bytes 589856 | tf_op jit(solution)/shard_map/ppermute | solution.py:14
  143.6 6.1 %collective-permute-start.21 = (bf16[2304,128]{1,0:T(8,128)(2,1)}, bf16[2304,128]{1,0:T(8,128)(2,1)S(1)}, u32[]{:S(2)}, u32[]{:S(2)}) collective-permute-start(bf16[2304,128]{1,0:T(8,128)(2,1)} %collective-permute-done.20), channel_id=1, source_target_pairs={{0,1},{1,0},{2,3},{3,2},{4,5},{5,4},{6,7},{7,6},{8,9},{9,8},{10,11... | collective-permute-start | bytes 1769480 | tf_op jit(solution)/shard_map/ppermute | solution.py:14
  151.6 1.7 %fusion.9 = f32[288,2304]{1,0:T(8,128)S(1)} fusion(bf16[256,288]{0,1:T(8,128)(2,1)S(1)} %collective-permute-done.19, bf16[2304,128]{1,0:T(8,128)(2,1)S(1)} %collective-permute-done.21, bf16[2304,128]{1,0:T(8,128)(2,1)} %collective-permute-done.20), kind=kOutput, calls=%fused_computation.20 | convolution fusion | flops 342097920 | bytes 3981312 | tf_op jit(solution)/shard_map/dot_general | solution.py:117
  155.7 1.6 fusion.2
  157.3 2.0 %collective-permute-done.18 = bf16[256,288]{0,1:T(8,128)(2,1)S(1)} collective-permute-done((bf16[256,288]{0,1:T(8,128)(2,1)S(1)}, bf16[256,288]{0,1:T(8,128)(2,1)S(1)}, u32[]{:S(2)}, u32[]{:S(2)}) %collective-permute-start.18) | collective-permute-done | bytes 147488 | tf_op jit(solution)/shard_map/ppermute | solution.py:14
  159.9 1.6 fusion.1
  163.0 1.6 fusion
  (81 shorter events, 28.6 us)
Async XLA Ops:
  0.6 51.2 %copy-start = (bf16[288,4608]{1,0:T(8,128)(2,1)S(1)}, bf16[288,4608]{1,0:T(8,128)(2,1)}, u32[]{:S(2)}) copy-start(bf16[288,4608]{1,0:T(8,128)(2,1)} %param.9) | copy-start | bytes 7962628
  1.5 4.1 %collective-permute-start = (bf16[36,128]{1,0:T(8,128)(2,1)S(1)}, bf16[36,128]{1,0:T(8,128)(2,1)S(1)}, u32[]{:S(2)}, u32[]{:S(2)}) collective-permute-start(bf16[36,128]{1,0:T(8,128)(2,1)S(1)} %broadcast_select_fusion.10), channel_id=1, source_target_pairs={{0,1},{1,0},{2,3},{3,2},{4,5},{5,4},{6,7},{7,6},{8,9},{9,8},{10,11... | collective-permute-start | bytes 27656 | tf_op jit(solution)/shard_map/ppermute | solution.py:14
  28.4 7.9 %collective-permute-start.1 = (bf16[16,72,128]{2,1,0:T(8,128)(2,1)S(1)}, bf16[16,72,128]{2,1,0:T(8,128)(2,1)S(1)}, u32[]{:S(2)}, u32[]{:S(2)}) collective-permute-start(bf16[16,72,128]{2,1,0:T(8,128)(2,1)S(1)} %all_to_all.15), channel_id=1, source_target_pairs={{0,2},{2,4},{4,6},{6,0},{1,3},{3,5},{5,7},{7,1},{8,10},{10,12},{12... | collective-permute-start | bytes 884744 | tf_op jit(solution)/shard_map/ppermute | solution.py:19
  29.7 14.1 %collective-permute-start.2 = (bf16[16,72,128]{2,1,0:T(8,128)(2,1)S(1)}, bf16[16,72,128]{2,1,0:T(8,128)(2,1)S(1)}, u32[]{:S(2)}, u32[]{:S(2)}) collective-permute-start(bf16[16,72,128]{2,1,0:T(8,128)(2,1)S(1)} %all_to_all.15), channel_id=1, source_target_pairs={{0,4},{2,6},{4,0},{6,2},{1,5},{3,7},{5,1},{7,3},{8,12},{10,14},{12... | collective-permute-start | bytes 884744 | tf_op jit(solution)/shard_map/ppermute | solution.py:19
  32.3 11.6 %collective-permute-start.3 = (bf16[16,72,128]{2,1,0:T(8,128)(2,1)S(1)}, bf16[16,72,128]{2,1,0:T(8,128)(2,1)S(1)}, u32[]{:S(2)}, u32[]{:S(2)}) collective-permute-start(bf16[16,72,128]{2,1,0:T(8,128)(2,1)S(1)} %all_to_all.15), channel_id=1, source_target_pairs={{0,6},{2,0},{4,2},{6,4},{1,7},{3,1},{5,3},{7,5},{8,14},{10,8},{12,... | collective-permute-start | bytes 884744 | tf_op jit(solution)/shard_map/ppermute | solution.py:19
  33.4 15.9 %copy-start.8 = (bf16[4608,288]{0,1:T(8,128)(2,1)S(1)}, bf16[4608,288]{0,1:T(8,128)(2,1)}, u32[]{:S(2)}) copy-start(bf16[4608,288]{0,1:T(8,128)(2,1)} %param.7) | copy-start | bytes 7962628
  43.9 6.2 %copy-start.1 = (bf16[16,4,72,128]{3,2,1,0:T(8,128)(2,1)}, bf16[16,4,72,128]{3,2,1,0:T(8,128)(2,1)S(1)}, u32[]{:S(2)}) copy-start(bf16[16,4,72,128]{3,2,1,0:T(8,128)(2,1)S(1)} %bitcast_dynamic-update-slice_fusion.7) | copy-start | bytes 3538948
  43.9 6.3 %copy-start.9 = (bf16[4608,288]{0,1:T(8,128)(2,1)S(1)}, bf16[4608,288]{0,1:T(8,128)(2,1)}, u32[]{:S(2)}) copy-start(bf16[4608,288]{0,1:T(8,128)(2,1)} %param.8) | copy-start | bytes 7962628
  44.0 5.3 %collective-permute-start.4 = (bf16[4608,128]{1,0:T(8,128)(2,1)S(1)}, bf16[4608,128]{1,0:T(8,128)(2,1)S(1)}, u32[]{:S(2)}, u32[]{:S(2)}) collective-permute-start(bf16[4608,128]{1,0:T(8,128)(2,1)S(1)} %bitcast.64), channel_id=1, source_target_pairs={{0,1},{1,0},{2,3},{3,2},{4,5},{5,4},{6,7},{7,6},{8,9},{9,8},{10,11... | collective-permute-start | bytes 3538952 | tf_op jit(solution)/shard_map/ppermute | solution.py:14
  53.4 2.9 %collective-permute-start.5 = (bf16[4608,128]{0,1:T(8,128)(2,1)S(1)}, bf16[4608,128]{0,1:T(8,128)(2,1)S(1)}, u32[]{:S(2)}, u32[]{:S(2)}) collective-permute-start(bf16[4608,128]{0,1:T(8,128)(2,1)S(1)} %slice.79), channel_id=1, source_target_pairs={{0,1},{1,0},{2,3},{3,2},{4,5},{5,4},{6,7},{7,6},{8,9},{9,8},{10,11... | collective-permute-start | bytes 3538952 | tf_op jit(solution)/shard_map/ppermute | solution.py:14
  62.9 9.5 %collective-permute-start.6 = (bf16[16,72,128]{2,1,0:T(8,128)(2,1)S(1)}, bf16[16,72,128]{2,1,0:T(8,128)(2,1)S(1)}, u32[]{:S(2)}, u32[]{:S(2)}) collective-permute-start(bf16[16,72,128]{2,1,0:T(8,128)(2,1)S(1)} %get-tuple-element.4), channel_id=1, source_target_pairs={{0,2},{2,4},{4,6},{6,0},{1,3},{3,5},{5,7},{7,1},{8,10},{10,12},{12... | collective-permute-start | bytes 884744 | tf_op jit(solution)/shard_map/ppermute | solution.py:19
  63.8 15.2 %collective-permute-start.7 = (bf16[16,72,128]{2,1,0:T(8,128)(2,1)S(1)}, bf16[16,72,128]{2,1,0:T(8,128)(2,1)S(1)}, u32[]{:S(2)}, u32[]{:S(2)}) collective-permute-start(bf16[16,72,128]{2,1,0:T(8,128)(2,1)S(1)} %get-tuple-element.6), channel_id=1, source_target_pairs={{0,4},{2,6},{4,0},{6,2},{1,5},{3,7},{5,1},{7,3},{8,12},{10,14},{12... | collective-permute-start | bytes 884744 | tf_op jit(solution)/shard_map/ppermute | solution.py:19
  65.9 18.7 %copy-start.7 = (bf16[256,36]{0,1:T(8,128)(2,1)S(1)}, bf16[256,36]{0,1:T(8,128)(2,1)}, u32[]{:S(2)}) copy-start(bf16[256,36]{0,1:T(8,128)(2,1)} %param.6) | copy-start | bytes 55300
  65.9 13.1 %collective-permute-start.8 = (bf16[16,72,128]{2,1,0:T(8,128)(2,1)S(1)}, bf16[16,72,128]{2,1,0:T(8,128)(2,1)S(1)}, u32[]{:S(2)}, u32[]{:S(2)}) collective-permute-start(bf16[16,72,128]{2,1,0:T(8,128)(2,1)S(1)} %get-tuple-element.5), channel_id=1, source_target_pairs={{0,6},{2,0},{4,2},{6,4},{1,7},{3,1},{5,3},{7,5},{8,14},{10,8},{12,... | collective-permute-start | bytes 884744 | tf_op jit(solution)/shard_map/ppermute | solution.py:19
  81.0 15.2 %all-to-all-start.1 = ((bf16[16,72,128]{2,1,0:T(8,128)(2,1)}), bf16[16,72,128]{2,1,0:T(8,128)(2,1)S(1)}, u32[]{:S(2)}, u32[]{:S(2)}) async-start(bf16[16,72,128]{2,1,0:T(8,128)(2,1)} %fusion.15), calls=%async_computation.1 | async-start | bytes 589824 | tf_op jit(solution)/shard_map/all_to_all | solution.py:63
  84.6 2.7 %collective-permute-start.10 = (bf16[36,128]{1,0:T(8,128)(2,1)S(1)}, bf16[36,128]{1,0:T(8,128)(2,1)S(1)}, u32[]{:S(2)}, u32[]{:S(2)}) collective-permute-start(bf16[36,128]{1,0:T(8,128)(2,1)S(1)} %broadcast_select_fusion.2), channel_id=1, source_target_pairs={{0,1},{1,0},{2,3},{3,2},{4,5},{5,4},{6,7},{7,6},{8,9},{9,8},{10,11... | collective-permute-start | bytes 27656 | tf_op jit(solution)/shard_map/ppermute | solution.py:14
  97.0 15.5 %all-to-all-start.2 = ((bf16[16,72,128]{2,1,0:T(8,128)(2,1)}), bf16[16,72,128]{2,1,0:T(8,128)(2,1)S(1)}, u32[]{:S(2)}, u32[]{:S(2)}) async-start(bf16[16,72,128]{2,1,0:T(8,128)(2,1)} %broadcast_in_dim.41), calls=%async_computation.2 | async-start | bytes 589824 | tf_op jit(solution)/shard_map/all_to_all | solution.py:47
  112.5 8.7 %collective-permute-start.11 = (bf16[16,72,128]{2,1,0:T(8,128)(2,1)S(1)}, bf16[16,72,128]{2,1,0:T(8,128)(2,1)S(1)}, u32[]{:S(2)}, u32[]{:S(2)}) collective-permute-start(bf16[16,72,128]{2,1,0:T(8,128)(2,1)S(1)} %all-to-all-done.2), channel_id=1, source_target_pairs={{0,2},{2,4},{4,6},{6,0},{1,3},{3,5},{5,7},{7,1},{8,10},{10,12},{12... | collective-permute-start | bytes 884744 | tf_op jit(solution)/shard_map/ppermute | solution.py:19
  116.5 16.7 %collective-permute-start.15 = (bf16[2304,128]{1,0:T(8,128)(2,1)S(1)}, bf16[2304,128]{1,0:T(8,128)(2,1)}, u32[]{:S(2)}, u32[]{:S(2)}) collective-permute-start(bf16[2304,128]{1,0:T(8,128)(2,1)S(1)} %constant_dynamic-slice_fusion.1), channel_id=1, source_target_pairs={{0,128},{128,0},{1,129},{129,1},{2,130},{130,2},{3,131},{131,3},{4... | collective-permute-start | bytes 1769480 | tf_op jit(solution)/shard_map/ppermute | solution.py:14
  117.1 10.6 %collective-permute-start.12 = (bf16[16,72,128]{2,1,0:T(8,128)(2,1)S(1)}, bf16[16,72,128]{2,1,0:T(8,128)(2,1)S(1)}, u32[]{:S(2)}, u32[]{:S(2)}) collective-permute-start(bf16[16,72,128]{2,1,0:T(8,128)(2,1)S(1)} %all-to-all-done.2), channel_id=1, source_target_pairs={{0,4},{2,6},{4,0},{6,2},{1,5},{3,7},{5,1},{7,3},{8,12},{10,14},{12... | collective-permute-start | bytes 884744 | tf_op jit(solution)/shard_map/ppermute | solution.py:19
  119.9 10.2 %collective-permute-start.13 = (bf16[16,72,128]{2,1,0:T(8,128)(2,1)S(1)}, bf16[16,72,128]{2,1,0:T(8,128)(2,1)S(1)}, u32[]{:S(2)}, u32[]{:S(2)}) collective-permute-start(bf16[16,72,128]{2,1,0:T(8,128)(2,1)S(1)} %all-to-all-done.2), channel_id=1, source_target_pairs={{0,6},{2,0},{4,2},{6,4},{1,7},{3,1},{5,3},{7,5},{8,14},{10,8},{12,... | collective-permute-start | bytes 884744 | tf_op jit(solution)/shard_map/ppermute | solution.py:19
  132.0 11.6 %collective-permute-start.20 = (bf16[2304,128]{1,0:T(8,128)(2,1)}, bf16[2304,128]{1,0:T(8,128)(2,1)}, u32[]{:S(2)}, u32[]{:S(2)}) collective-permute-start(bf16[2304,128]{1,0:T(8,128)(2,1)} %constant_dynamic-slice_fusion), channel_id=1, source_target_pairs={{0,128},{128,0},{1,129},{129,1},{2,130},{130,2},{3,131},{131,3},{4... | collective-permute-start | bytes 1769480 | tf_op jit(solution)/shard_map/ppermute | solution.py:14
  133.2 16.5 %collective-permute-start.16 = (bf16[2304,128]{1,0:T(8,128)(2,1)}, bf16[2304,128]{1,0:T(8,128)(2,1)}, u32[]{:S(2)}, u32[]{:S(2)}) collective-permute-start(bf16[2304,128]{1,0:T(8,128)(2,1)} %collective-permute-done.15), channel_id=1, source_target_pairs={{0,1},{1,0},{2,3},{3,2},{4,5},{5,4},{6,7},{7,6},{8,9},{9,8},{10,11... | collective-permute-start | bytes 1769480 | tf_op jit(solution)/shard_map/ppermute | solution.py:14
  138.3 13.2 %collective-permute-start.19 = (bf16[256,288]{0,1:T(8,128)(2,1)S(1)}, bf16[256,288]{0,1:T(8,128)(2,1)S(1)}, u32[]{:S(2)}, u32[]{:S(2)}) collective-permute-start(bf16[256,288]{0,1:T(8,128)(2,1)S(1)} %get-tuple-element.17), channel_id=1, source_target_pairs={{0,128},{128,0},{1,129},{129,1},{2,130},{130,2},{3,131},{131,3},{4... | collective-permute-start | bytes 442376 | tf_op jit(solution)/shard_map/ppermute | solution.py:14
  138.7 14.5 %collective-permute-start.14 = (bf16[4608,128]{1,0:T(8,128)(2,1)S(1)}, bf16[4608,128]{1,0:T(8,128)(2,1)S(1)}, u32[]{:S(2)}, u32[]{:S(2)}) collective-permute-start(bf16[4608,128]{1,0:T(8,128)(2,1)S(1)} %bitcast.73), channel_id=1, source_target_pairs={{0,1},{1,0},{2,3},{3,2},{4,5},{5,4},{6,7},{7,6},{8,9},{9,8},{10,11... | collective-permute-start | bytes 3538952 | tf_op jit(solution)/shard_map/ppermute | solution.py:14
  139.0 11.9 %collective-permute-start.9 = (bf16[36,128]{1,0:T(8,128)(2,1)S(1)}, bf16[36,128]{1,0:T(8,128)(2,1)S(1)}, u32[]{:S(2)}, u32[]{:S(2)}) collective-permute-start(bf16[36,128]{1,0:T(8,128)(2,1)S(1)} %broadcast_select_fusion.6), channel_id=1, source_target_pairs={{0,1},{1,0},{2,3},{3,2},{4,5},{5,4},{6,7},{7,6},{8,9},{9,8},{10,11... | collective-permute-start | bytes 27656 | tf_op jit(solution)/shard_map/ppermute | solution.py:14
  143.6 7.9 %collective-permute-start.21 = (bf16[2304,128]{1,0:T(8,128)(2,1)}, bf16[2304,128]{1,0:T(8,128)(2,1)S(1)}, u32[]{:S(2)}, u32[]{:S(2)}) collective-permute-start(bf16[2304,128]{1,0:T(8,128)(2,1)} %collective-permute-done.20), channel_id=1, source_target_pairs={{0,1},{1,0},{2,3},{3,2},{4,5},{5,4},{6,7},{7,6},{8,9},{9,8},{10,11... | collective-permute-start | bytes 1769480 | tf_op jit(solution)/shard_map/ppermute | solution.py:14
  151.5 1.7 %copy-start.10 = (f32[256,288]{0,1:T(8,128)S(1)}, f32[256,288]{0,1:T(8,128)}, u32[]{:S(2)}) copy-start(f32[256,288]{0,1:T(8,128)} %get-tuple-element.18) | copy-start | bytes 884740
  154.1 5.2 %collective-permute-start.18 = (bf16[256,288]{0,1:T(8,128)(2,1)S(1)}, bf16[256,288]{0,1:T(8,128)(2,1)S(1)}, u32[]{:S(2)}, u32[]{:S(2)}) collective-permute-start(bf16[256,288]{0,1:T(8,128)(2,1)S(1)} %get-tuple-element.7), channel_id=1, source_target_pairs={{0,128},{128,0},{1,129},{129,1},{2,130},{130,2},{3,131},{131,3},{4... | collective-permute-start | bytes 442376 | tf_op jit(solution)/shard_map/ppermute | solution.py:14
  155.4 7.1 %collective-permute-start.17 = (bf16[256,288]{0,1:T(8,128)(2,1)S(1)}, bf16[256,288]{0,1:T(8,128)(2,1)S(1)}, u32[]{:S(2)}, u32[]{:S(2)}) collective-permute-start(bf16[256,288]{0,1:T(8,128)(2,1)S(1)} %get-tuple-element.8), channel_id=1, source_target_pairs={{0,128},{128,0},{1,129},{129,1},{2,130},{130,2},{3,131},{131,3},{4... | collective-permute-start | bytes 442376 | tf_op jit(solution)/shard_map/ppermute | solution.py:14
  157.3 2.6 %copy-start.2 = (bf16[16,4,72,128]{3,2,1,0:T(8,128)(2,1)S(1)}, bf16[16,4,72,128]{3,2,1,0:T(8,128)(2,1)}, u32[]{:S(2)}) copy-start(bf16[16,4,72,128]{3,2,1,0:T(8,128)(2,1)} %copy-done.1) | copy-start | bytes 3538948
  157.3 2.6 %copy-start.6 = (bf16[4608,128]{1,0:T(8,128)(2,1)S(1)}, bf16[4608,128]{1,0:T(8,128)(2,1)}, u32[]{:S(2)}) copy-start(bf16[4608,128]{1,0:T(8,128)(2,1)} %copy-done.5) | copy-start | bytes 3538948
  (3 other events, 3.7 us)

commit v2 on v1

v2 whole, which is shorter than its diff:
```python
import functools
import math

import jax
import jax.numpy as jnp
from jax import lax
from jax.experimental import pallas as pl
from jax.experimental.pallas import tpu as pltpu
from jax.experimental.layout import Layout, with_layout_constraint
from jax.sharding import Mesh, PartitionSpec as P

BF = jnp.bfloat16
F32 = jnp.float32
ZX = ("z", "xh")


def swap(x, axis):
    return lax.ppermute(x, axis, [(0, 1), (1, 0)])


def shift(x, axis, k):
    n = lax.axis_size(axis)
    return lax.ppermute(x, axis, [(i, (i + k) % n) for i in range(n)])


def pair_block(x, c):
    xt = x.T
    half = xt.shape[1] // 2
    first, second = xt[:, :half], xt[:, half:]
    mine = jnp.where(c == 0, first, second)
    theirs = swap(jnp.where(c == 0, second, first), "c")
    low = jnp.where(c == 0, mine, theirs)
    high = jnp.where(c == 0, theirs, mine)
    return jnp.concatenate([low, high], axis=0)


def unpair_block(block, c):
    rows = block.shape[0] // 2
    low, high = block[:rows], block[rows:]
    mine = jnp.where(c == 0, low, high)
    theirs = swap(jnp.where(c == 0, high, low), "c")
    first = jnp.where(c == 0, mine, theirs)
    second = jnp.where(c == 0, theirs, mine)
    return jnp.concatenate([first, second], axis=1).T


def gather_zx(block):
    groups = lax.axis_size("z") * lax.axis_size("xh")
    copies = jnp.broadcast_to(block[None], (groups,) + block.shape)
    return lax.all_to_all(copies, ZX, 0, 0)


def gather_y(part, y, axis, *meanwhile):
    ny = lax.axis_size("y")
    part = jnp.expand_dims(part, axis)
    pieces = {k: shift(part, "y", k) for k in (2, 1, 3)}
    whole = jnp.broadcast_to(part, part.shape[:axis] + (ny,) + part.shape[axis + 1 :])
    pieces[1], whole, *meanwhile = barrier(pieces[1], whole, *meanwhile)
    for k in (1, 3, 2):
        whole = lax.dynamic_update_slice_in_dim(whole, pieces[k], lax.rem(y - k + ny, ny), axis)
    return (whole, *meanwhile)


def dot(a, b, i, j):
    return lax.dot_general(a, b, (((i,), (j,)), ((), ())), preferred_element_type=F32)


def row_major(x):
    return with_layout_constraint(x, Layout(major_to_minor=tuple(range(x.ndim))))


def barrier(*values):
    return lax.optimization_barrier(values)


def regroup_kernel(rows, y_ref, w_ref, out_ref):
    ny = out_ref.shape[0]
    groups = out_ref.shape[2] // rows
    for p in range(ny):
        k = lax.rem(p + ny - y_ref[0], ny)
        for g in range(groups):
            start = (g * ny + p) * rows
            out_ref[k, :, g * rows : (g + 1) * rows] = w_ref[:, start : start + rows]


def regroup(weight, y, ny, rows):
    units, features = weight.shape
    block = 32
    return pl.pallas_call(
        functools.partial(regroup_kernel, rows),
        grid_spec=pltpu.PrefetchScalarGridSpec(
            num_scalar_prefetch=1,
            grid=(units // block,),
            in_specs=[pl.BlockSpec((block, features), lambda i, y: (i, 0))],
            out_specs=pl.BlockSpec((ny, block, features // ny), lambda i, y: (0, i, 0)),
        ),
        out_shape=jax.ShapeDtypeStruct((ny, units, features // ny), weight.dtype),
        cost_estimate=pl.CostEstimate(flops=0, bytes_accessed=4 * units * features, transcendentals=0),
        name="regroup",
    )(y.reshape(1), weight)


def shards(tokens, teacher, gate_weight, up_weight, down_weight):
    c, y, d = lax.axis_index("c"), lax.axis_index("y"), lax.axis_index("dp")
    ny = lax.axis_size("y")
    features, units = gate_weight.shape
    groups = lax.axis_size("z") * lax.axis_size("xh")
    rows = features // (groups * ny)
    half = features // 2
    factor = 1.0 / math.sqrt(tokens.shape[0] * lax.axis_size("dp"))

    block, down_weight = barrier(pair_block(tokens, c), down_weight)
    part = gather_zx(block)
    down = regroup(down_weight, y, ny, rows)
    part, down = barrier(part, down)
    (x_mine,) = gather_y(part, y, 1)
    x_mine = x_mine.reshape(features, -1)
    count = x_mine.shape[1]
    x = jnp.concatenate([x_mine, swap(x_mine, "c")], axis=1)

    gate = dot(gate_weight, x, 0, 0)
    upper = dot(up_weight, x, 0, 0)
    sigma = jax.nn.sigmoid(gate)
    silu = gate * sigma
    slope = (upper * sigma * (1.0 + gate * (1.0 - sigma))).astype(BF)
    hidden = (silu * upper).astype(BF)
    silu = silu.astype(BF)

    def pair(k):
        other = swap(row_major(dot(down[k], hidden[:, count:], 0, 0).astype(BF)), "c")
        return row_major(dot(down[k], hidden[:, :count], 0, 0)) + other.astype(F32)

    arrived = [shift(pair(k).astype(BF), "y", k) for k in (2, 1, 3)]
    total = pair(0)
    for piece in arrived:
        total = total + piece.astype(F32)
    held_p = swap(jnp.stack([hidden, silu, slope]), "dp")
    teach = pair_block(teacher, c).astype(F32)
    total, held_p, teach = barrier(total.astype(BF), held_p, teach)
    sums = lax.all_to_all(total.reshape(groups, rows, count), ZX, 0, 0)
    summed = jnp.sum(sums.astype(F32), axis=0)
    student = unpair_block(summed.astype(BF), c)
    errors = ((summed - teach) * factor).astype(BF)

    e_part = gather_zx(errors)
    xs = lax.dynamic_slice_in_dim(x_mine, (1 - d) * half, half, 0)
    e_part, student, xs = barrier(e_part, student, xs)
    keep, give = d * (groups // 2), (1 - d) * (groups // 2)
    e_got = swap(lax.dynamic_slice_in_dim(e_part, give, groups // 2, 0), "dp")
    xp_mine = swap(xs, "dp")
    e_pieces = {0: e_part, **{k: shift(e_part, "y", k) for k in (2, 1, 3)}}
    back = 0.0
    kept = {}
    for k in (0, 1, 3, 2):
        piece = e_pieces[k].reshape(groups * rows, count)
        other = swap(piece, "c")
        if k:
            other, back = barrier(other, back)
        piece = jnp.concatenate([piece, other], axis=1)
        kept[k] = lax.dynamic_slice_in_dim(piece.reshape(groups, rows, 2 * count), keep, groups // 2, 0)
        back = back + dot(down[(ny - k) % ny], piece, 1, 0)
    narrow, e_got = barrier(back.astype(BF), e_got)
    back_p = swap(narrow, "dp").astype(F32)
    got_pieces = {0: e_got, **{k: shift(e_got, "y", k) for k in (2, 1, 3)}}
    hidden_p, silu_p, slope_p = held_p[0], held_p[1].astype(F32), held_p[2].astype(F32)
    up_back = jnp.concatenate([(back * silu).astype(BF), (back_p * silu_p).astype(BF)], axis=1)
    gate_back = jnp.concatenate([(back * slope).astype(BF), (back_p * slope_p).astype(BF)], axis=1)

    def assembled(pieces):
        whole = jnp.broadcast_to(pieces[0][:, None], (groups // 2, ny) + pieces[0].shape[1:])
        for k in (1, 3, 2):
            whole = lax.dynamic_update_slice_in_dim(whole, pieces[k][:, None], lax.rem(y - k + ny, ny), 1)
        return whole.reshape(half, -1)

    eo, ep_mine = assembled(kept), assembled(got_pieces)
    errors_both = jnp.concatenate([eo, ep_mine, swap(ep_mine, "c")], axis=1)
    xo = lax.dynamic_slice_in_dim(x, d * half, half, 0)
    x_both = jnp.concatenate([xo, xp_mine, swap(xp_mine, "c")], axis=1)
    grad_gate = dot(x_both, gate_back, 1, 1)
    grad_up = dot(x_both, up_back, 1, 1)
    grad_down = dot(jnp.concatenate([hidden, hidden_p], axis=1), errors_both, 1, 1)
    return student, grad_gate.astype(BF), grad_up.astype(BF), grad_down.astype(BF)


def solution(mesh):
    mp = ("z", "xh", "y", "c")
    fine = Mesh(mesh.devices.reshape(2, 8, 2, 4, 2), ("dp",) + mp)
    return jax.shard_map(
        shards,
        mesh=fine,
        in_specs=(P("dp", mp), P("dp", mp), P(None, mp), P(None, mp), P(mp, None)),
        out_specs=(P("dp", mp), P("dp", mp), P("dp", mp), P(mp, "dp")),
        check_vma=False,
    )
```

time: 166 us -> 156 us (0.940)
  blocking collectives: 22 us -> 0 us
  starting transfers between devices: 45.4 us -> 58.5 us
  Pallas kernels: 0 us -> 7.72 us
  waiting for transfers between devices: 66 us -> 59.5 us
  local copies, waits for them, and re-layouts: 10.3 us -> 6.24 us
    all_to_all x1 -> x0, blocking collectives: 22 us -> none  [gather_half(): part = lax.all_to_all(copies, ZX, 0, 0)]
    all_to_all x2 -> x3, starting transfers between devices: 7.69 us -> 16.2 us  [the longest x2 12.6 us: gather_zx(): return lax.all_to_all(copies, ZX, 0, 0)]
    pallas_call x0 -> x1, Pallas kernels: none -> 7.72 us  [regroup(): pl.pallas_call(functools.partial(regroup_kernel, rows), grid_spec=pltpu.P...]
    ppermute x13 -> x18, waiting for transfers between devices: 13.9 us -> 6.19 us  [swap(): return lax.ppermute(x, axis, [(0, 1), (1, 0)])]
    all_to_all x2 -> x3, waiting for transfers between devices: 20.3 us -> 25.5 us  [the longest x2 16.1 us: gather_zx(): return lax.all_to_all(copies, ZX, 0, 0)]
    ppermute x13 -> x18, starting transfers between devices: 22.7 us -> 27.1 us  [swap(): return lax.ppermute(x, axis, [(0, 1), (1, 0)])]
    ppermute x9 -> x12, waiting for transfers between devices: 31.8 us -> 27.8 us  [shift(): return lax.ppermute(x, axis, [(i, (i + k) % n) for i in range(n)])]
    add x1 -> x0, local copies, waits for them, and re-layouts: 3.06 us -> none  [shards(): pair = (terms[:, :count] + received.astype(F32)).reshape(shape4)]
  transfers between devices with their start and end apart: 24 -> 33, of which waited for: 18 -> 15; matrix products, arithmetic and copies ran while one was open for 7% -> 12% of each run, Pallas kernels for 0% -> 5%
where the time goes in v2:
time: 156 us; the launch traced here: 155 us
  waiting for transfers between devices  59.5 us (38%)
  starting transfers between devices  58.5 us (38%)
  matrix products  13.8 us (9%)
  other arithmetic  8.07 us (5%)
  Pallas kernels  7.72 us (5%)
  local copies, waits for them, and re-layouts  6.24 us (4%)
    ppermute x12, waiting for transfers between devices, shift(): return lax.ppermute(x, axis, [(i, (i + k) % n) for i in range(n)])  27.8 us
    ppermute x18, starting transfers between devices, swap(): return lax.ppermute(x, axis, [(0, 1), (1, 0)])  27.1 us
    all_to_all x2, waiting for transfers between devices, gather_zx(): return lax.all_to_all(copies, ZX, 0, 0)  16.1 us
    ppermute x12, starting transfers between devices, shift(): return lax.ppermute(x, axis, [(i, (i + k) % n) for i in range(n)])  15.2 us
    dot_general x17, matrix products, dot(): lax.dot_general(a, b, (((i,), (j,)), ((), ())), preferred_element_type=F32)  13.8 us
    all_to_all x2, starting transfers between devices, gather_zx(): return lax.all_to_all(copies, ZX, 0, 0)  12.6 us
    all_to_all x1, waiting for transfers between devices, shards(): sums = lax.all_to_all(total.reshape(groups, rows, count), ZX, 0, 0)  9.48 us
    pallas_call x1, Pallas kernels, regroup(): pl.pallas_call(functools.partial(regroup_kernel, rows), grid_spec=pltpu.P...  7.72 us
  transfers between devices with their start and end apart: 33, of which 15 were waited for; matrix products, arithmetic and copies ran while one was open for 12% of the time, Pallas kernels for 5%

profile of v2, /device:TPU:1, one launch (start us, length us, event | category | flops | bytes accessed | tf_op | source)
XLA Modules:
  0.0 154.9 jit_solution(13028209602170883277)
XLA Ops:
  1.5 3.2 %collective-permute-start = (bf16[36,128]{1,0:T(8,128)(2,1)S(1)}, bf16[36,128]{1,0:T(8,128)(2,1)S(1)}, u32[]{:S(2)}, u32[]{:S(2)}) collective-permute-start(bf16[36,128]{1,0:T(8,128)(2,1)S(1)} %broadcast_select_fusion.10), channel_id=1, source_target_pairs={{0,1},{1,0},{2,3},{3,2},{4,5},{5,4},{6,7},{7,6},{8,9},{9,8},{10,11... | collective-permute-start | bytes 27656 | tf_op jit(solution)/shard_map/ppermute | solution.py:18
  7.1 9.0 %all-to-all-start = ((bf16[16,72,128]{2,1,0:T(8,128)(2,1)}), bf16[16,72,128]{2,1,0:T(8,128)(2,1)S(1)}, u32[]{:S(2)}, u32[]{:S(2)}) async-start(bf16[16,72,128]{2,1,0:T(8,128)(2,1)} %broadcast_in_dim.24), calls=%async_computation | async-start | bytes 589824 | tf_op jit(solution)/shard_map/all_to_all | solution.py:50
  16.1 7.7 %regroup.1 = bf16[4,288,1152]{2,1,0:T(8,128)(2,1)} custom-call(s32[1]{0:T(128)} %bitcast.1.y_ref, bf16[288,4608]{1,0:T(8,128)(2,1)} %w_ref), custom_call_target="tpu_custom_call" | custom-call | bytes 5308416 | tf_op jit(solution)/shard_map/regroup/pallas_call | solution.py:89
  23.8 5.4 %all-to-all-done = bf16[16,72,128]{2,1,0:T(8,128)(2,1)S(1)} async-done(((bf16[16,72,128]{2,1,0:T(8,128)(2,1)}), bf16[16,72,128]{2,1,0:T(8,128)(2,1)S(1)}, u32[]{:S(2)}, u32[]{:S(2)}) %all-to-all-start) | async-done | bytes 294944 | tf_op jit(solution)/shard_map/all_to_all | solution.py:50
  32.0 1.6 %collective-permute-start.3 = (bf16[16,1,72,128]{3,2,1,0:T(8,128)(2,1)S(1)}, bf16[16,1,72,128]{3,2,1,0:T(8,128)(2,1)S(1)}, u32[]{:S(2)}, u32[]{:S(2)}) collective-permute-start(bf16[16,1,72,128]{3,2,1,0:T(8,128)(2,1)S(1)} %bitcast.104), channel_id=1, source_target_pairs={{0,4},{2,6},{4,0},{6,2},{1,5},{3,7},{5,1},{7,3},{8,12},{10,14},{12... | collective-permute-start | bytes 884744 | tf_op jit(solution)/shard_map/ppermute | solution.py:23
  33.7 3.7 %collective-permute-done.1 = bf16[16,1,72,128]{3,2,1,0:T(8,128)(2,1)} collective-permute-done((bf16[16,1,72,128]{3,2,1,0:T(8,128)(2,1)S(1)}, bf16[16,1,72,128]{3,2,1,0:T(8,128)(2,1)}, u32[]{:S(2)}, u32[]{:S(2)}) %collective-permute-start.1) | collective-permute-done | bytes 294944 | tf_op jit(solution)/shard_map/ppermute | solution.py:23
  38.6 6.1 %collective-permute-done.3 = bf16[16,1,72,128]{3,2,1,0:T(8,128)(2,1)S(1)} collective-permute-done((bf16[16,1,72,128]{3,2,1,0:T(8,128)(2,1)S(1)}, bf16[16,1,72,128]{3,2,1,0:T(8,128)(2,1)S(1)}, u32[]{:S(2)}, u32[]{:S(2)}) %collective-permute-start.3) | collective-permute-done | bytes 294944 | tf_op jit(solution)/shard_map/ppermute | solution.py:23
  44.7 2.9 %collective-permute-start.4 = (bf16[4608,128]{1,0:T(8,128)(2,1)S(1)}, bf16[4608,128]{1,0:T(8,128)(2,1)S(1)}, u32[]{:S(2)}, u32[]{:S(2)}) collective-permute-start(bf16[4608,128]{1,0:T(8,128)(2,1)S(1)} %bitcast.94), channel_id=1, source_target_pairs={{0,1},{1,0},{2,3},{3,2},{4,5},{5,4},{6,7},{7,6},{8,9},{9,8},{10,11... | collective-permute-start | bytes 3538952 | tf_op jit(solution)/shard_map/ppermute | solution.py:18
  47.8 2.4 %collective-permute-done.13 = bf16[36,128]{1,0:T(8,128)(2,1)S(1)} collective-permute-done((bf16[36,128]{1,0:T(8,128)(2,1)S(1)}, bf16[36,128]{1,0:T(8,128)(2,1)S(1)}, u32[]{:S(2)}, u32[]{:S(2)}) %collective-permute-start.13) | collective-permute-done | bytes 9248 | tf_op jit(solution)/shard_map/ppermute | solution.py:18
  57.2 1.6 %collective-permute-start.11 = (bf16[1152,128]{1,0:T(8,128)(2,1)S(1)}, bf16[1152,128]{1,0:T(8,128)(2,1)S(1)}, u32[]{:S(2)}, u32[]{:S(2)}) collective-permute-start(bf16[1152,128]{1,0:T(8,128)(2,1)S(1)} %add_convert_fusion.1), channel_id=1, source_target_pairs={{0,6},{2,0},{4,2},{6,4},{1,7},{3,1},{5,3},{7,5},{8,14},{10,8},{12,... | collective-permute-start | bytes 884744 | tf_op jit(solution)/shard_map/ppermute | solution.py:23
  60.1 1.8 %collective-permute-start.7 = (bf16[1152,128]{1,0:T(8,128)(2,1)S(1)}, bf16[1152,128]{1,0:T(8,128)(2,1)S(1)}, u32[]{:S(2)}, u32[]{:S(2)}) collective-permute-start(bf16[1152,128]{1,0:T(8,128)(2,1)S(1)} %add_convert_fusion.3), channel_id=1, source_target_pairs={{0,4},{2,6},{4,0},{6,2},{1,5},{3,7},{5,1},{7,3},{8,12},{10,14},{12... | collective-permute-start | bytes 884744 | tf_op jit(solution)/shard_map/ppermute | solution.py:23
  62.8 2.7 %collective-permute-done.11 = bf16[1152,128]{1,0:T(8,128)(2,1)S(1)} collective-permute-done((bf16[1152,128]{1,0:T(8,128)(2,1)S(1)}, bf16[1152,128]{1,0:T(8,128)(2,1)S(1)}, u32[]{:S(2)}, u32[]{:S(2)}) %collective-permute-start.11) | collective-permute-done | bytes 294944 | tf_op jit(solution)/shard_map/ppermute | solution.py:23
  65.5 4.1 %collective-permute-done.9 = bf16[1152,128]{1,0:T(8,128)(2,1)S(1)} collective-permute-done((bf16[1152,128]{1,0:T(8,128)(2,1)S(1)}, bf16[1152,128]{1,0:T(8,128)(2,1)S(1)}, u32[]{:S(2)}, u32[]{:S(2)}) %collective-permute-start.9) | collective-permute-done | bytes 294944 | tf_op jit(solution)/shard_map/ppermute | solution.py:23
  69.6 4.5 %collective-permute-done.7 = bf16[1152,128]{1,0:T(8,128)(2,1)S(1)} collective-permute-done((bf16[1152,128]{1,0:T(8,128)(2,1)S(1)}, bf16[1152,128]{1,0:T(8,128)(2,1)S(1)}, u32[]{:S(2)}, u32[]{:S(2)}) %collective-permute-start.7) | collective-permute-done | bytes 294944 | tf_op jit(solution)/shard_map/ppermute | solution.py:23
  75.0 3.6 %all-to-all-start.1 = ((bf16[16,72,128]{2,1,0:T(8,128)(2,1)}), bf16[16,72,128]{2,1,0:T(8,128)(2,1)S(1)}, u32[]{:S(2)}, u32[]{:S(2)}) async-start(bf16[16,72,128]{2,1,0:T(8,128)(2,1)} %bitcast.14), calls=%async_computation.1 | async-start | bytes 589824 | tf_op jit(solution)/shard_map/all_to_all | solution.py:140
  78.7 1.9 %constant_dynamic-slice_fusion.1 = bf16[2304,128]{1,0:T(8,128)(2,1)} fusion(bf16[4608,128]{1,0:T(8,128)(2,1)} %bitcast.97, s32[]{:T(128)S(6)} %select_n.98), kind=kLoop, calls=%fused_computation.138 | loop fusion | bytes 1179652 | tf_op jit(solution)/shard_map/dynamic_slice | solution.py:146
  80.6 9.5 %all-to-all-done.1 = bf16[16,72,128]{2,1,0:T(8,128)(2,1)S(1)} async-done(((bf16[16,72,128]{2,1,0:T(8,128)(2,1)}), bf16[16,72,128]{2,1,0:T(8,128)(2,1)S(1)}, u32[]{:S(2)}, u32[]{:S(2)}) %all-to-all-start.1) | async-done | bytes 294944 | tf_op jit(solution)/shard_map/all_to_all | solution.py:140
  91.5 4.1 %collective-permute-start.14 = (bf16[36,128]{1,0:T(8,128)(2,1)}, bf16[36,128]{1,0:T(8,128)(2,1)S(1)}, u32[]{:S(2)}, u32[]{:S(2)}) collective-permute-start(bf16[36,128]{1,0:T(8,128)(2,1)} %broadcast_select_fusion.2), channel_id=1, source_target_pairs={{0,1},{1,0},{2,3},{3,2},{4,5},{5,4},{6,7},{7,6},{8,9},{9,8},{10,11... | collective-permute-start | bytes 27656 | tf_op jit(solution)/shard_map/ppermute | solution.py:18
  96.4 3.5 %all-to-all-start.2 = ((bf16[16,72,128]{2,1,0:T(8,128)(2,1)}), bf16[16,72,128]{2,1,0:T(8,128)(2,1)S(1)}, u32[]{:S(2)}, u32[]{:S(2)}) async-start(bf16[16,72,128]{2,1,0:T(8,128)(2,1)} %broadcast_in_dim.53), calls=%async_computation.2 | async-start | bytes 589824 | tf_op jit(solution)/shard_map/all_to_all | solution.py:50
  99.9 2.4 %fusion.7 = bf16[2304,256]{1,0:T(8,128)(2,1)} fusion(s32[]{:T(128)S(6)} %select_n.99, bf16[4608,128]{1,0:T(8,128)(2,1)} %bitcast.98, bf16[4608,128]{1,0:T(8,128)(2,1)} %copy-done.5), kind=kLoop, calls=%fused_computation.18 | loop fusion | flops 2359296 | bytes 3538948 | tf_op jit(solution)/shard_map/concatenate | solution.py:119
  102.9 10.6 %all-to-all-done.2 = bf16[16,72,128]{2,1,0:T(8,128)(2,1)S(1)} async-done(((bf16[16,72,128]{2,1,0:T(8,128)(2,1)}), bf16[16,72,128]{2,1,0:T(8,128)(2,1)S(1)}, u32[]{:S(2)}, u32[]{:S(2)}) %all-to-all-start.2) | async-done | bytes 294944 | tf_op jit(solution)/shard_map/all_to_all | solution.py:50
  113.6 2.7 %collective-permute-start.19 = (bf16[16,72,128]{2,1,0:T(8,128)(2,1)S(1)}, bf16[16,72,128]{2,1,0:T(8,128)(2,1)S(1)}, u32[]{:S(2)}, u32[]{:S(2)}) collective-permute-start(bf16[16,72,128]{2,1,0:T(8,128)(2,1)S(1)} %all-to-all-done.2), channel_id=1, source_target_pairs={{0,6},{2,0},{4,2},{6,4},{1,7},{3,1},{5,3},{7,5},{8,14},{10,8},{12,... | collective-permute-start | bytes 884744 | tf_op jit(solution)/shard_map/ppermute | solution.py:23
  116.2 2.7 %collective-permute-start.23 = (bf16[1152,128]{1,0:T(8,128)(2,1)S(1)}, bf16[1152,128]{1,0:T(8,128)(2,1)S(1)}, u32[]{:S(2)}, u32[]{:S(2)}) collective-permute-start(bf16[1152,128]{1,0:T(8,128)(2,1)S(1)} %bitcast.99), channel_id=1, source_target_pairs={{0,1},{1,0},{2,3},{3,2},{4,5},{5,4},{6,7},{7,6},{8,9},{9,8},{10,11... | collective-permute-start | bytes 884744 | tf_op jit(solution)/shard_map/ppermute | solution.py:18
  120.6 1.6 %collective-permute-done.21 = bf16[16,72,128]{2,1,0:T(8,128)(2,1)S(1)} collective-permute-done((bf16[16,72,128]{2,1,0:T(8,128)(2,1)S(1)}, bf16[16,72,128]{2,1,0:T(8,128)(2,1)S(1)}, u32[]{:S(2)}, u32[]{:S(2)}) %collective-permute-start.21) | collective-permute-done | bytes 294944 | tf_op jit(solution)/shard_map/ppermute | solution.py:23
  122.2 8.3 %collective-permute-start.22 = (bf16[1152,128]{1,0:T(8,128)(2,1)S(1)}, bf16[1152,128]{1,0:T(8,128)(2,1)S(1)}, u32[]{:S(2)}, u32[]{:S(2)}) collective-permute-start(bf16[1152,128]{1,0:T(8,128)(2,1)S(1)} %bitcast.112), channel_id=1, source_target_pairs={{0,1},{1,0},{2,3},{3,2},{4,5},{5,4},{6,7},{7,6},{8,9},{9,8},{10,11... | collective-permute-start | bytes 884744 | tf_op jit(solution)/shard_map/ppermute | solution.py:18
  132.5 1.6 %collective-permute-done.15 = bf16[2304,128]{1,0:T(8,128)(2,1)S(1)} collective-permute-done((bf16[2304,128]{1,0:T(8,128)(2,1)}, bf16[2304,128]{1,0:T(8,128)(2,1)S(1)}, u32[]{:S(2)}, u32[]{:S(2)}) %collective-permute-start.15) | collective-permute-done | bytes 589856 | tf_op jit(solution)/shard_map/ppermute | solution.py:18
  137.3 3.0 %collective-permute-start.28 = (bf16[8,72,128]{2,1,0:T(8,128)(2,1)S(1)}, bf16[8,72,128]{2,1,0:T(8,128)(2,1)S(1)}, u32[]{:S(2)}, u32[]{:S(2)}) collective-permute-start(bf16[8,72,128]{2,1,0:T(8,128)(2,1)S(1)} %collective-permute-done.24), channel_id=1, source_target_pairs={{0,4},{2,6},{4,0},{6,2},{1,5},{3,7},{5,1},{7,3},{8,12},{10,14},{12... | collective-permute-start | bytes 442376 | tf_op jit(solution)/shard_map/ppermute | solution.py:23
  140.3 1.5 collective-permute-start.26
  142.3 5.1 %collective-permute-done.26 = bf16[8,72,128]{2,1,0:T(8,128)(2,1)S(1)} collective-permute-done((bf16[8,72,128]{2,1,0:T(8,128)(2,1)S(1)}, bf16[8,72,128]{2,1,0:T(8,128)(2,1)S(1)}, u32[]{:S(2)}, u32[]{:S(2)}) %collective-permute-start.26) | collective-permute-done | bytes 147488 | tf_op jit(solution)/shard_map/ppermute | solution.py:23
  149.0 1.9 %convolution_convert_fusion.1 = bf16[2304,288]{0,1:T(8,128)(2,1)} fusion(bf16[2304,128]{1,0:T(8,128)(2,1)S(1)} %collective-permute-done.16, bf16[2304,128]{1,0:T(8,128)(2,1)S(1)} %collective-permute-done.15, bf16[2304,256]{1,0:T(8,128)(2,1)S(1)} %copy-done.4, bf16[288,256]{1,0:T(8,128)(2,1)S(1)} %get-tuple-element.47, bf16[288,256]{1,0:T(8,128)(2,1)S(1)} %get-tuple-element.44), kind=kOutput, calls=%fused_computation.1 | convolution fusion | flops 687808512 | bytes 3981312 | tf_op jit(solution)/shard_map/dot_general | solution.py:65
  151.0 1.9 %convolution_convert_fusion.2 = bf16[2304,288]{0,1:T(8,128)(2,1)} fusion(bf16[2304,128]{1,0:T(8,128)(2,1)S(1)} %collective-permute-done.16, bf16[2304,128]{1,0:T(8,128)(2,1)S(1)} %collective-permute-done.15, bf16[2304,256]{1,0:T(8,128)(2,1)S(1)} %copy-done.4, bf16[288,256]{1,0:T(8,128)(2,1)S(1)} %get-tuple-element.48, bf16[288,256]{1,0:T(8,128)(2,1)S(1)} %get-tuple-element.46), kind=kOutput, calls=%fused_computation.2 | convolution fusion | flops 687808512 | bytes 3981312 | tf_op jit(solution)/shard_map/dot_general | solution.py:65
  152.9 1.9 %convolution_convert_fusion = bf16[288,2304]{1,0:T(8,128)(2,1)} fusion(bf16[2304,128]{1,0:T(8,128)(2,1)S(1)} %collective-permute-done.29, bf16[2304,128]{1,0:T(8,128)(2,1)S(1)} %bitcast.107, bf16[2304,256]{1,0:T(8,128)(2,1)S(1)} %bitcast.101, bf16[288,256]{1,0:T(8,128)(2,1)S(1)} %slice_bitcast_fusion, bf16[288,256]{1,0:T(8,128)(2,1)S(1)} %copy-done.7), kind=kOutput, calls=%fused_computation | convolution fusion | flops 687808512 | bytes 3981312 | tf_op jit(solution)/shard_map/dot_general | solution.py:65
  (116 shorter events, 28.9 us)
Async XLA Ops:
  1.5 4.1 %collective-permute-start = (bf16[36,128]{1,0:T(8,128)(2,1)S(1)}, bf16[36,128]{1,0:T(8,128)(2,1)S(1)}, u32[]{:S(2)}, u32[]{:S(2)}) collective-permute-start(bf16[36,128]{1,0:T(8,128)(2,1)S(1)} %broadcast_select_fusion.10), channel_id=1, source_target_pairs={{0,1},{1,0},{2,3},{3,2},{4,5},{5,4},{6,7},{7,6},{8,9},{9,8},{10,11... | collective-permute-start | bytes 27656 | tf_op jit(solution)/shard_map/ppermute | solution.py:18
  7.1 22.2 %all-to-all-start = ((bf16[16,72,128]{2,1,0:T(8,128)(2,1)}), bf16[16,72,128]{2,1,0:T(8,128)(2,1)S(1)}, u32[]{:S(2)}, u32[]{:S(2)}) async-start(bf16[16,72,128]{2,1,0:T(8,128)(2,1)} %broadcast_in_dim.24), calls=%async_computation | async-start | bytes 589824 | tf_op jit(solution)/shard_map/all_to_all | solution.py:50
  29.3 8.0 %collective-permute-start.1 = (bf16[16,1,72,128]{3,2,1,0:T(8,128)(2,1)S(1)}, bf16[16,1,72,128]{3,2,1,0:T(8,128)(2,1)}, u32[]{:S(2)}, u32[]{:S(2)}) collective-permute-start(bf16[16,1,72,128]{3,2,1,0:T(8,128)(2,1)S(1)} %bitcast.102), channel_id=1, source_target_pairs={{0,2},{2,4},{4,6},{6,0},{1,3},{3,5},{5,7},{7,1},{8,10},{10,12},{12... | collective-permute-start | bytes 884744 | tf_op jit(solution)/shard_map/ppermute | solution.py:23
  30.6 7.9 %collective-permute-start.2 = (bf16[16,1,72,128]{3,2,1,0:T(8,128)(2,1)S(1)}, bf16[16,1,72,128]{3,2,1,0:T(8,128)(2,1)S(1)}, u32[]{:S(2)}, u32[]{:S(2)}) collective-permute-start(bf16[16,1,72,128]{3,2,1,0:T(8,128)(2,1)S(1)} %bitcast.103), channel_id=1, source_target_pairs={{0,6},{2,0},{4,2},{6,4},{1,7},{3,1},{5,3},{7,5},{8,14},{10,8},{12,... | collective-permute-start | bytes 884744 | tf_op jit(solution)/shard_map/ppermute | solution.py:23
  32.0 12.6 %collective-permute-start.3 = (bf16[16,1,72,128]{3,2,1,0:T(8,128)(2,1)S(1)}, bf16[16,1,72,128]{3,2,1,0:T(8,128)(2,1)S(1)}, u32[]{:S(2)}, u32[]{:S(2)}) collective-permute-start(bf16[16,1,72,128]{3,2,1,0:T(8,128)(2,1)S(1)} %bitcast.104), channel_id=1, source_target_pairs={{0,4},{2,6},{4,0},{6,2},{1,5},{3,7},{5,1},{7,3},{8,12},{10,14},{12... | collective-permute-start | bytes 884744 | tf_op jit(solution)/shard_map/ppermute | solution.py:23
  44.7 6.0 %collective-permute-start.4 = (bf16[4608,128]{1,0:T(8,128)(2,1)S(1)}, bf16[4608,128]{1,0:T(8,128)(2,1)S(1)}, u32[]{:S(2)}, u32[]{:S(2)}) collective-permute-start(bf16[4608,128]{1,0:T(8,128)(2,1)S(1)} %bitcast.94), channel_id=1, source_target_pairs={{0,1},{1,0},{2,3},{3,2},{4,5},{5,4},{6,7},{7,6},{8,9},{9,8},{10,11... | collective-permute-start | bytes 3538952 | tf_op jit(solution)/shard_map/ppermute | solution.py:18
  47.6 2.5 %collective-permute-start.13 = (bf16[36,128]{1,0:T(8,128)(2,1)S(1)}, bf16[36,128]{1,0:T(8,128)(2,1)S(1)}, u32[]{:S(2)}, u32[]{:S(2)}) collective-permute-start(bf16[36,128]{1,0:T(8,128)(2,1)S(1)} %broadcast_select_fusion.6), channel_id=1, source_target_pairs={{0,1},{1,0},{2,3},{3,2},{4,5},{5,4},{6,7},{7,6},{8,9},{9,8},{10,11... | collective-permute-start | bytes 27656 | tf_op jit(solution)/shard_map/ppermute | solution.py:18
  55.5 3.4 %collective-permute-start.8 = (bf16[1152,128]{1,0:T(8,128)(2,1)S(1)}, bf16[1152,128]{1,0:T(8,128)(2,1)S(1)}, u32[]{:S(2)}, u32[]{:S(2)}) collective-permute-start(bf16[1152,128]{1,0:T(8,128)(2,1)S(1)} %convolution_convert_fusion.4), channel_id=1, source_target_pairs={{0,1},{1,0},{2,3},{3,2},{4,5},{5,4},{6,7},{7,6},{8,9},{9,8},{10,11... | collective-permute-start | bytes 884744 | tf_op jit(solution)/shard_map/ppermute | solution.py:18
  56.2 6.6 %collective-permute-start.5 = (bf16[1152,128]{1,0:T(8,128)(2,1)S(1)}, bf16[1152,128]{1,0:T(8,128)(2,1)S(1)}, u32[]{:S(2)}, u32[]{:S(2)}) collective-permute-start(bf16[1152,128]{1,0:T(8,128)(2,1)S(1)} %convolution_convert_fusion.6), channel_id=1, source_target_pairs={{0,1},{1,0},{2,3},{3,2},{4,5},{5,4},{6,7},{7,6},{8,9},{9,8},{10,11... | collective-permute-start | bytes 884744 | tf_op jit(solution)/shard_map/ppermute | solution.py:18
  56.6 3.0 %collective-permute-start.6 = (bf16[1152,128]{1,0:T(8,128)(2,1)S(1)}, bf16[1152,128]{1,0:T(8,128)(2,1)S(1)}, u32[]{:S(2)}, u32[]{:S(2)}) collective-permute-start(bf16[1152,128]{1,0:T(8,128)(2,1)S(1)} %convolution_convert_fusion.5), channel_id=1, source_target_pairs={{0,1},{1,0},{2,3},{3,2},{4,5},{5,4},{6,7},{7,6},{8,9},{9,8},{10,11... | collective-permute-start | bytes 884744 | tf_op jit(solution)/shard_map/ppermute | solution.py:18
  57.2 8.3 %collective-permute-start.11 = (bf16[1152,128]{1,0:T(8,128)(2,1)S(1)}, bf16[1152,128]{1,0:T(8,128)(2,1)S(1)}, u32[]{:S(2)}, u32[]{:S(2)}) collective-permute-start(bf16[1152,128]{1,0:T(8,128)(2,1)S(1)} %add_convert_fusion.1), channel_id=1, source_target_pairs={{0,6},{2,0},{4,2},{6,4},{1,7},{3,1},{5,3},{7,5},{8,14},{10,8},{12,... | collective-permute-start | bytes 884744 | tf_op jit(solution)/shard_map/ppermute | solution.py:23
  59.3 10.3 %collective-permute-start.9 = (bf16[1152,128]{1,0:T(8,128)(2,1)S(1)}, bf16[1152,128]{1,0:T(8,128)(2,1)S(1)}, u32[]{:S(2)}, u32[]{:S(2)}) collective-permute-start(bf16[1152,128]{1,0:T(8,128)(2,1)S(1)} %add_convert_fusion.2), channel_id=1, source_target_pairs={{0,2},{2,4},{4,6},{6,0},{1,3},{3,5},{5,7},{7,1},{8,10},{10,12},{12... | collective-permute-start | bytes 884744 | tf_op jit(solution)/shard_map/ppermute | solution.py:23
  60.1 14.0 %collective-permute-start.7 = (bf16[1152,128]{1,0:T(8,128)(2,1)S(1)}, bf16[1152,128]{1,0:T(8,128)(2,1)S(1)}, u32[]{:S(2)}, u32[]{:S(2)}) collective-permute-start(bf16[1152,128]{1,0:T(8,128)(2,1)S(1)} %add_convert_fusion.3), channel_id=1, source_target_pairs={{0,4},{2,6},{4,0},{6,2},{1,5},{3,7},{5,1},{7,3},{8,12},{10,14},{12... | collective-permute-start | bytes 884744 | tf_op jit(solution)/shard_map/ppermute | solution.py:23
  61.9 13.1 %collective-permute-start.12 = (bf16[3,288,256]{2,1,0:T(8,128)(2,1)S(1)}, bf16[3,288,256]{2,1,0:T(8,128)(2,1)S(1)}, u32[]{:S(2)}, u32[]{:S(2)}) collective-permute-start(bf16[3,288,256]{2,1,0:T(8,128)(2,1)S(1)} %pad_maximum_fusion.10), channel_id=1, source_target_pairs={{0,128},{128,0},{1,129},{129,1},{2,130},{130,2},{3,131},{131,3},{4... | collective-permute-start | bytes 1327112 | tf_op jit(solution)/shard_map/ppermute | solution.py:18
  75.0 15.0 %all-to-all-start.1 = ((bf16[16,72,128]{2,1,0:T(8,128)(2,1)}), bf16[16,72,128]{2,1,0:T(8,128)(2,1)S(1)}, u32[]{:S(2)}, u32[]{:S(2)}) async-start(bf16[16,72,128]{2,1,0:T(8,128)(2,1)} %bitcast.14), calls=%async_computation.1 | async-start | bytes 589824 | tf_op jit(solution)/shard_map/all_to_all | solution.py:140
  91.5 10.8 %collective-permute-start.14 = (bf16[36,128]{1,0:T(8,128)(2,1)}, bf16[36,128]{1,0:T(8,128)(2,1)S(1)}, u32[]{:S(2)}, u32[]{:S(2)}) collective-permute-start(bf16[36,128]{1,0:T(8,128)(2,1)} %broadcast_select_fusion.2), channel_id=1, source_target_pairs={{0,1},{1,0},{2,3},{3,2},{4,5},{5,4},{6,7},{7,6},{8,9},{9,8},{10,11... | collective-permute-start | bytes 27656 | tf_op jit(solution)/shard_map/ppermute | solution.py:18
  96.4 17.2 %all-to-all-start.2 = ((bf16[16,72,128]{2,1,0:T(8,128)(2,1)}), bf16[16,72,128]{2,1,0:T(8,128)(2,1)S(1)}, u32[]{:S(2)}, u32[]{:S(2)}) async-start(bf16[16,72,128]{2,1,0:T(8,128)(2,1)} %broadcast_in_dim.53), calls=%async_computation.2 | async-start | bytes 589824 | tf_op jit(solution)/shard_map/all_to_all | solution.py:50
  113.6 8.6 %collective-permute-start.21 = (bf16[16,72,128]{2,1,0:T(8,128)(2,1)S(1)}, bf16[16,72,128]{2,1,0:T(8,128)(2,1)S(1)}, u32[]{:S(2)}, u32[]{:S(2)}) collective-permute-start(bf16[16,72,128]{2,1,0:T(8,128)(2,1)S(1)} %all-to-all-done.2), channel_id=1, source_target_pairs={{0,2},{2,4},{4,6},{6,0},{1,3},{3,5},{5,7},{7,1},{8,10},{10,12},{12... | collective-permute-start | bytes 884744 | tf_op jit(solution)/shard_map/ppermute | solution.py:23
  113.6 17.0 %collective-permute-start.19 = (bf16[16,72,128]{2,1,0:T(8,128)(2,1)S(1)}, bf16[16,72,128]{2,1,0:T(8,128)(2,1)S(1)}, u32[]{:S(2)}, u32[]{:S(2)}) collective-permute-start(bf16[16,72,128]{2,1,0:T(8,128)(2,1)S(1)} %all-to-all-done.2), channel_id=1, source_target_pairs={{0,6},{2,0},{4,2},{6,4},{1,7},{3,1},{5,3},{7,5},{8,14},{10,8},{12,... | collective-permute-start | bytes 884744 | tf_op jit(solution)/shard_map/ppermute | solution.py:23
  116.2 14.3 %collective-permute-start.17 = (bf16[16,72,128]{2,1,0:T(8,128)(2,1)S(1)}, bf16[16,72,128]{2,1,0:T(8,128)(2,1)S(1)}, u32[]{:S(2)}, u32[]{:S(2)}) collective-permute-start(bf16[16,72,128]{2,1,0:T(8,128)(2,1)S(1)} %all-to-all-done.2), channel_id=1, source_target_pairs={{0,4},{2,6},{4,0},{6,2},{1,5},{3,7},{5,1},{7,3},{8,12},{10,14},{12... | collective-permute-start | bytes 884744 | tf_op jit(solution)/shard_map/ppermute | solution.py:23
  116.2 4.0 %collective-permute-start.23 = (bf16[1152,128]{1,0:T(8,128)(2,1)S(1)}, bf16[1152,128]{1,0:T(8,128)(2,1)S(1)}, u32[]{:S(2)}, u32[]{:S(2)}) collective-permute-start(bf16[1152,128]{1,0:T(8,128)(2,1)S(1)} %bitcast.99), channel_id=1, source_target_pairs={{0,1},{1,0},{2,3},{3,2},{4,5},{5,4},{6,7},{7,6},{8,9},{9,8},{10,11... | collective-permute-start | bytes 884744 | tf_op jit(solution)/shard_map/ppermute | solution.py:18
  119.0 15.2 %collective-permute-start.15 = (bf16[2304,128]{1,0:T(8,128)(2,1)}, bf16[2304,128]{1,0:T(8,128)(2,1)S(1)}, u32[]{:S(2)}, u32[]{:S(2)}) collective-permute-start(bf16[2304,128]{1,0:T(8,128)(2,1)} %constant_dynamic-slice_fusion.1), channel_id=1, source_target_pairs={{0,128},{128,0},{1,129},{129,1},{2,130},{130,2},{3,131},{131,3},{4... | collective-permute-start | bytes 1769480 | tf_op jit(solution)/shard_map/ppermute | solution.py:18
  120.2 17.1 %collective-permute-start.24 = (bf16[8,72,128]{2,1,0:T(8,128)(2,1)S(1)}, bf16[8,72,128]{2,1,0:T(8,128)(2,1)S(1)}, u32[]{:S(2)}, u32[]{:S(2)}) collective-permute-start(bf16[8,72,128]{2,1,0:T(8,128)(2,1)S(1)} %constant_dynamic-slice_fusion), channel_id=1, source_target_pairs={{0,128},{128,0},{1,129},{129,1},{2,130},{130,2},{3,131},{131,3},{4... | collective-permute-start | bytes 442376 | tf_op jit(solution)/shard_map/ppermute | solution.py:18
  122.2 13.2 %collective-permute-start.22 = (bf16[1152,128]{1,0:T(8,128)(2,1)S(1)}, bf16[1152,128]{1,0:T(8,128)(2,1)S(1)}, u32[]{:S(2)}, u32[]{:S(2)}) collective-permute-start(bf16[1152,128]{1,0:T(8,128)(2,1)S(1)} %bitcast.112), channel_id=1, source_target_pairs={{0,1},{1,0},{2,3},{3,2},{4,5},{5,4},{6,7},{7,6},{8,9},{9,8},{10,11... | collective-permute-start | bytes 884744 | tf_op jit(solution)/shard_map/ppermute | solution.py:18
  130.5 5.2 %collective-permute-start.20 = (bf16[1152,128]{1,0:T(8,128)(2,1)S(1)}, bf16[1152,128]{1,0:T(8,128)(2,1)S(1)}, u32[]{:S(2)}, u32[]{:S(2)}) collective-permute-start(bf16[1152,128]{1,0:T(8,128)(2,1)S(1)} %bitcast.114), channel_id=1, source_target_pairs={{0,1},{1,0},{2,3},{3,2},{4,5},{5,4},{6,7},{7,6},{8,9},{9,8},{10,11... | collective-permute-start | bytes 884744 | tf_op jit(solution)/shard_map/ppermute | solution.py:18
  130.5 5.7 %collective-permute-start.18 = (bf16[1152,128]{1,0:T(8,128)(2,1)S(1)}, bf16[1152,128]{1,0:T(8,128)(2,1)S(1)}, u32[]{:S(2)}, u32[]{:S(2)}) collective-permute-start(bf16[1152,128]{1,0:T(8,128)(2,1)S(1)} %bitcast.110), channel_id=1, source_target_pairs={{0,1},{1,0},{2,3},{3,2},{4,5},{5,4},{6,7},{7,6},{8,9},{9,8},{10,11... | collective-permute-start | bytes 884744 | tf_op jit(solution)/shard_map/ppermute | solution.py:18
  134.2 14.9 %collective-permute-start.16 = (bf16[2304,128]{1,0:T(8,128)(2,1)S(1)}, bf16[2304,128]{1,0:T(8,128)(2,1)S(1)}, u32[]{:S(2)}, u32[]{:S(2)}) collective-permute-start(bf16[2304,128]{1,0:T(8,128)(2,1)S(1)} %collective-permute-done.15), channel_id=1, source_target_pairs={{0,1},{1,0},{2,3},{3,2},{4,5},{5,4},{6,7},{7,6},{8,9},{9,8},{10,11... | collective-permute-start | bytes 1769480 | tf_op jit(solution)/shard_map/ppermute | solution.py:18
  137.3 10.3 %collective-permute-start.28 = (bf16[8,72,128]{2,1,0:T(8,128)(2,1)S(1)}, bf16[8,72,128]{2,1,0:T(8,128)(2,1)S(1)}, u32[]{:S(2)}, u32[]{:S(2)}) collective-permute-start(bf16[8,72,128]{2,1,0:T(8,128)(2,1)S(1)} %collective-permute-done.24), channel_id=1, source_target_pairs={{0,4},{2,6},{4,0},{6,2},{1,5},{3,7},{5,1},{7,3},{8,12},{10,14},{12... | collective-permute-start | bytes 442376 | tf_op jit(solution)/shard_map/ppermute | solution.py:23
  140.3 7.2 %collective-permute-start.27 = (bf16[8,72,128]{2,1,0:T(8,128)(2,1)S(1)}, bf16[8,72,128]{2,1,0:T(8,128)(2,1)S(1)}, u32[]{:S(2)}, u32[]{:S(2)}) collective-permute-start(bf16[8,72,128]{2,1,0:T(8,128)(2,1)S(1)} %collective-permute-done.24), channel_id=1, source_target_pairs={{0,6},{2,0},{4,2},{6,4},{1,7},{3,1},{5,3},{7,5},{8,14},{10,8},{12,... | collective-permute-start | bytes 442376 | tf_op jit(solution)/shard_map/ppermute | solution.py:23
  140.3 7.1 %collective-permute-start.26 = (bf16[8,72,128]{2,1,0:T(8,128)(2,1)S(1)}, bf16[8,72,128]{2,1,0:T(8,128)(2,1)S(1)}, u32[]{:S(2)}, u32[]{:S(2)}) collective-permute-start(bf16[8,72,128]{2,1,0:T(8,128)(2,1)S(1)} %collective-permute-done.24), channel_id=1, source_target_pairs={{0,2},{2,4},{4,6},{6,0},{1,3},{3,5},{5,7},{7,1},{8,10},{10,12},{12... | collective-permute-start | bytes 442376 | tf_op jit(solution)/shard_map/ppermute | solution.py:23
  141.8 7.2 %collective-permute-start.25 = (bf16[288,256]{1,0:T(8,128)(2,1)S(1)}, bf16[288,256]{1,0:T(8,128)(2,1)S(1)}, u32[]{:S(2)}, u32[]{:S(2)}) collective-permute-start(bf16[288,256]{1,0:T(8,128)(2,1)S(1)} %get-tuple-element.41), channel_id=1, source_target_pairs={{0,128},{128,0},{1,129},{129,1},{2,130},{130,2},{3,131},{131,3},{4... | collective-permute-start | bytes 442376 | tf_op jit(solution)/shard_map/ppermute | solution.py:18
  147.6 5.3 %collective-permute-start.29 = (bf16[2304,128]{1,0:T(8,128)(2,1)S(1)}, bf16[2304,128]{1,0:T(8,128)(2,1)S(1)}, u32[]{:S(2)}, u32[]{:S(2)}) collective-permute-start(bf16[2304,128]{1,0:T(8,128)(2,1)S(1)} %bitcast.106), channel_id=1, source_target_pairs={{0,1},{1,0},{2,3},{3,2},{4,5},{5,4},{6,7},{7,6},{8,9},{9,8},{10,11... | collective-permute-start | bytes 1769480 | tf_op jit(solution)/shard_map/ppermute | solution.py:18
  (15 other events, 144.2 us)

commit v3 on v2

--- a/solution.py
+++ b/solution.py
@@ -85,7 +85,7 @@
 
 def regroup(weight, y, ny, rows):
     units, features = weight.shape
-    block = 32
+    block = units // 3
     return pl.pallas_call(
         functools.partial(regroup_kernel, rows),
         grid_spec=pltpu.PrefetchScalarGridSpec(
@@ -116,19 +116,22 @@
     (x_mine,) = gather_y(part, y, 1)
     x_mine = x_mine.reshape(features, -1)
     count = x_mine.shape[1]
-    x = jnp.concatenate([x_mine, swap(x_mine, "c")], axis=1)
-
-    gate = dot(gate_weight, x, 0, 0)
-    upper = dot(up_weight, x, 0, 0)
-    sigma = jax.nn.sigmoid(gate)
-    silu = gate * sigma
-    slope = (upper * sigma * (1.0 + gate * (1.0 - sigma))).astype(BF)
-    hidden = (silu * upper).astype(BF)
-    silu = silu.astype(BF)
+    x_other = swap(x_mine, "c")
+
+    def forward(tokens_half):
+        gate = dot(gate_weight, tokens_half, 0, 0)
+        upper = dot(up_weight, tokens_half, 0, 0)
+        sigma = jax.nn.sigmoid(gate)
+        silu = gate * sigma
+        slope = upper * sigma * (1.0 + gate * (1.0 - sigma))
+        return [t.astype(BF) for t in (silu * upper, silu, slope)]
+
+    held_mine, held_other = forward(x_mine), forward(x_other)
+    hidden, silu, slope = (jnp.concatenate(t, axis=1) for t in zip(held_mine, held_other))
 
     def pair(k):
-        other = swap(row_major(dot(down[k], hidden[:, count:], 0, 0).astype(BF)), "c")
-        return row_major(dot(down[k], hidden[:, :count], 0, 0)) + other.astype(F32)
+        other = swap(row_major(dot(down[k], held_other[0], 0, 0).astype(BF)), "c")
+        return row_major(dot(down[k], held_mine[0], 0, 0)) + other.astype(F32)
 
     arrived = [shift(pair(k).astype(BF), "y", k) for k in (2, 1, 3)]
     total = pair(0)
@@ -142,17 +145,21 @@
     student = unpair_block(summed.astype(BF), c)
     errors = ((summed - teach) * factor).astype(BF)
 
+    xs = lax.dynamic_slice_in_dim(x_mine, (1 - d) * half, half, 0)
+    errors, xs, x_mine, x_other = barrier(errors, xs, x_mine, x_other)
+    xp_mine = swap(xs, "dp")
     e_part = gather_zx(errors)
-    xs = lax.dynamic_slice_in_dim(x_mine, (1 - d) * half, half, 0)
-    e_part, student, xs = barrier(e_part, student, xs)
+    xo = [lax.dynamic_slice_in_dim(t, d * half, half, 0) for t in (x_mine, x_other)]
+    e_part, student, *xo = barrier(e_part, student, *xo)
     keep, give = d * (groups // 2), (1 - d) * (groups // 2)
     e_got = swap(lax.dynamic_slice_in_dim(e_part, give, groups // 2, 0), "dp")
-    xp_mine = swap(xs, "dp")
     e_pieces = {0: e_part, **{k: shift(e_part, "y", k) for k in (2, 1, 3)}}
     back = 0.0
     kept = {}
     for k in (0, 1, 3, 2):
         piece = e_pieces[k].reshape(groups * rows, count)
+        if k == 1:
+            piece, back = barrier(piece, back)
         other = swap(piece, "c")
         if k:
             other, back = barrier(other, back)
@@ -172,12 +179,12 @@
             whole = lax.dynamic_update_slice_in_dim(whole, pieces[k][:, None], lax.rem(y - k + ny, ny), 1)
         return whole.reshape(half, -1)
 
-    eo, ep_mine = assembled(kept), assembled(got_pieces)
-    errors_both = jnp.concatenate([eo, ep_mine, swap(ep_mine, "c")], axis=1)
-    xo = lax.dynamic_slice_in_dim(x, d * half, half, 0)
-    x_both = jnp.concatenate([xo, xp_mine, swap(xp_mine, "c")], axis=1)
+    x_both = jnp.concatenate([*xo, xp_mine, swap(xp_mine, "c")], axis=1)
     grad_gate = dot(x_both, gate_back, 1, 1)
     grad_up = dot(x_both, up_back, 1, 1)
+    grad_gate, *got_late = barrier(grad_gate, *(got_pieces[k] for k in (1, 2, 3)))
+    eo, ep_mine = assembled(kept), assembled(dict(enumerate([got_pieces[0], *got_late])))
+    errors_both = jnp.concatenate([eo, ep_mine, swap(ep_mine, "c")], axis=1)
     grad_down = dot(jnp.concatenate([hidden, hidden_p], axis=1), errors_both, 1, 1)
     return student, grad_gate.astype(BF), grad_up.astype(BF), grad_down.astype(BF)
 

time: 156 us -> 149 us (0.955)
  waiting for transfers between devices: 59.5 us -> 48.8 us
  local copies, waits for them, and re-layouts: 6.24 us -> 13.3 us
  other arithmetic: 8.07 us -> 5.58 us
  Pallas kernels: 7.72 us -> 5.25 us
    ppermute x12, waiting for transfers between devices: 27.8 us -> 16.5 us  [shift(): return lax.ppermute(x, axis, [(i, (i + k) % n) for i in range(n)])]
    dynamic_slice x0 -> x2, local copies, waits for them, and re-layouts: none -> 3.03 us  [shards(): lax.dynamic_slice_in_dim(t, d * half, half, 0)]
    unnamed x28 -> x52, local copies, waits for them, and re-layouts: 1.27 us -> 4.25 us
    pallas_call x1, Pallas kernels: 7.72 us -> 5.25 us  [regroup(): pl.pallas_call(functools.partial(regroup_kernel, rows), grid_spec=pltpu.P...]
    concatenate x1 -> x0, other arithmetic: 2.39 us -> none  [shards(): x = jnp.concatenate([x_mine, swap(x_mine, 'c')], axis=1)]
    dot_general x17 -> x19, matrix products: 13.8 us -> 14.4 us  [dot(): lax.dot_general(a, b, (((i,), (j,)), ((), ())), preferred_element_type=F32)]
  transfers between devices with their start and end apart: 33 -> 33, of which waited for: 15 -> 10; matrix products, arithmetic and copies ran while one was open for 12% -> 16% of each run, Pallas kernels for 5% -> 4%
where the time goes in v3:
time: 149 us; the launch traced here: 148 us
  starting transfers between devices  59.1 us (40%)
  waiting for transfers between devices  48.8 us (33%)
  matrix products  14.4 us (10%)
  local copies, waits for them, and re-layouts  13.3 us (9%)
  other arithmetic  5.58 us (4%)
  Pallas kernels  5.25 us (4%)
    ppermute x18, starting transfers between devices, swap(): return lax.ppermute(x, axis, [(0, 1), (1, 0)])  26.2 us
    all_to_all x2, waiting for transfers between devices, gather_zx(): return lax.all_to_all(copies, ZX, 0, 0)  17.6 us
    ppermute x12, starting transfers between devices, shift(): return lax.ppermute(x, axis, [(i, (i + k) % n) for i in range(n)])  16.7 us
    ppermute x12, waiting for transfers between devices, shift(): return lax.ppermute(x, axis, [(i, (i + k) % n) for i in range(n)])  16.5 us
    dot_general x19, matrix products, dot(): lax.dot_general(a, b, (((i,), (j,)), ((), ())), preferred_element_type=F32)  14.4 us
    all_to_all x2, starting transfers between devices, gather_zx(): return lax.all_to_all(copies, ZX, 0, 0)  12.6 us
    all_to_all x1, waiting for transfers between devices, shards(): sums = lax.all_to_all(total.reshape(groups, rows, count), ZX, 0, 0)  9.85 us
    pallas_call x1, Pallas kernels, regroup(): pl.pallas_call(functools.partial(regroup_kernel, rows), grid_spec=pltpu.P...  5.25 us
  transfers between devices with their start and end apart: 33, of which 10 were waited for; matrix products, arithmetic and copies ran while one was open for 16% of the time, Pallas kernels for 4%

profile of v3, /device:TPU:1, one launch (start us, length us, event | category | flops | bytes accessed | tf_op | source)
XLA Modules:
  0.0 147.8 jit_solution(2773970580690486696)
XLA Ops:
  1.5 3.2 %collective-permute-start = (bf16[36,128]{1,0:T(8,128)(2,1)S(1)}, bf16[36,128]{1,0:T(8,128)(2,1)S(1)}, u32[]{:S(2)}, u32[]{:S(2)}) collective-permute-start(bf16[36,128]{1,0:T(8,128)(2,1)S(1)} %broadcast_select_fusion.10), channel_id=1, source_target_pairs={{0,1},{1,0},{2,3},{3,2},{4,5},{5,4},{6,7},{7,6},{8,9},{9,8},{10,11... | collective-permute-start | bytes 27656 | tf_op jit(solution)/shard_map/ppermute | solution.py:18
  7.1 9.0 %all-to-all-start = ((bf16[16,72,128]{2,1,0:T(8,128)(2,1)}), bf16[16,72,128]{2,1,0:T(8,128)(2,1)S(1)}, u32[]{:S(2)}, u32[]{:S(2)}) async-start(bf16[16,72,128]{2,1,0:T(8,128)(2,1)} %broadcast_in_dim.24), calls=%async_computation | async-start | bytes 589824 | tf_op jit(solution)/shard_map/all_to_all | solution.py:50
  16.1 5.2 %regroup.1 = bf16[4,288,1152]{2,1,0:T(8,128)(2,1)} custom-call(s32[1]{0:T(128)} %bitcast.1.y_ref, bf16[288,4608]{1,0:T(8,128)(2,1)} %w_ref), custom_call_target="tpu_custom_call" | custom-call | bytes 5308416 | tf_op jit(solution)/shard_map/regroup/pallas_call | solution.py:89
  21.4 7.9 %all-to-all-done = bf16[16,72,128]{2,1,0:T(8,128)(2,1)S(1)} async-done(((bf16[16,72,128]{2,1,0:T(8,128)(2,1)}), bf16[16,72,128]{2,1,0:T(8,128)(2,1)S(1)}, u32[]{:S(2)}, u32[]{:S(2)}) %all-to-all-start) | async-done | bytes 294944 | tf_op jit(solution)/shard_map/all_to_all | solution.py:50
  29.3 1.3 collective-permute-start.1
  30.6 1.4 collective-permute-start.2
  32.0 1.6 %collective-permute-start.3 = (bf16[16,1,72,128]{3,2,1,0:T(8,128)(2,1)S(1)}, bf16[16,1,72,128]{3,2,1,0:T(8,128)(2,1)S(1)}, u32[]{:S(2)}, u32[]{:S(2)}) collective-permute-start(bf16[16,1,72,128]{3,2,1,0:T(8,128)(2,1)S(1)} %bitcast.123), channel_id=1, source_target_pairs={{0,4},{2,6},{4,0},{6,2},{1,5},{3,7},{5,1},{7,3},{8,12},{10,14},{12... | collective-permute-start | bytes 884744 | tf_op jit(solution)/shard_map/ppermute | solution.py:23
  33.7 1.3 broadcast_select_fusion.6
  35.0 2.7 %collective-permute-start.13 = (bf16[36,128]{1,0:T(8,128)(2,1)}, bf16[36,128]{1,0:T(8,128)(2,1)S(1)}, u32[]{:S(2)}, u32[]{:S(2)}) collective-permute-start(bf16[36,128]{1,0:T(8,128)(2,1)} %broadcast_select_fusion.6), channel_id=1, source_target_pairs={{0,1},{1,0},{2,3},{3,2},{4,5},{5,4},{6,7},{7,6},{8,9},{9,8},{10,11... | collective-permute-start | bytes 27656 | tf_op jit(solution)/shard_map/ppermute | solution.py:18
  39.1 5.5 %collective-permute-done.3 = bf16[16,1,72,128]{3,2,1,0:T(8,128)(2,1)S(1)} collective-permute-done((bf16[16,1,72,128]{3,2,1,0:T(8,128)(2,1)S(1)}, bf16[16,1,72,128]{3,2,1,0:T(8,128)(2,1)S(1)}, u32[]{:S(2)}, u32[]{:S(2)}) %collective-permute-start.3) | collective-permute-done | bytes 294944 | tf_op jit(solution)/shard_map/ppermute | solution.py:23
  44.7 2.9 %collective-permute-start.4 = (bf16[4608,128]{1,0:T(8,128)(2,1)S(1)}, bf16[4608,128]{1,0:T(8,128)(2,1)S(1)}, u32[]{:S(2)}, u32[]{:S(2)}) collective-permute-start(bf16[4608,128]{1,0:T(8,128)(2,1)S(1)} %bitcast.113), channel_id=1, source_target_pairs={{0,1},{1,0},{2,3},{3,2},{4,5},{5,4},{6,7},{7,6},{8,9},{9,8},{10,11... | collective-permute-start | bytes 3538952 | tf_op jit(solution)/shard_map/ppermute | solution.py:18
  56.3 1.9 %collective-permute-start.7 = (bf16[1152,128]{1,0:T(8,128)(2,1)S(1)}, bf16[1152,128]{1,0:T(8,128)(2,1)S(1)}, u32[]{:S(2)}, u32[]{:S(2)}) collective-permute-start(bf16[1152,128]{1,0:T(8,128)(2,1)S(1)} %add_convert_fusion.3), channel_id=1, source_target_pairs={{0,4},{2,6},{4,0},{6,2},{1,5},{3,7},{5,1},{7,3},{8,12},{10,14},{12... | collective-permute-start | bytes 884744 | tf_op jit(solution)/shard_map/ppermute | solution.py:23
  59.5 2.4 %collective-permute-start.11 = (bf16[1152,128]{1,0:T(8,128)(2,1)S(1)}, bf16[1152,128]{1,0:T(8,128)(2,1)S(1)}, u32[]{:S(2)}, u32[]{:S(2)}) collective-permute-start(bf16[1152,128]{1,0:T(8,128)(2,1)S(1)} %add_convert_fusion.1), channel_id=1, source_target_pairs={{0,6},{2,0},{4,2},{6,4},{1,7},{3,1},{5,3},{7,5},{8,14},{10,8},{12,... | collective-permute-start | bytes 884744 | tf_op jit(solution)/shard_map/ppermute | solution.py:23
  62.5 3.7 %collective-permute-done.7 = bf16[1152,128]{1,0:T(8,128)(2,1)S(1)} collective-permute-done((bf16[1152,128]{1,0:T(8,128)(2,1)S(1)}, bf16[1152,128]{1,0:T(8,128)(2,1)S(1)}, u32[]{:S(2)}, u32[]{:S(2)}) %collective-permute-start.7) | collective-permute-done | bytes 294944 | tf_op jit(solution)/shard_map/ppermute | solution.py:23
  66.2 6.9 %collective-permute-done.9 = bf16[1152,128]{1,0:T(8,128)(2,1)S(1)} collective-permute-done((bf16[1152,128]{1,0:T(8,128)(2,1)S(1)}, bf16[1152,128]{1,0:T(8,128)(2,1)S(1)}, u32[]{:S(2)}, u32[]{:S(2)}) %collective-permute-start.9) | collective-permute-done | bytes 294944 | tf_op jit(solution)/shard_map/ppermute | solution.py:23
  74.0 3.6 %all-to-all-start.1 = ((bf16[16,72,128]{2,1,0:T(8,128)(2,1)}), bf16[16,72,128]{2,1,0:T(8,128)(2,1)S(1)}, u32[]{:S(2)}, u32[]{:S(2)}) async-start(bf16[16,72,128]{2,1,0:T(8,128)(2,1)} %bitcast.16), calls=%async_computation.1 | async-start | bytes 589824 | tf_op jit(solution)/shard_map/all_to_all | solution.py:143
  77.6 1.9 %constant_dynamic-slice_fusion.3 = bf16[2304,128]{1,0:T(8,128)(2,1)} fusion(bf16[4608,128]{1,0:T(8,128)(2,1)} %bitcast.116, s32[]{:T(128)S(6)} %select_n.95), kind=kLoop, calls=%fused_computation.138 | loop fusion | bytes 1179652 | tf_op jit(solution)/shard_map/dynamic_slice | solution.py:148
  80.2 9.9 %all-to-all-done.1 = bf16[16,72,128]{2,1,0:T(8,128)(2,1)S(1)} async-done(((bf16[16,72,128]{2,1,0:T(8,128)(2,1)}), bf16[16,72,128]{2,1,0:T(8,128)(2,1)S(1)}, u32[]{:S(2)}, u32[]{:S(2)}) %all-to-all-start.1) | async-done | bytes 294944 | tf_op jit(solution)/shard_map/all_to_all | solution.py:143
  91.3 2.7 %collective-permute-start.14 = (bf16[36,128]{1,0:T(8,128)(2,1)}, bf16[36,128]{1,0:T(8,128)(2,1)S(1)}, u32[]{:S(2)}, u32[]{:S(2)}) collective-permute-start(bf16[36,128]{1,0:T(8,128)(2,1)} %broadcast_select_fusion.2), channel_id=1, source_target_pairs={{0,1},{1,0},{2,3},{3,2},{4,5},{5,4},{6,7},{7,6},{8,9},{9,8},{10,11... | collective-permute-start | bytes 27656 | tf_op jit(solution)/shard_map/ppermute | solution.py:18
  94.8 3.5 %all-to-all-start.2 = ((bf16[16,72,128]{2,1,0:T(8,128)(2,1)}), bf16[16,72,128]{2,1,0:T(8,128)(2,1)S(1)}, u32[]{:S(2)}, u32[]{:S(2)}) async-start(bf16[16,72,128]{2,1,0:T(8,128)(2,1)} %broadcast_in_dim.53), calls=%async_computation.2 | async-start | bytes 589824 | tf_op jit(solution)/shard_map/all_to_all | solution.py:50
  99.4 1.9 %constant_dynamic-slice_fusion.2 = bf16[2304,128]{1,0:T(8,128)(2,1)} fusion(bf16[4608,128]{1,0:T(8,128)(2,1)} %bitcast.117, s32[]{:T(128)S(6)} %select_n.100), kind=kLoop, calls=%fused_computation.137 | loop fusion | bytes 1179652 | tf_op jit(solution)/shard_map/dynamic_slice | solution.py:152
  102.3 9.7 %all-to-all-done.2 = bf16[16,72,128]{2,1,0:T(8,128)(2,1)S(1)} async-done(((bf16[16,72,128]{2,1,0:T(8,128)(2,1)}), bf16[16,72,128]{2,1,0:T(8,128)(2,1)S(1)}, u32[]{:S(2)}, u32[]{:S(2)}) %all-to-all-start.2) | async-done | bytes 294944 | tf_op jit(solution)/shard_map/all_to_all | solution.py:50
  112.8 1.9 %collective-permute-start.19 = (bf16[16,72,128]{2,1,0:T(8,128)(2,1)S(1)}, bf16[16,72,128]{2,1,0:T(8,128)(2,1)S(1)}, u32[]{:S(2)}, u32[]{:S(2)}) collective-permute-start(bf16[16,72,128]{2,1,0:T(8,128)(2,1)S(1)} %all-to-all-done.2), channel_id=1, source_target_pairs={{0,6},{2,0},{4,2},{6,4},{1,7},{3,1},{5,3},{7,5},{8,14},{10,8},{12,... | collective-permute-start | bytes 884744 | tf_op jit(solution)/shard_map/ppermute | solution.py:23
  115.2 2.9 %collective-permute-start.22 = (bf16[1152,128]{1,0:T(8,128)(2,1)S(1)}, bf16[1152,128]{1,0:T(8,128)(2,1)S(1)}, u32[]{:S(2)}, u32[]{:S(2)}) collective-permute-start(bf16[1152,128]{1,0:T(8,128)(2,1)S(1)} %bitcast.118), channel_id=1, source_target_pairs={{0,1},{1,0},{2,3},{3,2},{4,5},{5,4},{6,7},{7,6},{8,9},{9,8},{10,11... | collective-permute-start | bytes 884744 | tf_op jit(solution)/shard_map/ppermute | solution.py:18
  122.3 2.8 %collective-permute-start.23 = (bf16[1152,128]{1,0:T(8,128)(2,1)S(1)}, bf16[1152,128]{1,0:T(8,128)(2,1)S(1)}, u32[]{:S(2)}, u32[]{:S(2)}) collective-permute-start(bf16[1152,128]{1,0:T(8,128)(2,1)S(1)} %bitcast.128), channel_id=1, source_target_pairs={{0,1},{1,0},{2,3},{3,2},{4,5},{5,4},{6,7},{7,6},{8,9},{9,8},{10,11... | collective-permute-start | bytes 884744 | tf_op jit(solution)/shard_map/ppermute | solution.py:18
  125.1 3.1 %collective-permute-start.20 = (bf16[1152,128]{1,0:T(8,128)(2,1)S(1)}, bf16[1152,128]{1,0:T(8,128)(2,1)S(1)}, u32[]{:S(2)}, u32[]{:S(2)}) collective-permute-start(bf16[1152,128]{1,0:T(8,128)(2,1)S(1)} %bitcast.132), channel_id=1, source_target_pairs={{0,1},{1,0},{2,3},{3,2},{4,5},{5,4},{6,7},{7,6},{8,9},{9,8},{10,11... | collective-permute-start | bytes 884744 | tf_op jit(solution)/shard_map/ppermute | solution.py:18
  131.6 3.4 %collective-permute-start.27 = (bf16[8,72,128]{2,1,0:T(8,128)(2,1)S(1)}, bf16[8,72,128]{2,1,0:T(8,128)(2,1)S(1)}, u32[]{:S(2)}, u32[]{:S(2)}) collective-permute-start(bf16[8,72,128]{2,1,0:T(8,128)(2,1)S(1)} %collective-permute-done.24), channel_id=1, source_target_pairs={{0,4},{2,6},{4,0},{6,2},{1,5},{3,7},{5,1},{7,3},{8,12},{10,14},{12... | collective-permute-start | bytes 442376 | tf_op jit(solution)/shard_map/ppermute | solution.py:23
  135.5 4.0 %collective-permute-done.25 = bf16[288,256]{1,0:T(8,128)(2,1)S(1)} collective-permute-done((bf16[288,256]{1,0:T(8,128)(2,1)S(1)}, bf16[288,256]{1,0:T(8,128)(2,1)S(1)}, u32[]{:S(2)}, u32[]{:S(2)}) %collective-permute-start.25) | collective-permute-done | bytes 147488 | tf_op jit(solution)/shard_map/ppermute | solution.py:18
  139.5 2.0 %fusion.61 = bf16[2304,288]{0,1:T(8,128)(2,1)} fusion(bf16[2304,512]{1,0:T(8,128)(2,1)S(1)} %constant_dynamic-update-slice_fusion, bf16[288,256]{1,0:T(8,128)(2,1)S(1)} %get-tuple-element.70, bf16[288,256]{1,0:T(8,128)(2,1)S(1)} %get-tuple-element.68), kind=kOutput, calls=%fused_computation.79 | convolution fusion | flops 680067072 | bytes 3981312 | tf_op jit(solution)/shard_map/dot_general | solution.py:65
  142.0 1.6 %collective-permute-start.29 = (bf16[2304,128]{1,0:T(8,128)(2,1)S(1)}, bf16[2304,128]{1,0:T(8,128)(2,1)S(1)}, u32[]{:S(2)}, u32[]{:S(2)}) collective-permute-start(bf16[2304,128]{1,0:T(8,128)(2,1)S(1)} %bitcast.125), channel_id=1, source_target_pairs={{0,1},{1,0},{2,3},{3,2},{4,5},{5,4},{6,7},{7,6},{8,9},{9,8},{10,11... | collective-permute-start | bytes 1769480 | tf_op jit(solution)/shard_map/ppermute | solution.py:18
  143.9 1.9 %convolution_convert_fusion.1 = bf16[2304,288]{0,1:T(8,128)(2,1)} fusion(bf16[2304,512]{1,0:T(8,128)(2,1)S(1)} %constant_dynamic-update-slice_fusion, bf16[288,256]{1,0:T(8,128)(2,1)S(1)} %get-tuple-element.69, bf16[288,256]{1,0:T(8,128)(2,1)S(1)} %get-tuple-element.66), kind=kOutput, calls=%fused_computation.1 | convolution fusion | flops 680730624 | bytes 3981312 | tf_op jit(solution)/shard_map/dot_general | solution.py:65
  145.8 2.0 %convolution_convert_fusion = bf16[288,2304]{1,0:T(8,128)(2,1)} fusion(bf16[2304,128]{1,0:T(8,128)(2,1)S(1)} %collective-permute-done.29, bf16[2304,128]{1,0:T(8,128)(2,1)S(1)} %bitcast.126, bf16[2304,256]{1,0:T(8,128)(2,1)S(1)} %bitcast.120, bf16[288,256]{1,0:T(8,128)(2,1)S(1)} %copy-done.20, bf16[288,128]{1,0:T(8,128)(2,1)S(1)} %copy-done.23, ...), kind=kOutput, calls=%fused_computation | convolution fusion | flops 688103424 | bytes 3981312 | tf_op jit(solution)/shard_map/dot_general | solution.py:65
  (147 shorter events, 30.5 us)
Async XLA Ops:
  1.5 4.1 %collective-permute-start = (bf16[36,128]{1,0:T(8,128)(2,1)S(1)}, bf16[36,128]{1,0:T(8,128)(2,1)S(1)}, u32[]{:S(2)}, u32[]{:S(2)}) collective-permute-start(bf16[36,128]{1,0:T(8,128)(2,1)S(1)} %broadcast_select_fusion.10), channel_id=1, source_target_pairs={{0,1},{1,0},{2,3},{3,2},{4,5},{5,4},{6,7},{7,6},{8,9},{9,8},{10,11... | collective-permute-start | bytes 27656 | tf_op jit(solution)/shard_map/ppermute | solution.py:18
  7.1 22.2 %all-to-all-start = ((bf16[16,72,128]{2,1,0:T(8,128)(2,1)}), bf16[16,72,128]{2,1,0:T(8,128)(2,1)S(1)}, u32[]{:S(2)}, u32[]{:S(2)}) async-start(bf16[16,72,128]{2,1,0:T(8,128)(2,1)} %broadcast_in_dim.24), calls=%async_computation | async-start | bytes 589824 | tf_op jit(solution)/shard_map/all_to_all | solution.py:50
  29.3 8.4 %collective-permute-start.1 = (bf16[16,1,72,128]{3,2,1,0:T(8,128)(2,1)S(1)}, bf16[16,1,72,128]{3,2,1,0:T(8,128)(2,1)}, u32[]{:S(2)}, u32[]{:S(2)}) collective-permute-start(bf16[16,1,72,128]{3,2,1,0:T(8,128)(2,1)S(1)} %bitcast.121), channel_id=1, source_target_pairs={{0,2},{2,4},{4,6},{6,0},{1,3},{3,5},{5,7},{7,1},{8,10},{10,12},{12... | collective-permute-start | bytes 884744 | tf_op jit(solution)/shard_map/ppermute | solution.py:23
  30.6 8.5 %collective-permute-start.2 = (bf16[16,1,72,128]{3,2,1,0:T(8,128)(2,1)S(1)}, bf16[16,1,72,128]{3,2,1,0:T(8,128)(2,1)S(1)}, u32[]{:S(2)}, u32[]{:S(2)}) collective-permute-start(bf16[16,1,72,128]{3,2,1,0:T(8,128)(2,1)S(1)} %bitcast.122), channel_id=1, source_target_pairs={{0,6},{2,0},{4,2},{6,4},{1,7},{3,1},{5,3},{7,5},{8,14},{10,8},{12,... | collective-permute-start | bytes 884744 | tf_op jit(solution)/shard_map/ppermute | solution.py:23
  32.0 12.6 %collective-permute-start.3 = (bf16[16,1,72,128]{3,2,1,0:T(8,128)(2,1)S(1)}, bf16[16,1,72,128]{3,2,1,0:T(8,128)(2,1)S(1)}, u32[]{:S(2)}, u32[]{:S(2)}) collective-permute-start(bf16[16,1,72,128]{3,2,1,0:T(8,128)(2,1)S(1)} %bitcast.123), channel_id=1, source_target_pairs={{0,4},{2,6},{4,0},{6,2},{1,5},{3,7},{5,1},{7,3},{8,12},{10,14},{12... | collective-permute-start | bytes 884744 | tf_op jit(solution)/shard_map/ppermute | solution.py:23
  35.0 12.6 %collective-permute-start.13 = (bf16[36,128]{1,0:T(8,128)(2,1)}, bf16[36,128]{1,0:T(8,128)(2,1)S(1)}, u32[]{:S(2)}, u32[]{:S(2)}) collective-permute-start(bf16[36,128]{1,0:T(8,128)(2,1)} %broadcast_select_fusion.6), channel_id=1, source_target_pairs={{0,1},{1,0},{2,3},{3,2},{4,5},{5,4},{6,7},{7,6},{8,9},{9,8},{10,11... | collective-permute-start | bytes 27656 | tf_op jit(solution)/shard_map/ppermute | solution.py:18
  44.7 6.0 %collective-permute-start.4 = (bf16[4608,128]{1,0:T(8,128)(2,1)S(1)}, bf16[4608,128]{1,0:T(8,128)(2,1)S(1)}, u32[]{:S(2)}, u32[]{:S(2)}) collective-permute-start(bf16[4608,128]{1,0:T(8,128)(2,1)S(1)} %bitcast.113), channel_id=1, source_target_pairs={{0,1},{1,0},{2,3},{3,2},{4,5},{5,4},{6,7},{7,6},{8,9},{9,8},{10,11... | collective-permute-start | bytes 3538952 | tf_op jit(solution)/shard_map/ppermute | solution.py:18
  53.6 2.2 %collective-permute-start.6 = (bf16[1152,128]{1,0:T(8,128)(2,1)S(1)}, bf16[1152,128]{1,0:T(8,128)(2,1)S(1)}, u32[]{:S(2)}, u32[]{:S(2)}) collective-permute-start(bf16[1152,128]{1,0:T(8,128)(2,1)S(1)} %convolution_convert_fusion.4), channel_id=1, source_target_pairs={{0,1},{1,0},{2,3},{3,2},{4,5},{5,4},{6,7},{7,6},{8,9},{9,8},{10,11... | collective-permute-start | bytes 884744 | tf_op jit(solution)/shard_map/ppermute | solution.py:18
  54.2 4.0 %collective-permute-start.8 = (bf16[1152,128]{1,0:T(8,128)(2,1)S(1)}, bf16[1152,128]{1,0:T(8,128)(2,1)S(1)}, u32[]{:S(2)}, u32[]{:S(2)}) collective-permute-start(bf16[1152,128]{1,0:T(8,128)(2,1)S(1)} %convolution_convert_fusion.3), channel_id=1, source_target_pairs={{0,1},{1,0},{2,3},{3,2},{4,5},{5,4},{6,7},{7,6},{8,9},{9,8},{10,11... | collective-permute-start | bytes 884744 | tf_op jit(solution)/shard_map/ppermute | solution.py:18
  55.2 7.3 %collective-permute-start.5 = (bf16[1152,128]{1,0:T(8,128)(2,1)S(1)}, bf16[1152,128]{1,0:T(8,128)(2,1)S(1)}, u32[]{:S(2)}, u32[]{:S(2)}) collective-permute-start(bf16[1152,128]{1,0:T(8,128)(2,1)S(1)} %convolution_convert_fusion.5), channel_id=1, source_target_pairs={{0,1},{1,0},{2,3},{3,2},{4,5},{5,4},{6,7},{7,6},{8,9},{9,8},{10,11... | collective-permute-start | bytes 884744 | tf_op jit(solution)/shard_map/ppermute | solution.py:18
  55.3 3.7 %collective-permute-start.10 = (bf16[1152,128]{1,0:T(8,128)(2,1)S(1)}, bf16[1152,128]{1,0:T(8,128)(2,1)S(1)}, u32[]{:S(2)}, u32[]{:S(2)}) collective-permute-start(bf16[1152,128]{1,0:T(8,128)(2,1)S(1)} %convolution_convert_fusion.2), channel_id=1, source_target_pairs={{0,1},{1,0},{2,3},{3,2},{4,5},{5,4},{6,7},{7,6},{8,9},{9,8},{10,11... | collective-permute-start | bytes 884744 | tf_op jit(solution)/shard_map/ppermute | solution.py:18
  56.3 10.0 %collective-permute-start.7 = (bf16[1152,128]{1,0:T(8,128)(2,1)S(1)}, bf16[1152,128]{1,0:T(8,128)(2,1)S(1)}, u32[]{:S(2)}, u32[]{:S(2)}) collective-permute-start(bf16[1152,128]{1,0:T(8,128)(2,1)S(1)} %add_convert_fusion.3), channel_id=1, source_target_pairs={{0,4},{2,6},{4,0},{6,2},{1,5},{3,7},{5,1},{7,3},{8,12},{10,14},{12... | collective-permute-start | bytes 884744 | tf_op jit(solution)/shard_map/ppermute | solution.py:23
  58.6 14.5 %collective-permute-start.9 = (bf16[1152,128]{1,0:T(8,128)(2,1)S(1)}, bf16[1152,128]{1,0:T(8,128)(2,1)S(1)}, u32[]{:S(2)}, u32[]{:S(2)}) collective-permute-start(bf16[1152,128]{1,0:T(8,128)(2,1)S(1)} %add_convert_fusion.2), channel_id=1, source_target_pairs={{0,2},{2,4},{4,6},{6,0},{1,3},{3,5},{5,7},{7,1},{8,10},{10,12},{12... | collective-permute-start | bytes 884744 | tf_op jit(solution)/shard_map/ppermute | solution.py:23
  59.5 13.6 %collective-permute-start.11 = (bf16[1152,128]{1,0:T(8,128)(2,1)S(1)}, bf16[1152,128]{1,0:T(8,128)(2,1)S(1)}, u32[]{:S(2)}, u32[]{:S(2)}) collective-permute-start(bf16[1152,128]{1,0:T(8,128)(2,1)S(1)} %add_convert_fusion.1), channel_id=1, source_target_pairs={{0,6},{2,0},{4,2},{6,4},{1,7},{3,1},{5,3},{7,5},{8,14},{10,8},{12,... | collective-permute-start | bytes 884744 | tf_op jit(solution)/shard_map/ppermute | solution.py:23
  62.1 11.9 %collective-permute-start.12 = (bf16[3,288,256]{2,1,0:T(8,128)(2,1)S(1)}, bf16[3,288,256]{2,1,0:T(8,128)(2,1)S(1)}, u32[]{:S(2)}, u32[]{:S(2)}) collective-permute-start(bf16[3,288,256]{2,1,0:T(8,128)(2,1)S(1)} %pad_maximum_fusion), channel_id=1, source_target_pairs={{0,128},{128,0},{1,129},{129,1},{2,130},{130,2},{3,131},{131,3},{4... | collective-permute-start | bytes 1327112 | tf_op jit(solution)/shard_map/ppermute | solution.py:18
  74.0 16.1 %all-to-all-start.1 = ((bf16[16,72,128]{2,1,0:T(8,128)(2,1)}), bf16[16,72,128]{2,1,0:T(8,128)(2,1)S(1)}, u32[]{:S(2)}, u32[]{:S(2)}) async-start(bf16[16,72,128]{2,1,0:T(8,128)(2,1)} %bitcast.16), calls=%async_computation.1 | async-start | bytes 589824 | tf_op jit(solution)/shard_map/all_to_all | solution.py:143
  91.3 10.3 %collective-permute-start.14 = (bf16[36,128]{1,0:T(8,128)(2,1)}, bf16[36,128]{1,0:T(8,128)(2,1)S(1)}, u32[]{:S(2)}, u32[]{:S(2)}) collective-permute-start(bf16[36,128]{1,0:T(8,128)(2,1)} %broadcast_select_fusion.2), channel_id=1, source_target_pairs={{0,1},{1,0},{2,3},{3,2},{4,5},{5,4},{6,7},{7,6},{8,9},{9,8},{10,11... | collective-permute-start | bytes 27656 | tf_op jit(solution)/shard_map/ppermute | solution.py:18
  94.8 17.2 %all-to-all-start.2 = ((bf16[16,72,128]{2,1,0:T(8,128)(2,1)}), bf16[16,72,128]{2,1,0:T(8,128)(2,1)S(1)}, u32[]{:S(2)}, u32[]{:S(2)}) async-start(bf16[16,72,128]{2,1,0:T(8,128)(2,1)} %broadcast_in_dim.53), calls=%async_computation.2 | async-start | bytes 589824 | tf_op jit(solution)/shard_map/all_to_all | solution.py:50
  101.4 18.1 %collective-permute-start.15 = (bf16[2304,128]{1,0:T(8,128)(2,1)}, bf16[2304,128]{1,0:T(8,128)(2,1)}, u32[]{:S(2)}, u32[]{:S(2)}) collective-permute-start(bf16[2304,128]{1,0:T(8,128)(2,1)} %constant_dynamic-slice_fusion.3), channel_id=1, source_target_pairs={{0,128},{128,0},{1,129},{129,1},{2,130},{130,2},{3,131},{131,3},{4... | collective-permute-start | bytes 1769480 | tf_op jit(solution)/shard_map/ppermute | solution.py:18
  112.0 10.3 %collective-permute-start.21 = (bf16[16,72,128]{2,1,0:T(8,128)(2,1)S(1)}, bf16[16,72,128]{2,1,0:T(8,128)(2,1)S(1)}, u32[]{:S(2)}, u32[]{:S(2)}) collective-permute-start(bf16[16,72,128]{2,1,0:T(8,128)(2,1)S(1)} %all-to-all-done.2), channel_id=1, source_target_pairs={{0,2},{2,4},{4,6},{6,0},{1,3},{3,5},{5,7},{7,1},{8,10},{10,12},{12... | collective-permute-start | bytes 884744 | tf_op jit(solution)/shard_map/ppermute | solution.py:23
  112.8 12.3 %collective-permute-start.19 = (bf16[16,72,128]{2,1,0:T(8,128)(2,1)S(1)}, bf16[16,72,128]{2,1,0:T(8,128)(2,1)S(1)}, u32[]{:S(2)}, u32[]{:S(2)}) collective-permute-start(bf16[16,72,128]{2,1,0:T(8,128)(2,1)S(1)} %all-to-all-done.2), channel_id=1, source_target_pairs={{0,6},{2,0},{4,2},{6,4},{1,7},{3,1},{5,3},{7,5},{8,14},{10,8},{12,... | collective-permute-start | bytes 884744 | tf_op jit(solution)/shard_map/ppermute | solution.py:23
  114.7 13.6 %collective-permute-start.17 = (bf16[16,72,128]{2,1,0:T(8,128)(2,1)S(1)}, bf16[16,72,128]{2,1,0:T(8,128)(2,1)S(1)}, u32[]{:S(2)}, u32[]{:S(2)}) collective-permute-start(bf16[16,72,128]{2,1,0:T(8,128)(2,1)S(1)} %all-to-all-done.2), channel_id=1, source_target_pairs={{0,4},{2,6},{4,0},{6,2},{1,5},{3,7},{5,1},{7,3},{8,12},{10,14},{12... | collective-permute-start | bytes 884744 | tf_op jit(solution)/shard_map/ppermute | solution.py:23
  115.2 5.8 %collective-permute-start.22 = (bf16[1152,128]{1,0:T(8,128)(2,1)S(1)}, bf16[1152,128]{1,0:T(8,128)(2,1)S(1)}, u32[]{:S(2)}, u32[]{:S(2)}) collective-permute-start(bf16[1152,128]{1,0:T(8,128)(2,1)S(1)} %bitcast.118), channel_id=1, source_target_pairs={{0,1},{1,0},{2,3},{3,2},{4,5},{5,4},{6,7},{7,6},{8,9},{9,8},{10,11... | collective-permute-start | bytes 884744 | tf_op jit(solution)/shard_map/ppermute | solution.py:18
  119.5 11.2 %collective-permute-start.24 = (bf16[8,72,128]{2,1,0:T(8,128)(2,1)S(1)}, bf16[8,72,128]{2,1,0:T(8,128)(2,1)S(1)}, u32[]{:S(2)}, u32[]{:S(2)}) collective-permute-start(bf16[8,72,128]{2,1,0:T(8,128)(2,1)S(1)} %constant_dynamic-slice_fusion), channel_id=1, source_target_pairs={{0,128},{128,0},{1,129},{129,1},{2,130},{130,2},{3,131},{131,3},{4... | collective-permute-start | bytes 442376 | tf_op jit(solution)/shard_map/ppermute | solution.py:18
  121.1 14.3 %collective-permute-start.16 = (bf16[2304,128]{1,0:T(8,128)(2,1)}, bf16[2304,128]{1,0:T(8,128)(2,1)S(1)}, u32[]{:S(2)}, u32[]{:S(2)}) collective-permute-start(bf16[2304,128]{1,0:T(8,128)(2,1)} %collective-permute-done.15), channel_id=1, source_target_pairs={{0,1},{1,0},{2,3},{3,2},{4,5},{5,4},{6,7},{7,6},{8,9},{9,8},{10,11... | collective-permute-start | bytes 1769480 | tf_op jit(solution)/shard_map/ppermute | solution.py:18
  122.3 6.8 %collective-permute-start.23 = (bf16[1152,128]{1,0:T(8,128)(2,1)S(1)}, bf16[1152,128]{1,0:T(8,128)(2,1)S(1)}, u32[]{:S(2)}, u32[]{:S(2)}) collective-permute-start(bf16[1152,128]{1,0:T(8,128)(2,1)S(1)} %bitcast.128), channel_id=1, source_target_pairs={{0,1},{1,0},{2,3},{3,2},{4,5},{5,4},{6,7},{7,6},{8,9},{9,8},{10,11... | collective-permute-start | bytes 884744 | tf_op jit(solution)/shard_map/ppermute | solution.py:18
  125.1 4.5 %collective-permute-start.20 = (bf16[1152,128]{1,0:T(8,128)(2,1)S(1)}, bf16[1152,128]{1,0:T(8,128)(2,1)S(1)}, u32[]{:S(2)}, u32[]{:S(2)}) collective-permute-start(bf16[1152,128]{1,0:T(8,128)(2,1)S(1)} %bitcast.132), channel_id=1, source_target_pairs={{0,1},{1,0},{2,3},{3,2},{4,5},{5,4},{6,7},{7,6},{8,9},{9,8},{10,11... | collective-permute-start | bytes 884744 | tf_op jit(solution)/shard_map/ppermute | solution.py:18
  130.7 10.8 %collective-permute-start.26 = (bf16[8,72,128]{2,1,0:T(8,128)(2,1)S(1)}, bf16[8,72,128]{2,1,0:T(8,128)(2,1)S(1)}, u32[]{:S(2)}, u32[]{:S(2)}) collective-permute-start(bf16[8,72,128]{2,1,0:T(8,128)(2,1)S(1)} %collective-permute-done.24), channel_id=1, source_target_pairs={{0,2},{2,4},{4,6},{6,0},{1,3},{3,5},{5,7},{7,1},{8,10},{10,12},{12... | collective-permute-start | bytes 442376 | tf_op jit(solution)/shard_map/ppermute | solution.py:23
  131.6 10.2 %collective-permute-start.27 = (bf16[8,72,128]{2,1,0:T(8,128)(2,1)S(1)}, bf16[8,72,128]{2,1,0:T(8,128)(2,1)S(1)}, u32[]{:S(2)}, u32[]{:S(2)}) collective-permute-start(bf16[8,72,128]{2,1,0:T(8,128)(2,1)S(1)} %collective-permute-done.24), channel_id=1, source_target_pairs={{0,4},{2,6},{4,0},{6,2},{1,5},{3,7},{5,1},{7,3},{8,12},{10,14},{12... | collective-permute-start | bytes 442376 | tf_op jit(solution)/shard_map/ppermute | solution.py:23
  135.0 6.8 %collective-permute-start.28 = (bf16[8,72,128]{2,1,0:T(8,128)(2,1)S(1)}, bf16[8,72,128]{2,1,0:T(8,128)(2,1)S(1)}, u32[]{:S(2)}, u32[]{:S(2)}) collective-permute-start(bf16[8,72,128]{2,1,0:T(8,128)(2,1)S(1)} %collective-permute-done.24), channel_id=1, source_target_pairs={{0,6},{2,0},{4,2},{6,4},{1,7},{3,1},{5,3},{7,5},{8,14},{10,8},{12,... | collective-permute-start | bytes 442376 | tf_op jit(solution)/shard_map/ppermute | solution.py:23
  135.0 4.4 %collective-permute-start.25 = (bf16[288,256]{1,0:T(8,128)(2,1)S(1)}, bf16[288,256]{1,0:T(8,128)(2,1)S(1)}, u32[]{:S(2)}, u32[]{:S(2)}) collective-permute-start(bf16[288,256]{1,0:T(8,128)(2,1)S(1)} %get-tuple-element.59), channel_id=1, source_target_pairs={{0,128},{128,0},{1,129},{129,1},{2,130},{130,2},{3,131},{131,3},{4... | collective-permute-start | bytes 442376 | tf_op jit(solution)/shard_map/ppermute | solution.py:18
  142.0 3.8 %collective-permute-start.29 = (bf16[2304,128]{1,0:T(8,128)(2,1)S(1)}, bf16[2304,128]{1,0:T(8,128)(2,1)S(1)}, u32[]{:S(2)}, u32[]{:S(2)}) collective-permute-start(bf16[2304,128]{1,0:T(8,128)(2,1)S(1)} %bitcast.125), channel_id=1, source_target_pairs={{0,1},{1,0},{2,3},{3,2},{4,5},{5,4},{6,7},{7,6},{8,9},{9,8},{10,11... | collective-permute-start | bytes 1769480 | tf_op jit(solution)/shard_map/ppermute | solution.py:18
  (25 other events, 195.6 us)

commit v4 on v3

--- a/solution.py
+++ b/solution.py
@@ -142,7 +142,6 @@
     total, held_p, teach = barrier(total.astype(BF), held_p, teach)
     sums = lax.all_to_all(total.reshape(groups, rows, count), ZX, 0, 0)
     summed = jnp.sum(sums.astype(F32), axis=0)
-    student = unpair_block(summed.astype(BF), c)
     errors = ((summed - teach) * factor).astype(BF)
 
     xs = lax.dynamic_slice_in_dim(x_mine, (1 - d) * half, half, 0)
@@ -150,7 +149,8 @@
     xp_mine = swap(xs, "dp")
     e_part = gather_zx(errors)
     xo = [lax.dynamic_slice_in_dim(t, d * half, half, 0) for t in (x_mine, x_other)]
-    e_part, student, *xo = barrier(e_part, student, *xo)
+    e_part, summed, *xo = barrier(e_part, summed.astype(BF), *xo)
+    student = unpair_block(summed, c)
     keep, give = d * (groups // 2), (1 - d) * (groups // 2)
     e_got = swap(lax.dynamic_slice_in_dim(e_part, give, groups // 2, 0), "dp")
     e_pieces = {0: e_part, **{k: shift(e_part, "y", k) for k in (2, 1, 3)}}
@@ -166,12 +166,12 @@
         piece = jnp.concatenate([piece, other], axis=1)
         kept[k] = lax.dynamic_slice_in_dim(piece.reshape(groups, rows, 2 * count), keep, groups // 2, 0)
         back = back + dot(down[(ny - k) % ny], piece, 1, 0)
-    narrow, e_got = barrier(back.astype(BF), e_got)
-    back_p = swap(narrow, "dp").astype(F32)
+    back_p = swap(back.astype(BF), "dp").astype(F32)
+    up_own, gate_own, e_got = barrier((back * silu).astype(BF), (back * slope).astype(BF), e_got)
     got_pieces = {0: e_got, **{k: shift(e_got, "y", k) for k in (2, 1, 3)}}
     hidden_p, silu_p, slope_p = held_p[0], held_p[1].astype(F32), held_p[2].astype(F32)
-    up_back = jnp.concatenate([(back * silu).astype(BF), (back_p * silu_p).astype(BF)], axis=1)
-    gate_back = jnp.concatenate([(back * slope).astype(BF), (back_p * slope_p).astype(BF)], axis=1)
+    up_back = jnp.concatenate([up_own, (back_p * silu_p).astype(BF)], axis=1)
+    gate_back = jnp.concatenate([gate_own, (back_p * slope_p).astype(BF)], axis=1)
 
     def assembled(pieces):
         whole = jnp.broadcast_to(pieces[0][:, None], (groups // 2, ny) + pieces[0].shape[1:])

time: 149 us -> 143 us (0.960)
  starting transfers between devices: 59.1 us -> 54.8 us
    ppermute x18, starting transfers between devices: 26.2 us -> 21.8 us  [swap(): return lax.ppermute(x, axis, [(0, 1), (1, 0)])]
    all_to_all x2, waiting for transfers between devices: 17.6 us -> 15.8 us  [gather_zx(): return lax.all_to_all(copies, ZX, 0, 0)]
    unnamed x52 -> x50, local copies, waits for them, and re-layouts: 4.25 us -> 3.64 us
  transfers between devices with their start and end apart: 33 -> 33, of which waited for: 10 -> 11; matrix products, arithmetic and copies ran while one was open for 16% -> 17% of each run, Pallas kernels for 4% -> 4%
where the time goes in v4:
time: 143 us; the launch traced here: 142 us
  starting transfers between devices  54.8 us (38%)
  waiting for transfers between devices  47.5 us (33%)
  matrix products  14.3 us (10%)
  local copies, waits for them, and re-layouts  12.7 us (9%)
  other arithmetic  6.36 us (4%)
  Pallas kernels  5.25 us (4%)
    ppermute x18, starting transfers between devices, swap(): return lax.ppermute(x, axis, [(0, 1), (1, 0)])  21.8 us
    ppermute x12, starting transfers between devices, shift(): return lax.ppermute(x, axis, [(i, (i + k) % n) for i in range(n)])  16.8 us
    ppermute x12, waiting for transfers between devices, shift(): return lax.ppermute(x, axis, [(i, (i + k) % n) for i in range(n)])  16.4 us
    all_to_all x2, waiting for transfers between devices, gather_zx(): return lax.all_to_all(copies, ZX, 0, 0)  15.8 us
    dot_general x19, matrix products, dot(): lax.dot_general(a, b, (((i,), (j,)), ((), ())), preferred_element_type=F32)  14.3 us
    all_to_all x2, starting transfers between devices, gather_zx(): return lax.all_to_all(copies, ZX, 0, 0)  12.6 us
    all_to_all x1, waiting for transfers between devices, shards(): sums = lax.all_to_all(total.reshape(groups, rows, count), ZX, 0, 0)  9.81 us
    ppermute x18, waiting for transfers between devices, swap(): return lax.ppermute(x, axis, [(0, 1), (1, 0)])  5.51 us
  transfers between devices with their start and end apart: 33, of which 11 were waited for; matrix products, arithmetic and copies ran while one was open for 17% of the time, Pallas kernels for 4%

profile of v4, /device:TPU:1, one launch (start us, length us, event | category | flops | bytes accessed | tf_op | source)
XLA Modules:
  0.0 142.3 jit_solution(17763706874650297145)
XLA Ops:
  1.5 3.2 %collective-permute-start = (bf16[36,128]{1,0:T(8,128)(2,1)S(1)}, bf16[36,128]{1,0:T(8,128)(2,1)S(1)}, u32[]{:S(2)}, u32[]{:S(2)}) collective-permute-start(bf16[36,128]{1,0:T(8,128)(2,1)S(1)} %broadcast_select_fusion.10), channel_id=1, source_target_pairs={{0,1},{1,0},{2,3},{3,2},{4,5},{5,4},{6,7},{7,6},{8,9},{9,8},{10,11... | collective-permute-start | bytes 27656 | tf_op jit(solution)/shard_map/ppermute | solution.py:18
  7.1 9.0 %all-to-all-start = ((bf16[16,72,128]{2,1,0:T(8,128)(2,1)}), bf16[16,72,128]{2,1,0:T(8,128)(2,1)S(1)}, u32[]{:S(2)}, u32[]{:S(2)}) async-start(bf16[16,72,128]{2,1,0:T(8,128)(2,1)} %broadcast_in_dim.24), calls=%async_computation | async-start | bytes 589824 | tf_op jit(solution)/shard_map/all_to_all | solution.py:50
  16.1 5.3 %regroup.1 = bf16[4,288,1152]{2,1,0:T(8,128)(2,1)} custom-call(s32[1]{0:T(128)} %bitcast.1.y_ref, bf16[288,4608]{1,0:T(8,128)(2,1)} %w_ref), custom_call_target="tpu_custom_call" | custom-call | bytes 5308416 | tf_op jit(solution)/shard_map/regroup/pallas_call | solution.py:89
  21.4 7.9 %all-to-all-done = bf16[16,72,128]{2,1,0:T(8,128)(2,1)S(1)} async-done(((bf16[16,72,128]{2,1,0:T(8,128)(2,1)}), bf16[16,72,128]{2,1,0:T(8,128)(2,1)S(1)}, u32[]{:S(2)}, u32[]{:S(2)}) %all-to-all-start) | async-done | bytes 294944 | tf_op jit(solution)/shard_map/all_to_all | solution.py:50
  29.3 1.3 collective-permute-start.1
  30.6 1.4 %collective-permute-start.2 = (bf16[16,1,72,128]{3,2,1,0:T(8,128)(2,1)S(1)}, bf16[16,1,72,128]{3,2,1,0:T(8,128)(2,1)S(1)}, u32[]{:S(2)}, u32[]{:S(2)}) collective-permute-start(bf16[16,1,72,128]{3,2,1,0:T(8,128)(2,1)S(1)} %bitcast.122), channel_id=1, source_target_pairs={{0,6},{2,0},{4,2},{6,4},{1,7},{3,1},{5,3},{7,5},{8,14},{10,8},{12,... | collective-permute-start | bytes 884744 | tf_op jit(solution)/shard_map/ppermute | solution.py:23
  32.0 1.6 %collective-permute-start.3 = (bf16[16,1,72,128]{3,2,1,0:T(8,128)(2,1)S(1)}, bf16[16,1,72,128]{3,2,1,0:T(8,128)(2,1)S(1)}, u32[]{:S(2)}, u32[]{:S(2)}) collective-permute-start(bf16[16,1,72,128]{3,2,1,0:T(8,128)(2,1)S(1)} %bitcast.123), channel_id=1, source_target_pairs={{0,4},{2,6},{4,0},{6,2},{1,5},{3,7},{5,1},{7,3},{8,12},{10,14},{12... | collective-permute-start | bytes 884744 | tf_op jit(solution)/shard_map/ppermute | solution.py:23
  33.7 1.3 broadcast_select_fusion.6
  35.0 2.7 %collective-permute-start.13 = (bf16[36,128]{1,0:T(8,128)(2,1)}, bf16[36,128]{1,0:T(8,128)(2,1)S(1)}, u32[]{:S(2)}, u32[]{:S(2)}) collective-permute-start(bf16[36,128]{1,0:T(8,128)(2,1)} %broadcast_select_fusion.6), channel_id=1, source_target_pairs={{0,1},{1,0},{2,3},{3,2},{4,5},{5,4},{6,7},{7,6},{8,9},{9,8},{10,11... | collective-permute-start | bytes 27656 | tf_op jit(solution)/shard_map/ppermute | solution.py:18
  39.1 5.5 %collective-permute-done.3 = bf16[16,1,72,128]{3,2,1,0:T(8,128)(2,1)S(1)} collective-permute-done((bf16[16,1,72,128]{3,2,1,0:T(8,128)(2,1)S(1)}, bf16[16,1,72,128]{3,2,1,0:T(8,128)(2,1)S(1)}, u32[]{:S(2)}, u32[]{:S(2)}) %collective-permute-start.3) | collective-permute-done | bytes 294944 | tf_op jit(solution)/shard_map/ppermute | solution.py:23
  44.7 2.9 %collective-permute-start.4 = (bf16[4608,128]{1,0:T(8,128)(2,1)S(1)}, bf16[4608,128]{1,0:T(8,128)(2,1)S(1)}, u32[]{:S(2)}, u32[]{:S(2)}) collective-permute-start(bf16[4608,128]{1,0:T(8,128)(2,1)S(1)} %bitcast.113), channel_id=1, source_target_pairs={{0,1},{1,0},{2,3},{3,2},{4,5},{5,4},{6,7},{7,6},{8,9},{9,8},{10,11... | collective-permute-start | bytes 3538952 | tf_op jit(solution)/shard_map/ppermute | solution.py:18
  56.3 1.9 %collective-permute-start.7 = (bf16[1152,128]{1,0:T(8,128)(2,1)S(1)}, bf16[1152,128]{1,0:T(8,128)(2,1)S(1)}, u32[]{:S(2)}, u32[]{:S(2)}) collective-permute-start(bf16[1152,128]{1,0:T(8,128)(2,1)S(1)} %add_convert_fusion.3), channel_id=1, source_target_pairs={{0,4},{2,6},{4,0},{6,2},{1,5},{3,7},{5,1},{7,3},{8,12},{10,14},{12... | collective-permute-start | bytes 884744 | tf_op jit(solution)/shard_map/ppermute | solution.py:23
  59.5 2.4 %collective-permute-start.11 = (bf16[1152,128]{1,0:T(8,128)(2,1)S(1)}, bf16[1152,128]{1,0:T(8,128)(2,1)S(1)}, u32[]{:S(2)}, u32[]{:S(2)}) collective-permute-start(bf16[1152,128]{1,0:T(8,128)(2,1)S(1)} %add_convert_fusion.1), channel_id=1, source_target_pairs={{0,6},{2,0},{4,2},{6,4},{1,7},{3,1},{5,3},{7,5},{8,14},{10,8},{12,... | collective-permute-start | bytes 884744 | tf_op jit(solution)/shard_map/ppermute | solution.py:23
  62.5 3.7 %collective-permute-done.7 = bf16[1152,128]{1,0:T(8,128)(2,1)S(1)} collective-permute-done((bf16[1152,128]{1,0:T(8,128)(2,1)S(1)}, bf16[1152,128]{1,0:T(8,128)(2,1)S(1)}, u32[]{:S(2)}, u32[]{:S(2)}) %collective-permute-start.7) | collective-permute-done | bytes 294944 | tf_op jit(solution)/shard_map/ppermute | solution.py:23
  66.2 6.9 %collective-permute-done.9 = bf16[1152,128]{1,0:T(8,128)(2,1)S(1)} collective-permute-done((bf16[1152,128]{1,0:T(8,128)(2,1)S(1)}, bf16[1152,128]{1,0:T(8,128)(2,1)S(1)}, u32[]{:S(2)}, u32[]{:S(2)}) %collective-permute-start.9) | collective-permute-done | bytes 294944 | tf_op jit(solution)/shard_map/ppermute | solution.py:23
  74.0 3.6 %all-to-all-start.1 = ((bf16[16,72,128]{2,1,0:T(8,128)(2,1)}), bf16[16,72,128]{2,1,0:T(8,128)(2,1)S(1)}, u32[]{:S(2)}, u32[]{:S(2)}) async-start(bf16[16,72,128]{2,1,0:T(8,128)(2,1)} %bitcast.16), calls=%async_computation.1 | async-start | bytes 589824 | tf_op jit(solution)/shard_map/all_to_all | solution.py:143
  77.6 1.9 %constant_dynamic-slice_fusion.3 = bf16[2304,128]{1,0:T(8,128)(2,1)} fusion(bf16[4608,128]{1,0:T(8,128)(2,1)} %bitcast.116, s32[]{:T(128)S(6)} %select_n.95), kind=kLoop, calls=%fused_computation.138 | loop fusion | bytes 1179652 | tf_op jit(solution)/shard_map/dynamic_slice | solution.py:147
  80.2 9.8 %all-to-all-done.1 = bf16[16,72,128]{2,1,0:T(8,128)(2,1)S(1)} async-done(((bf16[16,72,128]{2,1,0:T(8,128)(2,1)}), bf16[16,72,128]{2,1,0:T(8,128)(2,1)S(1)}, u32[]{:S(2)}, u32[]{:S(2)}) %all-to-all-start.1) | async-done | bytes 294944 | tf_op jit(solution)/shard_map/all_to_all | solution.py:143
  91.5 3.5 %all-to-all-start.2 = ((bf16[16,72,128]{2,1,0:T(8,128)(2,1)}), bf16[16,72,128]{2,1,0:T(8,128)(2,1)S(1)}, u32[]{:S(2)}, u32[]{:S(2)}) async-start(bf16[16,72,128]{2,1,0:T(8,128)(2,1)} %broadcast_in_dim.53), calls=%async_computation.2 | async-start | bytes 589824 | tf_op jit(solution)/shard_map/all_to_all | solution.py:50
  96.5 1.9 %constant_dynamic-slice_fusion.2 = bf16[2304,128]{1,0:T(8,128)(2,1)} fusion(bf16[4608,128]{1,0:T(8,128)(2,1)} %bitcast.117, s32[]{:T(128)S(6)} %select_n.96), kind=kLoop, calls=%fused_computation.137 | loop fusion | bytes 1179652 | tf_op jit(solution)/shard_map/dynamic_slice | solution.py:151
  98.5 7.9 %all-to-all-done.2 = bf16[16,72,128]{2,1,0:T(8,128)(2,1)S(1)} async-done(((bf16[16,72,128]{2,1,0:T(8,128)(2,1)}), bf16[16,72,128]{2,1,0:T(8,128)(2,1)S(1)}, u32[]{:S(2)}, u32[]{:S(2)}) %all-to-all-start.2) | async-done | bytes 294944 | tf_op jit(solution)/shard_map/all_to_all | solution.py:50
  106.4 1.8 %collective-permute-start.21 = (bf16[16,72,128]{2,1,0:T(8,128)(2,1)S(1)}, bf16[16,72,128]{2,1,0:T(8,128)(2,1)S(1)}, u32[]{:S(2)}, u32[]{:S(2)}) collective-permute-start(bf16[16,72,128]{2,1,0:T(8,128)(2,1)S(1)} %all-to-all-done.2), channel_id=1, source_target_pairs={{0,2},{2,4},{4,6},{6,0},{1,3},{3,5},{5,7},{7,1},{8,10},{10,12},{12... | collective-permute-start | bytes 884744 | tf_op jit(solution)/shard_map/ppermute | solution.py:23
  109.0 1.6 %collective-permute-start.17 = (bf16[16,72,128]{2,1,0:T(8,128)(2,1)S(1)}, bf16[16,72,128]{2,1,0:T(8,128)(2,1)S(1)}, u32[]{:S(2)}, u32[]{:S(2)}) collective-permute-start(bf16[16,72,128]{2,1,0:T(8,128)(2,1)S(1)} %all-to-all-done.2), channel_id=1, source_target_pairs={{0,4},{2,6},{4,0},{6,2},{1,5},{3,7},{5,1},{7,3},{8,12},{10,14},{12... | collective-permute-start | bytes 884744 | tf_op jit(solution)/shard_map/ppermute | solution.py:23
  112.6 4.6 %collective-permute-start.14 = (bf16[36,128]{1,0:T(8,128)(2,1)S(1)}, bf16[36,128]{1,0:T(8,128)(2,1)S(1)}, u32[]{:S(2)}, u32[]{:S(2)}) collective-permute-start(bf16[36,128]{1,0:T(8,128)(2,1)S(1)} %broadcast_select_fusion.2), channel_id=1, source_target_pairs={{0,1},{1,0},{2,3},{3,2},{4,5},{5,4},{6,7},{7,6},{8,9},{9,8},{10,11... | collective-permute-start | bytes 27656 | tf_op jit(solution)/shard_map/ppermute | solution.py:18
  119.3 1.2 constant_dynamic-update-slice_fusion.1
  122.0 2.3 %collective-permute-start.18 = (bf16[1152,128]{1,0:T(8,128)(2,1)S(1)}, bf16[1152,128]{1,0:T(8,128)(2,1)S(1)}, u32[]{:S(2)}, u32[]{:S(2)}) collective-permute-start(bf16[1152,128]{1,0:T(8,128)(2,1)S(1)} %bitcast.130), channel_id=1, source_target_pairs={{0,1},{1,0},{2,3},{3,2},{4,5},{5,4},{6,7},{7,6},{8,9},{9,8},{10,11... | collective-permute-start | bytes 884744 | tf_op jit(solution)/shard_map/ppermute | solution.py:18
  127.0 2.3 %collective-permute-start.27 = (bf16[8,72,128]{2,1,0:T(8,128)(2,1)S(1)}, bf16[8,72,128]{2,1,0:T(8,128)(2,1)S(1)}, u32[]{:S(2)}, u32[]{:S(2)}) collective-permute-start(bf16[8,72,128]{2,1,0:T(8,128)(2,1)S(1)} %collective-permute-done.24), channel_id=1, source_target_pairs={{0,4},{2,6},{4,0},{6,2},{1,5},{3,7},{5,1},{7,3},{8,12},{10,14},{12... | collective-permute-start | bytes 442376 | tf_op jit(solution)/shard_map/ppermute | solution.py:23
  130.0 3.9 %collective-permute-done.25 = bf16[288,256]{1,0:T(8,128)(2,1)S(1)} collective-permute-done((bf16[288,256]{1,0:T(8,128)(2,1)S(1)}, bf16[288,256]{1,0:T(8,128)(2,1)S(1)}, u32[]{:S(2)}, u32[]{:S(2)}) %collective-permute-start.25) | collective-permute-done | bytes 147488 | tf_op jit(solution)/shard_map/ppermute | solution.py:18
  133.9 1.9 %fusion.61 = bf16[2304,288]{0,1:T(8,128)(2,1)} fusion(bf16[2304,512]{1,0:T(8,128)(2,1)S(1)} %constant_dynamic-update-slice_fusion, bf16[288,256]{1,0:T(8,128)(2,1)S(1)} %get-tuple-element.69, bf16[288,256]{1,0:T(8,128)(2,1)S(1)} %get-tuple-element.60), kind=kOutput, calls=%fused_computation.79 | convolution fusion | flops 680067072 | bytes 3981312 | tf_op jit(solution)/shard_map/dot_general | solution.py:65
  136.2 1.8 %collective-permute-start.29 = (bf16[2304,128]{1,0:T(8,128)(2,1)S(1)}, bf16[2304,128]{1,0:T(8,128)(2,1)S(1)}, u32[]{:S(2)}, u32[]{:S(2)}) collective-permute-start(bf16[2304,128]{1,0:T(8,128)(2,1)S(1)} %bitcast.125), channel_id=1, source_target_pairs={{0,1},{1,0},{2,3},{3,2},{4,5},{5,4},{6,7},{7,6},{8,9},{9,8},{10,11... | collective-permute-start | bytes 1769480 | tf_op jit(solution)/shard_map/ppermute | solution.py:18
  138.3 1.9 %convolution_convert_fusion.1 = bf16[2304,288]{0,1:T(8,128)(2,1)} fusion(bf16[2304,512]{1,0:T(8,128)(2,1)S(1)} %constant_dynamic-update-slice_fusion, bf16[288,256]{1,0:T(8,128)(2,1)S(1)} %get-tuple-element.68, bf16[288,256]{1,0:T(8,128)(2,1)S(1)} %get-tuple-element.64), kind=kOutput, calls=%fused_computation.1 | convolution fusion | flops 680730624 | bytes 3981312 | tf_op jit(solution)/shard_map/dot_general | solution.py:65
  140.3 2.0 %convolution_convert_fusion = bf16[288,2304]{1,0:T(8,128)(2,1)} fusion(bf16[2304,128]{1,0:T(8,128)(2,1)S(1)} %collective-permute-done.29, bf16[2304,128]{1,0:T(8,128)(2,1)S(1)} %bitcast.126, bf16[2304,256]{1,0:T(8,128)(2,1)S(1)} %bitcast.120, bf16[288,256]{1,0:T(8,128)(2,1)S(1)} %copy-done.19, bf16[288,128]{1,0:T(8,128)(2,1)S(1)} %copy-done.22, ...), kind=kOutput, calls=%fused_computation | convolution fusion | flops 688103424 | bytes 3981312 | tf_op jit(solution)/shard_map/dot_general | solution.py:65
  (145 shorter events, 29.6 us)
Async XLA Ops:
  1.5 4.1 %collective-permute-start = (bf16[36,128]{1,0:T(8,128)(2,1)S(1)}, bf16[36,128]{1,0:T(8,128)(2,1)S(1)}, u32[]{:S(2)}, u32[]{:S(2)}) collective-permute-start(bf16[36,128]{1,0:T(8,128)(2,1)S(1)} %broadcast_select_fusion.10), channel_id=1, source_target_pairs={{0,1},{1,0},{2,3},{3,2},{4,5},{5,4},{6,7},{7,6},{8,9},{9,8},{10,11... | collective-permute-start | bytes 27656 | tf_op jit(solution)/shard_map/ppermute | solution.py:18
  7.1 22.2 %all-to-all-start = ((bf16[16,72,128]{2,1,0:T(8,128)(2,1)}), bf16[16,72,128]{2,1,0:T(8,128)(2,1)S(1)}, u32[]{:S(2)}, u32[]{:S(2)}) async-start(bf16[16,72,128]{2,1,0:T(8,128)(2,1)} %broadcast_in_dim.24), calls=%async_computation | async-start | bytes 589824 | tf_op jit(solution)/shard_map/all_to_all | solution.py:50
  29.3 8.4 %collective-permute-start.1 = (bf16[16,1,72,128]{3,2,1,0:T(8,128)(2,1)S(1)}, bf16[16,1,72,128]{3,2,1,0:T(8,128)(2,1)}, u32[]{:S(2)}, u32[]{:S(2)}) collective-permute-start(bf16[16,1,72,128]{3,2,1,0:T(8,128)(2,1)S(1)} %bitcast.121), channel_id=1, source_target_pairs={{0,2},{2,4},{4,6},{6,0},{1,3},{3,5},{5,7},{7,1},{8,10},{10,12},{12... | collective-permute-start | bytes 884744 | tf_op jit(solution)/shard_map/ppermute | solution.py:23
  30.6 8.5 %collective-permute-start.2 = (bf16[16,1,72,128]{3,2,1,0:T(8,128)(2,1)S(1)}, bf16[16,1,72,128]{3,2,1,0:T(8,128)(2,1)S(1)}, u32[]{:S(2)}, u32[]{:S(2)}) collective-permute-start(bf16[16,1,72,128]{3,2,1,0:T(8,128)(2,1)S(1)} %bitcast.122), channel_id=1, source_target_pairs={{0,6},{2,0},{4,2},{6,4},{1,7},{3,1},{5,3},{7,5},{8,14},{10,8},{12,... | collective-permute-start | bytes 884744 | tf_op jit(solution)/shard_map/ppermute | solution.py:23
  32.0 12.6 %collective-permute-start.3 = (bf16[16,1,72,128]{3,2,1,0:T(8,128)(2,1)S(1)}, bf16[16,1,72,128]{3,2,1,0:T(8,128)(2,1)S(1)}, u32[]{:S(2)}, u32[]{:S(2)}) collective-permute-start(bf16[16,1,72,128]{3,2,1,0:T(8,128)(2,1)S(1)} %bitcast.123), channel_id=1, source_target_pairs={{0,4},{2,6},{4,0},{6,2},{1,5},{3,7},{5,1},{7,3},{8,12},{10,14},{12... | collective-permute-start | bytes 884744 | tf_op jit(solution)/shard_map/ppermute | solution.py:23
  35.0 12.6 %collective-permute-start.13 = (bf16[36,128]{1,0:T(8,128)(2,1)}, bf16[36,128]{1,0:T(8,128)(2,1)S(1)}, u32[]{:S(2)}, u32[]{:S(2)}) collective-permute-start(bf16[36,128]{1,0:T(8,128)(2,1)} %broadcast_select_fusion.6), channel_id=1, source_target_pairs={{0,1},{1,0},{2,3},{3,2},{4,5},{5,4},{6,7},{7,6},{8,9},{9,8},{10,11... | collective-permute-start | bytes 27656 | tf_op jit(solution)/shard_map/ppermute | solution.py:18
  44.7 6.0 %collective-permute-start.4 = (bf16[4608,128]{1,0:T(8,128)(2,1)S(1)}, bf16[4608,128]{1,0:T(8,128)(2,1)S(1)}, u32[]{:S(2)}, u32[]{:S(2)}) collective-permute-start(bf16[4608,128]{1,0:T(8,128)(2,1)S(1)} %bitcast.113), channel_id=1, source_target_pairs={{0,1},{1,0},{2,3},{3,2},{4,5},{5,4},{6,7},{7,6},{8,9},{9,8},{10,11... | collective-permute-start | bytes 3538952 | tf_op jit(solution)/shard_map/ppermute | solution.py:18
  54.2 4.0 %collective-permute-start.8 = (bf16[1152,128]{1,0:T(8,128)(2,1)S(1)}, bf16[1152,128]{1,0:T(8,128)(2,1)S(1)}, u32[]{:S(2)}, u32[]{:S(2)}) collective-permute-start(bf16[1152,128]{1,0:T(8,128)(2,1)S(1)} %convolution_convert_fusion.3), channel_id=1, source_target_pairs={{0,1},{1,0},{2,3},{3,2},{4,5},{5,4},{6,7},{7,6},{8,9},{9,8},{10,11... | collective-permute-start | bytes 884744 | tf_op jit(solution)/shard_map/ppermute | solution.py:18
  55.2 7.3 %collective-permute-start.5 = (bf16[1152,128]{1,0:T(8,128)(2,1)S(1)}, bf16[1152,128]{1,0:T(8,128)(2,1)S(1)}, u32[]{:S(2)}, u32[]{:S(2)}) collective-permute-start(bf16[1152,128]{1,0:T(8,128)(2,1)S(1)} %convolution_convert_fusion.5), channel_id=1, source_target_pairs={{0,1},{1,0},{2,3},{3,2},{4,5},{5,4},{6,7},{7,6},{8,9},{9,8},{10,11... | collective-permute-start | bytes 884744 | tf_op jit(solution)/shard_map/ppermute | solution.py:18
  55.3 3.7 %collective-permute-start.10 = (bf16[1152,128]{1,0:T(8,128)(2,1)S(1)}, bf16[1152,128]{1,0:T(8,128)(2,1)S(1)}, u32[]{:S(2)}, u32[]{:S(2)}) collective-permute-start(bf16[1152,128]{1,0:T(8,128)(2,1)S(1)} %convolution_convert_fusion.2), channel_id=1, source_target_pairs={{0,1},{1,0},{2,3},{3,2},{4,5},{5,4},{6,7},{7,6},{8,9},{9,8},{10,11... | collective-permute-start | bytes 884744 | tf_op jit(solution)/shard_map/ppermute | solution.py:18
  56.3 10.0 %collective-permute-start.7 = (bf16[1152,128]{1,0:T(8,128)(2,1)S(1)}, bf16[1152,128]{1,0:T(8,128)(2,1)S(1)}, u32[]{:S(2)}, u32[]{:S(2)}) collective-permute-start(bf16[1152,128]{1,0:T(8,128)(2,1)S(1)} %add_convert_fusion.3), channel_id=1, source_target_pairs={{0,4},{2,6},{4,0},{6,2},{1,5},{3,7},{5,1},{7,3},{8,12},{10,14},{12... | collective-permute-start | bytes 884744 | tf_op jit(solution)/shard_map/ppermute | solution.py:23
  58.6 14.5 %collective-permute-start.9 = (bf16[1152,128]{1,0:T(8,128)(2,1)S(1)}, bf16[1152,128]{1,0:T(8,128)(2,1)S(1)}, u32[]{:S(2)}, u32[]{:S(2)}) collective-permute-start(bf16[1152,128]{1,0:T(8,128)(2,1)S(1)} %add_convert_fusion.2), channel_id=1, source_target_pairs={{0,2},{2,4},{4,6},{6,0},{1,3},{3,5},{5,7},{7,1},{8,10},{10,12},{12... | collective-permute-start | bytes 884744 | tf_op jit(solution)/shard_map/ppermute | solution.py:23
  59.5 13.6 %collective-permute-start.11 = (bf16[1152,128]{1,0:T(8,128)(2,1)S(1)}, bf16[1152,128]{1,0:T(8,128)(2,1)S(1)}, u32[]{:S(2)}, u32[]{:S(2)}) collective-permute-start(bf16[1152,128]{1,0:T(8,128)(2,1)S(1)} %add_convert_fusion.1), channel_id=1, source_target_pairs={{0,6},{2,0},{4,2},{6,4},{1,7},{3,1},{5,3},{7,5},{8,14},{10,8},{12,... | collective-permute-start | bytes 884744 | tf_op jit(solution)/shard_map/ppermute | solution.py:23
  62.1 11.9 %collective-permute-start.12 = (bf16[3,288,256]{2,1,0:T(8,128)(2,1)S(1)}, bf16[3,288,256]{2,1,0:T(8,128)(2,1)S(1)}, u32[]{:S(2)}, u32[]{:S(2)}) collective-permute-start(bf16[3,288,256]{2,1,0:T(8,128)(2,1)S(1)} %pad_maximum_fusion), channel_id=1, source_target_pairs={{0,128},{128,0},{1,129},{129,1},{2,130},{130,2},{3,131},{131,3},{4... | collective-permute-start | bytes 1327112 | tf_op jit(solution)/shard_map/ppermute | solution.py:18
  74.0 16.0 %all-to-all-start.1 = ((bf16[16,72,128]{2,1,0:T(8,128)(2,1)}), bf16[16,72,128]{2,1,0:T(8,128)(2,1)S(1)}, u32[]{:S(2)}, u32[]{:S(2)}) async-start(bf16[16,72,128]{2,1,0:T(8,128)(2,1)} %bitcast.16), calls=%async_computation.1 | async-start | bytes 589824 | tf_op jit(solution)/shard_map/all_to_all | solution.py:143
  91.5 14.9 %all-to-all-start.2 = ((bf16[16,72,128]{2,1,0:T(8,128)(2,1)}), bf16[16,72,128]{2,1,0:T(8,128)(2,1)S(1)}, u32[]{:S(2)}, u32[]{:S(2)}) async-start(bf16[16,72,128]{2,1,0:T(8,128)(2,1)} %broadcast_in_dim.53), calls=%async_computation.2 | async-start | bytes 589824 | tf_op jit(solution)/shard_map/all_to_all | solution.py:50
  95.0 24.0 %collective-permute-start.15 = (bf16[2304,128]{1,0:T(8,128)(2,1)}, bf16[2304,128]{1,0:T(8,128)(2,1)}, u32[]{:S(2)}, u32[]{:S(2)}) collective-permute-start(bf16[2304,128]{1,0:T(8,128)(2,1)} %constant_dynamic-slice_fusion.3), channel_id=1, source_target_pairs={{0,128},{128,0},{1,129},{129,1},{2,130},{130,2},{3,131},{131,3},{4... | collective-permute-start | bytes 1769480 | tf_op jit(solution)/shard_map/ppermute | solution.py:18
  106.4 15.1 %collective-permute-start.21 = (bf16[16,72,128]{2,1,0:T(8,128)(2,1)S(1)}, bf16[16,72,128]{2,1,0:T(8,128)(2,1)S(1)}, u32[]{:S(2)}, u32[]{:S(2)}) collective-permute-start(bf16[16,72,128]{2,1,0:T(8,128)(2,1)S(1)} %all-to-all-done.2), channel_id=1, source_target_pairs={{0,2},{2,4},{4,6},{6,0},{1,3},{3,5},{5,7},{7,1},{8,10},{10,12},{12... | collective-permute-start | bytes 884744 | tf_op jit(solution)/shard_map/ppermute | solution.py:23
  108.2 13.4 %collective-permute-start.19 = (bf16[16,72,128]{2,1,0:T(8,128)(2,1)S(1)}, bf16[16,72,128]{2,1,0:T(8,128)(2,1)S(1)}, u32[]{:S(2)}, u32[]{:S(2)}) collective-permute-start(bf16[16,72,128]{2,1,0:T(8,128)(2,1)S(1)} %all-to-all-done.2), channel_id=1, source_target_pairs={{0,6},{2,0},{4,2},{6,4},{1,7},{3,1},{5,3},{7,5},{8,14},{10,8},{12,... | collective-permute-start | bytes 884744 | tf_op jit(solution)/shard_map/ppermute | solution.py:23
  109.0 13.0 %collective-permute-start.17 = (bf16[16,72,128]{2,1,0:T(8,128)(2,1)S(1)}, bf16[16,72,128]{2,1,0:T(8,128)(2,1)S(1)}, u32[]{:S(2)}, u32[]{:S(2)}) collective-permute-start(bf16[16,72,128]{2,1,0:T(8,128)(2,1)S(1)} %all-to-all-done.2), channel_id=1, source_target_pairs={{0,4},{2,6},{4,0},{6,2},{1,5},{3,7},{5,1},{7,3},{8,12},{10,14},{12... | collective-permute-start | bytes 884744 | tf_op jit(solution)/shard_map/ppermute | solution.py:23
  112.6 5.4 %collective-permute-start.14 = (bf16[36,128]{1,0:T(8,128)(2,1)S(1)}, bf16[36,128]{1,0:T(8,128)(2,1)S(1)}, u32[]{:S(2)}, u32[]{:S(2)}) collective-permute-start(bf16[36,128]{1,0:T(8,128)(2,1)S(1)} %broadcast_select_fusion.2), channel_id=1, source_target_pairs={{0,1},{1,0},{2,3},{3,2},{4,5},{5,4},{6,7},{7,6},{8,9},{9,8},{10,11... | collective-permute-start | bytes 27656 | tf_op jit(solution)/shard_map/ppermute | solution.py:18
  118.0 2.5 %collective-permute-start.22 = (bf16[1152,128]{1,0:T(8,128)(2,1)S(1)}, bf16[1152,128]{1,0:T(8,128)(2,1)S(1)}, u32[]{:S(2)}, u32[]{:S(2)}) collective-permute-start(bf16[1152,128]{1,0:T(8,128)(2,1)S(1)} %bitcast.118), channel_id=1, source_target_pairs={{0,1},{1,0},{2,3},{3,2},{4,5},{5,4},{6,7},{7,6},{8,9},{9,8},{10,11... | collective-permute-start | bytes 884744 | tf_op jit(solution)/shard_map/ppermute | solution.py:18
  119.0 7.1 %collective-permute-start.24 = (bf16[8,72,128]{2,1,0:T(8,128)(2,1)S(1)}, bf16[8,72,128]{2,1,0:T(8,128)(2,1)S(1)}, u32[]{:S(2)}, u32[]{:S(2)}) collective-permute-start(bf16[8,72,128]{2,1,0:T(8,128)(2,1)S(1)} %constant_dynamic-slice_fusion), channel_id=1, source_target_pairs={{0,128},{128,0},{1,129},{129,1},{2,130},{130,2},{3,131},{131,3},{4... | collective-permute-start | bytes 442376 | tf_op jit(solution)/shard_map/ppermute | solution.py:18
  120.5 9.3 %collective-permute-start.16 = (bf16[2304,128]{1,0:T(8,128)(2,1)}, bf16[2304,128]{1,0:T(8,128)(2,1)S(1)}, u32[]{:S(2)}, u32[]{:S(2)}) collective-permute-start(bf16[2304,128]{1,0:T(8,128)(2,1)} %collective-permute-done.15), channel_id=1, source_target_pairs={{0,1},{1,0},{2,3},{3,2},{4,5},{5,4},{6,7},{7,6},{8,9},{9,8},{10,11... | collective-permute-start | bytes 1769480 | tf_op jit(solution)/shard_map/ppermute | solution.py:18
  121.4 3.0 %collective-permute-start.23 = (bf16[1152,128]{1,0:T(8,128)(2,1)S(1)}, bf16[1152,128]{1,0:T(8,128)(2,1)S(1)}, u32[]{:S(2)}, u32[]{:S(2)}) collective-permute-start(bf16[1152,128]{1,0:T(8,128)(2,1)S(1)} %bitcast.128), channel_id=1, source_target_pairs={{0,1},{1,0},{2,3},{3,2},{4,5},{5,4},{6,7},{7,6},{8,9},{9,8},{10,11... | collective-permute-start | bytes 884744 | tf_op jit(solution)/shard_map/ppermute | solution.py:18
  121.6 3.4 %collective-permute-start.20 = (bf16[1152,128]{1,0:T(8,128)(2,1)S(1)}, bf16[1152,128]{1,0:T(8,128)(2,1)S(1)}, u32[]{:S(2)}, u32[]{:S(2)}) collective-permute-start(bf16[1152,128]{1,0:T(8,128)(2,1)S(1)} %bitcast.132), channel_id=1, source_target_pairs={{0,1},{1,0},{2,3},{3,2},{4,5},{5,4},{6,7},{7,6},{8,9},{9,8},{10,11... | collective-permute-start | bytes 884744 | tf_op jit(solution)/shard_map/ppermute | solution.py:18
  122.0 3.5 %collective-permute-start.18 = (bf16[1152,128]{1,0:T(8,128)(2,1)S(1)}, bf16[1152,128]{1,0:T(8,128)(2,1)S(1)}, u32[]{:S(2)}, u32[]{:S(2)}) collective-permute-start(bf16[1152,128]{1,0:T(8,128)(2,1)S(1)} %bitcast.130), channel_id=1, source_target_pairs={{0,1},{1,0},{2,3},{3,2},{4,5},{5,4},{6,7},{7,6},{8,9},{9,8},{10,11... | collective-permute-start | bytes 884744 | tf_op jit(solution)/shard_map/ppermute | solution.py:18
  126.1 9.8 %collective-permute-start.26 = (bf16[8,72,128]{2,1,0:T(8,128)(2,1)S(1)}, bf16[8,72,128]{2,1,0:T(8,128)(2,1)S(1)}, u32[]{:S(2)}, u32[]{:S(2)}) collective-permute-start(bf16[8,72,128]{2,1,0:T(8,128)(2,1)S(1)} %collective-permute-done.24), channel_id=1, source_target_pairs={{0,2},{2,4},{4,6},{6,0},{1,3},{3,5},{5,7},{7,1},{8,10},{10,12},{12... | collective-permute-start | bytes 442376 | tf_op jit(solution)/shard_map/ppermute | solution.py:23
  127.0 9.1 %collective-permute-start.27 = (bf16[8,72,128]{2,1,0:T(8,128)(2,1)S(1)}, bf16[8,72,128]{2,1,0:T(8,128)(2,1)S(1)}, u32[]{:S(2)}, u32[]{:S(2)}) collective-permute-start(bf16[8,72,128]{2,1,0:T(8,128)(2,1)S(1)} %collective-permute-done.24), channel_id=1, source_target_pairs={{0,4},{2,6},{4,0},{6,2},{1,5},{3,7},{5,1},{7,3},{8,12},{10,14},{12... | collective-permute-start | bytes 442376 | tf_op jit(solution)/shard_map/ppermute | solution.py:23
  129.3 6.8 %collective-permute-start.28 = (bf16[8,72,128]{2,1,0:T(8,128)(2,1)S(1)}, bf16[8,72,128]{2,1,0:T(8,128)(2,1)S(1)}, u32[]{:S(2)}, u32[]{:S(2)}) collective-permute-start(bf16[8,72,128]{2,1,0:T(8,128)(2,1)S(1)} %collective-permute-done.24), channel_id=1, source_target_pairs={{0,6},{2,0},{4,2},{6,4},{1,7},{3,1},{5,3},{7,5},{8,14},{10,8},{12,... | collective-permute-start | bytes 442376 | tf_op jit(solution)/shard_map/ppermute | solution.py:23
  129.5 4.3 %collective-permute-start.25 = (bf16[288,256]{1,0:T(8,128)(2,1)S(1)}, bf16[288,256]{1,0:T(8,128)(2,1)S(1)}, u32[]{:S(2)}, u32[]{:S(2)}) collective-permute-start(bf16[288,256]{1,0:T(8,128)(2,1)S(1)} %get-tuple-element.71), channel_id=1, source_target_pairs={{0,128},{128,0},{1,129},{129,1},{2,130},{130,2},{3,131},{131,3},{4... | collective-permute-start | bytes 442376 | tf_op jit(solution)/shard_map/ppermute | solution.py:18
  136.2 4.0 %collective-permute-start.29 = (bf16[2304,128]{1,0:T(8,128)(2,1)S(1)}, bf16[2304,128]{1,0:T(8,128)(2,1)S(1)}, u32[]{:S(2)}, u32[]{:S(2)}) collective-permute-start(bf16[2304,128]{1,0:T(8,128)(2,1)S(1)} %bitcast.125), channel_id=1, source_target_pairs={{0,1},{1,0},{2,3},{3,2},{4,5},{5,4},{6,7},{7,6},{8,9},{9,8},{10,11... | collective-permute-start | bytes 1769480 | tf_op jit(solution)/shard_map/ppermute | solution.py:18
  (24 other events, 207.9 us)

commit v5 on v4

--- a/solution.py
+++ b/solution.py
@@ -170,8 +170,7 @@
     up_own, gate_own, e_got = barrier((back * silu).astype(BF), (back * slope).astype(BF), e_got)
     got_pieces = {0: e_got, **{k: shift(e_got, "y", k) for k in (2, 1, 3)}}
     hidden_p, silu_p, slope_p = held_p[0], held_p[1].astype(F32), held_p[2].astype(F32)
-    up_back = jnp.concatenate([up_own, (back_p * silu_p).astype(BF)], axis=1)
-    gate_back = jnp.concatenate([gate_own, (back_p * slope_p).astype(BF)], axis=1)
+    up_back_p, gate_back_p = (back_p * silu_p).astype(BF), (back_p * slope_p).astype(BF)
 
     def assembled(pieces):
         whole = jnp.broadcast_to(pieces[0][:, None], (groups // 2, ny) + pieces[0].shape[1:])
@@ -179,9 +178,10 @@
             whole = lax.dynamic_update_slice_in_dim(whole, pieces[k][:, None], lax.rem(y - k + ny, ny), 1)
         return whole.reshape(half, -1)
 
-    x_both = jnp.concatenate([*xo, xp_mine, swap(xp_mine, "c")], axis=1)
-    grad_gate = dot(x_both, gate_back, 1, 1)
-    grad_up = dot(x_both, up_back, 1, 1)
+    x_own = jnp.concatenate(xo, axis=1)
+    xp = jnp.concatenate([xp_mine, swap(xp_mine, "c")], axis=1)
+    grad_gate = dot(x_own, gate_own, 1, 1) + dot(xp, gate_back_p, 1, 1)
+    grad_up = dot(x_own, up_own, 1, 1) + dot(xp, up_back_p, 1, 1)
     grad_gate, *got_late = barrier(grad_gate, *(got_pieces[k] for k in (1, 2, 3)))
     eo, ep_mine = assembled(kept), assembled(dict(enumerate([got_pieces[0], *got_late])))
     errors_both = jnp.concatenate([eo, ep_mine, swap(ep_mine, "c")], axis=1)

time: 143 us -> 146 us (1.021)
  waiting for transfers between devices: 47.5 us -> 49.9 us
  starting transfers between devices: 54.8 us -> 56.7 us
  local copies, waits for them, and re-layouts: 12.7 us -> 10.8 us
    ppermute x12, waiting for transfers between devices: 16.4 us -> 18.8 us  [shift(): return lax.ppermute(x, axis, [(i, (i + k) % n) for i in range(n)])]
    ppermute x12, starting transfers between devices: 16.8 us -> 18.5 us  [shift(): return lax.ppermute(x, axis, [(i, (i + k) % n) for i in range(n)])]
    unnamed x50 -> x53, local copies, waits for them, and re-layouts: 3.64 us -> 2.87 us
    dot_general x19 -> x21, matrix products: 14.3 us -> 14.8 us  [dot(): lax.dot_general(a, b, (((i,), (j,)), ((), ())), preferred_element_type=F32)]
  transfers between devices with their start and end apart: 33 -> 33, of which waited for: 11 -> 11; matrix products, arithmetic and copies ran while one was open for 17% -> 15% of each run, Pallas kernels for 4% -> 4%
where the time goes in v5:
time: 146 us; the launch traced here: 145 us
  starting transfers between devices  56.7 us (39%)
  waiting for transfers between devices  49.9 us (34%)
  matrix products  14.8 us (10%)
  local copies, waits for them, and re-layouts  10.8 us (7%)
  other arithmetic  6.3 us (4%)
  Pallas kernels  5.25 us (4%)
    ppermute x18, starting transfers between devices, swap(): return lax.ppermute(x, axis, [(0, 1), (1, 0)])  21.7 us
    ppermute x12, waiting for transfers between devices, shift(): return lax.ppermute(x, axis, [(i, (i + k) % n) for i in range(n)])  18.8 us
    ppermute x12, starting transfers between devices, shift(): return lax.ppermute(x, axis, [(i, (i + k) % n) for i in range(n)])  18.5 us
    all_to_all x2, waiting for transfers between devices, gather_zx(): return lax.all_to_all(copies, ZX, 0, 0)  17 us
    dot_general x21, matrix products, dot(): lax.dot_general(a, b, (((i,), (j,)), ((), ())), preferred_element_type=F32)  14.8 us
    all_to_all x2, starting transfers between devices, gather_zx(): return lax.all_to_all(copies, ZX, 0, 0)  12.8 us
    all_to_all x1, waiting for transfers between devices, shards(): sums = lax.all_to_all(total.reshape(groups, rows, count), ZX, 0, 0)  8.9 us
    pallas_call x1, Pallas kernels, regroup(): pl.pallas_call(functools.partial(regroup_kernel, rows), grid_spec=pltpu.P...  5.25 us
  transfers between devices with their start and end apart: 33, of which 11 were waited for; matrix products, arithmetic and copies ran while one was open for 15% of the time, Pallas kernels for 4%

profile of v5, /device:TPU:1, one launch (start us, length us, event | category | flops | bytes accessed | tf_op | source)
XLA Modules:
  0.0 145.1 jit_solution(8781697966215463322)
XLA Ops:
  1.5 3.2 %collective-permute-start = (bf16[36,128]{1,0:T(8,128)(2,1)S(1)}, bf16[36,128]{1,0:T(8,128)(2,1)S(1)}, u32[]{:S(2)}, u32[]{:S(2)}) collective-permute-start(bf16[36,128]{1,0:T(8,128)(2,1)S(1)} %broadcast_select_fusion.10), channel_id=1, source_target_pairs={{0,1},{1,0},{2,3},{3,2},{4,5},{5,4},{6,7},{7,6},{8,9},{9,8},{10,11... | collective-permute-start | bytes 27656 | tf_op jit(solution)/shard_map/ppermute | solution.py:18
  7.1 9.0 %all-to-all-start = ((bf16[16,72,128]{2,1,0:T(8,128)(2,1)}), bf16[16,72,128]{2,1,0:T(8,128)(2,1)S(1)}, u32[]{:S(2)}, u32[]{:S(2)}) async-start(bf16[16,72,128]{2,1,0:T(8,128)(2,1)} %broadcast_in_dim.24), calls=%async_computation | async-start | bytes 589824 | tf_op jit(solution)/shard_map/all_to_all | solution.py:50
  16.1 5.2 %regroup.1 = bf16[4,288,1152]{2,1,0:T(8,128)(2,1)} custom-call(s32[1]{0:T(128)} %bitcast.1.y_ref, bf16[288,4608]{1,0:T(8,128)(2,1)} %w_ref), custom_call_target="tpu_custom_call" | custom-call | bytes 5308416 | tf_op jit(solution)/shard_map/regroup/pallas_call | solution.py:89
  21.4 7.9 %all-to-all-done = bf16[16,72,128]{2,1,0:T(8,128)(2,1)S(1)} async-done(((bf16[16,72,128]{2,1,0:T(8,128)(2,1)}), bf16[16,72,128]{2,1,0:T(8,128)(2,1)S(1)}, u32[]{:S(2)}, u32[]{:S(2)}) %all-to-all-start) | async-done | bytes 294944 | tf_op jit(solution)/shard_map/all_to_all | solution.py:50
  29.3 1.3 collective-permute-start.1
  30.6 2.6 %collective-permute-start.3 = (bf16[16,1,72,128]{3,2,1,0:T(8,128)(2,1)S(1)}, bf16[16,1,72,128]{3,2,1,0:T(8,128)(2,1)S(1)}, u32[]{:S(2)}, u32[]{:S(2)}) collective-permute-start(bf16[16,1,72,128]{3,2,1,0:T(8,128)(2,1)S(1)} %bitcast.132), channel_id=1, source_target_pairs={{0,4},{2,6},{4,0},{6,2},{1,5},{3,7},{5,1},{7,3},{8,12},{10,14},{12... | collective-permute-start | bytes 884744 | tf_op jit(solution)/shard_map/ppermute | solution.py:23
  34.3 1.3 broadcast_select_fusion.6
  35.6 2.7 %collective-permute-start.13 = (bf16[36,128]{1,0:T(8,128)(2,1)}, bf16[36,128]{1,0:T(8,128)(2,1)S(1)}, u32[]{:S(2)}, u32[]{:S(2)}) collective-permute-start(bf16[36,128]{1,0:T(8,128)(2,1)} %broadcast_select_fusion.6), channel_id=1, source_target_pairs={{0,1},{1,0},{2,3},{3,2},{4,5},{5,4},{6,7},{7,6},{8,9},{9,8},{10,11... | collective-permute-start | bytes 27656 | tf_op jit(solution)/shard_map/ppermute | solution.py:18
  38.6 6.2 %collective-permute-done.2 = bf16[16,1,72,128]{3,2,1,0:T(8,128)(2,1)} collective-permute-done((bf16[16,1,72,128]{3,2,1,0:T(8,128)(2,1)S(1)}, bf16[16,1,72,128]{3,2,1,0:T(8,128)(2,1)}, u32[]{:S(2)}, u32[]{:S(2)}) %collective-permute-start.2) | collective-permute-done | bytes 294944 | tf_op jit(solution)/shard_map/ppermute | solution.py:23
  45.9 2.3 %collective-permute-start.4 = (bf16[4608,128]{1,0:T(8,128)(2,1)S(1)}, bf16[4608,128]{1,0:T(8,128)(2,1)S(1)}, u32[]{:S(2)}, u32[]{:S(2)}) collective-permute-start(bf16[4608,128]{1,0:T(8,128)(2,1)S(1)} %bitcast.123), channel_id=1, source_target_pairs={{0,1},{1,0},{2,3},{3,2},{4,5},{5,4},{6,7},{7,6},{8,9},{9,8},{10,11... | collective-permute-start | bytes 3538952 | tf_op jit(solution)/shard_map/ppermute | solution.py:18
  56.8 3.0 %collective-permute-start.7 = (bf16[1152,128]{1,0:T(8,128)(2,1)S(1)}, bf16[1152,128]{1,0:T(8,128)(2,1)S(1)}, u32[]{:S(2)}, u32[]{:S(2)}) collective-permute-start(bf16[1152,128]{1,0:T(8,128)(2,1)S(1)} %add_convert_fusion.3), channel_id=1, source_target_pairs={{0,4},{2,6},{4,0},{6,2},{1,5},{3,7},{5,1},{7,3},{8,12},{10,14},{12... | collective-permute-start | bytes 884744 | tf_op jit(solution)/shard_map/ppermute | solution.py:23
  60.9 2.7 %collective-permute-start.11 = (bf16[1152,128]{1,0:T(8,128)(2,1)S(1)}, bf16[1152,128]{1,0:T(8,128)(2,1)S(1)}, u32[]{:S(2)}, u32[]{:S(2)}) collective-permute-start(bf16[1152,128]{1,0:T(8,128)(2,1)S(1)} %add_convert_fusion.1), channel_id=1, source_target_pairs={{0,6},{2,0},{4,2},{6,4},{1,7},{3,1},{5,3},{7,5},{8,14},{10,8},{12,... | collective-permute-start | bytes 884744 | tf_op jit(solution)/shard_map/ppermute | solution.py:23
  64.1 2.7 %collective-permute-done.7 = bf16[1152,128]{1,0:T(8,128)(2,1)S(1)} collective-permute-done((bf16[1152,128]{1,0:T(8,128)(2,1)S(1)}, bf16[1152,128]{1,0:T(8,128)(2,1)S(1)}, u32[]{:S(2)}, u32[]{:S(2)}) %collective-permute-start.7) | collective-permute-done | bytes 294944 | tf_op jit(solution)/shard_map/ppermute | solution.py:23
  66.8 6.9 %collective-permute-done.9 = bf16[1152,128]{1,0:T(8,128)(2,1)S(1)} collective-permute-done((bf16[1152,128]{1,0:T(8,128)(2,1)S(1)}, bf16[1152,128]{1,0:T(8,128)(2,1)S(1)}, u32[]{:S(2)}, u32[]{:S(2)}) %collective-permute-start.9) | collective-permute-done | bytes 294944 | tf_op jit(solution)/shard_map/ppermute | solution.py:23
  74.6 3.6 %all-to-all-start.1 = ((bf16[16,72,128]{2,1,0:T(8,128)(2,1)}), bf16[16,72,128]{2,1,0:T(8,128)(2,1)S(1)}, u32[]{:S(2)}, u32[]{:S(2)}) async-start(bf16[16,72,128]{2,1,0:T(8,128)(2,1)} %bitcast.16), calls=%async_computation.1 | async-start | bytes 589824 | tf_op jit(solution)/shard_map/all_to_all | solution.py:143
  78.2 1.9 %constant_dynamic-slice_fusion.3 = bf16[2304,128]{1,0:T(8,128)(2,1)} fusion(bf16[4608,128]{1,0:T(8,128)(2,1)} %bitcast.126, s32[]{:T(128)S(6)} %select_n.95), kind=kLoop, calls=%fused_computation.137 | loop fusion | bytes 1179652 | tf_op jit(solution)/shard_map/dynamic_slice | solution.py:147
  80.8 8.9 %all-to-all-done.1 = bf16[16,72,128]{2,1,0:T(8,128)(2,1)S(1)} async-done(((bf16[16,72,128]{2,1,0:T(8,128)(2,1)}), bf16[16,72,128]{2,1,0:T(8,128)(2,1)S(1)}, u32[]{:S(2)}, u32[]{:S(2)}) %all-to-all-start.1) | async-done | bytes 294944 | tf_op jit(solution)/shard_map/all_to_all | solution.py:143
  91.1 3.8 %all-to-all-start.2 = ((bf16[16,72,128]{2,1,0:T(8,128)(2,1)}), bf16[16,72,128]{2,1,0:T(8,128)(2,1)S(1)}, u32[]{:S(2)}, u32[]{:S(2)}) async-start(bf16[16,72,128]{2,1,0:T(8,128)(2,1)} %broadcast_in_dim.53), calls=%async_computation.2 | async-start | bytes 589824 | tf_op jit(solution)/shard_map/all_to_all | solution.py:50
  95.3 1.1 constant_dynamic-slice_fusion.2
  97.3 9.1 %all-to-all-done.2 = bf16[16,72,128]{2,1,0:T(8,128)(2,1)S(1)} async-done(((bf16[16,72,128]{2,1,0:T(8,128)(2,1)}), bf16[16,72,128]{2,1,0:T(8,128)(2,1)S(1)}, u32[]{:S(2)}, u32[]{:S(2)}) %all-to-all-start.2) | async-done | bytes 294944 | tf_op jit(solution)/shard_map/all_to_all | solution.py:50
  106.4 2.9 %collective-permute-start.19 = (bf16[16,72,128]{2,1,0:T(8,128)(2,1)S(1)}, bf16[16,72,128]{2,1,0:T(8,128)(2,1)S(1)}, u32[]{:S(2)}, u32[]{:S(2)}) collective-permute-start(bf16[16,72,128]{2,1,0:T(8,128)(2,1)S(1)} %all-to-all-done.2), channel_id=1, source_target_pairs={{0,2},{2,4},{4,6},{6,0},{1,3},{3,5},{5,7},{7,1},{8,10},{10,12},{12... | collective-permute-start | bytes 884744 | tf_op jit(solution)/shard_map/ppermute | solution.py:23
  110.3 1.2 collective-permute-start.15
  112.2 4.4 %collective-permute-start.14 = (bf16[36,128]{1,0:T(8,128)(2,1)S(1)}, bf16[36,128]{1,0:T(8,128)(2,1)S(1)}, u32[]{:S(2)}, u32[]{:S(2)}) collective-permute-start(bf16[36,128]{1,0:T(8,128)(2,1)S(1)} %broadcast_select_fusion.2), channel_id=1, source_target_pairs={{0,1},{1,0},{2,3},{3,2},{4,5},{5,4},{6,7},{7,6},{8,9},{9,8},{10,11... | collective-permute-start | bytes 27656 | tf_op jit(solution)/shard_map/ppermute | solution.py:18
  119.1 1.2 constant_dynamic-update-slice_fusion.5
  121.0 1.1 collective-permute-start.21
  122.2 3.6 %collective-permute-start.16 = (bf16[1152,128]{1,0:T(8,128)(2,1)S(1)}, bf16[1152,128]{1,0:T(8,128)(2,1)S(1)}, u32[]{:S(2)}, u32[]{:S(2)}) collective-permute-start(bf16[1152,128]{1,0:T(8,128)(2,1)S(1)} %bitcast.140), channel_id=1, source_target_pairs={{0,1},{1,0},{2,3},{3,2},{4,5},{5,4},{6,7},{7,6},{8,9},{9,8},{10,11... | collective-permute-start | bytes 884744 | tf_op jit(solution)/shard_map/ppermute | solution.py:18
  127.9 1.8 %collective-permute-start.28 = (bf16[8,72,128]{2,1,0:T(8,128)(2,1)S(1)}, bf16[8,72,128]{2,1,0:T(8,128)(2,1)S(1)}, u32[]{:S(2)}, u32[]{:S(2)}) collective-permute-start(bf16[8,72,128]{2,1,0:T(8,128)(2,1)S(1)} %collective-permute-done.22), channel_id=1, source_target_pairs={{0,6},{2,0},{4,2},{6,4},{1,7},{3,1},{5,3},{7,5},{8,14},{10,8},{12,... | collective-permute-start | bytes 442376 | tf_op jit(solution)/shard_map/ppermute | solution.py:23
  131.9 3.6 %collective-permute-done.25 = bf16[288,256]{1,0:T(8,128)(2,1)S(1)} collective-permute-done((bf16[288,256]{1,0:T(8,128)(2,1)S(1)}, bf16[288,256]{1,0:T(8,128)(2,1)S(1)}, u32[]{:S(2)}, u32[]{:S(2)}) %collective-permute-start.25) | collective-permute-done | bytes 147488 | tf_op jit(solution)/shard_map/ppermute | solution.py:18
  135.5 1.6 %convolution_add_fusion.1 = bf16[2304,288]{0,1:T(8,128)(2,1)} fusion(f32[2304,288]{0,1:T(8,128)S(1)} %fusion.84, bf16[2304,256]{1,0:T(8,128)(2,1)S(1)} %constant_dynamic-update-slice_fusion.4, bf16[288,256]{1,0:T(8,128)(2,1)S(1)} %collective-permute-done.25, bf16[3,288,256]{2,1,0:T(8,128)(2,1)S(1)} %copy-done.9), kind=kOutput, calls=%fused_computation.1 | convolution fusion | flops 341360640 | bytes 5455872 | tf_op jit(solution)/shard_map/dot_general | solution.py:65
  137.1 3.0 %collective-permute-done.26 = bf16[8,72,128]{2,1,0:T(8,128)(2,1)S(1)} collective-permute-done((bf16[8,72,128]{2,1,0:T(8,128)(2,1)S(1)}, bf16[8,72,128]{2,1,0:T(8,128)(2,1)S(1)}, u32[]{:S(2)}, u32[]{:S(2)}) %collective-permute-start.26) | collective-permute-done | bytes 147488 | tf_op jit(solution)/shard_map/ppermute | solution.py:23
  141.5 1.6 %fusion = bf16[2304,288]{0,1:T(8,128)(2,1)} fusion(f32[2304,288]{0,1:T(8,128)S(1)} %fusion.85, bf16[2304,256]{1,0:T(8,128)(2,1)S(1)} %constant_dynamic-update-slice_fusion.4, bf16[288,256]{1,0:T(8,128)(2,1)S(1)} %collective-permute-done.25, bf16[3,288,256]{2,1,0:T(8,128)(2,1)S(1)} %copy-done.9), kind=kOutput, calls=%fused_computation.2 | convolution fusion | flops 341360640 | bytes 5455872 | tf_op jit(solution)/shard_map/dot_general | solution.py:65
  143.1 2.0 %convolution_convert_fusion = bf16[288,2304]{1,0:T(8,128)(2,1)} fusion(bf16[2304,128]{1,0:T(8,128)(2,1)S(1)} %collective-permute-done.29, bf16[2304,128]{1,0:T(8,128)(2,1)S(1)} %bitcast.136, bf16[2304,256]{1,0:T(8,128)(2,1)S(1)} %bitcast.130, bf16[288,256]{1,0:T(8,128)(2,1)S(1)} %copy-done.21, bf16[288,128]{1,0:T(8,128)(2,1)S(1)} %copy-done.24, ...), kind=kOutput, calls=%fused_computation.3 | convolution fusion | flops 688103424 | bytes 3981312 | tf_op jit(solution)/shard_map/dot_general | solution.py:65
  (150 shorter events, 30.2 us)
Async XLA Ops:
  1.5 4.1 %collective-permute-start = (bf16[36,128]{1,0:T(8,128)(2,1)S(1)}, bf16[36,128]{1,0:T(8,128)(2,1)S(1)}, u32[]{:S(2)}, u32[]{:S(2)}) collective-permute-start(bf16[36,128]{1,0:T(8,128)(2,1)S(1)} %broadcast_select_fusion.10), channel_id=1, source_target_pairs={{0,1},{1,0},{2,3},{3,2},{4,5},{5,4},{6,7},{7,6},{8,9},{9,8},{10,11... | collective-permute-start | bytes 27656 | tf_op jit(solution)/shard_map/ppermute | solution.py:18
  7.1 22.2 %all-to-all-start = ((bf16[16,72,128]{2,1,0:T(8,128)(2,1)}), bf16[16,72,128]{2,1,0:T(8,128)(2,1)S(1)}, u32[]{:S(2)}, u32[]{:S(2)}) async-start(bf16[16,72,128]{2,1,0:T(8,128)(2,1)} %broadcast_in_dim.24), calls=%async_computation | async-start | bytes 589824 | tf_op jit(solution)/shard_map/all_to_all | solution.py:50
  29.3 9.0 %collective-permute-start.1 = (bf16[16,1,72,128]{3,2,1,0:T(8,128)(2,1)S(1)}, bf16[16,1,72,128]{3,2,1,0:T(8,128)(2,1)S(1)}, u32[]{:S(2)}, u32[]{:S(2)}) collective-permute-start(bf16[16,1,72,128]{3,2,1,0:T(8,128)(2,1)S(1)} %bitcast.131), channel_id=1, source_target_pairs={{0,2},{2,4},{4,6},{6,0},{1,3},{3,5},{5,7},{7,1},{8,10},{10,12},{12... | collective-permute-start | bytes 884744 | tf_op jit(solution)/shard_map/ppermute | solution.py:23
  30.6 15.2 %collective-permute-start.3 = (bf16[16,1,72,128]{3,2,1,0:T(8,128)(2,1)S(1)}, bf16[16,1,72,128]{3,2,1,0:T(8,128)(2,1)S(1)}, u32[]{:S(2)}, u32[]{:S(2)}) collective-permute-start(bf16[16,1,72,128]{3,2,1,0:T(8,128)(2,1)S(1)} %bitcast.132), channel_id=1, source_target_pairs={{0,4},{2,6},{4,0},{6,2},{1,5},{3,7},{5,1},{7,3},{8,12},{10,14},{12... | collective-permute-start | bytes 884744 | tf_op jit(solution)/shard_map/ppermute | solution.py:23
  33.2 11.6 %collective-permute-start.2 = (bf16[16,1,72,128]{3,2,1,0:T(8,128)(2,1)S(1)}, bf16[16,1,72,128]{3,2,1,0:T(8,128)(2,1)}, u32[]{:S(2)}, u32[]{:S(2)}) collective-permute-start(bf16[16,1,72,128]{3,2,1,0:T(8,128)(2,1)S(1)} %bitcast.133), channel_id=1, source_target_pairs={{0,6},{2,0},{4,2},{6,4},{1,7},{3,1},{5,3},{7,5},{8,14},{10,8},{12,... | collective-permute-start | bytes 884744 | tf_op jit(solution)/shard_map/ppermute | solution.py:23
  35.6 12.6 %collective-permute-start.13 = (bf16[36,128]{1,0:T(8,128)(2,1)}, bf16[36,128]{1,0:T(8,128)(2,1)S(1)}, u32[]{:S(2)}, u32[]{:S(2)}) collective-permute-start(bf16[36,128]{1,0:T(8,128)(2,1)} %broadcast_select_fusion.6), channel_id=1, source_target_pairs={{0,1},{1,0},{2,3},{3,2},{4,5},{5,4},{6,7},{7,6},{8,9},{9,8},{10,11... | collective-permute-start | bytes 27656 | tf_op jit(solution)/shard_map/ppermute | solution.py:18
  45.9 5.4 %collective-permute-start.4 = (bf16[4608,128]{1,0:T(8,128)(2,1)S(1)}, bf16[4608,128]{1,0:T(8,128)(2,1)S(1)}, u32[]{:S(2)}, u32[]{:S(2)}) collective-permute-start(bf16[4608,128]{1,0:T(8,128)(2,1)S(1)} %bitcast.123), channel_id=1, source_target_pairs={{0,1},{1,0},{2,3},{3,2},{4,5},{5,4},{6,7},{7,6},{8,9},{9,8},{10,11... | collective-permute-start | bytes 3538952 | tf_op jit(solution)/shard_map/ppermute | solution.py:18
  54.2 2.2 %collective-permute-start.6 = (bf16[1152,128]{1,0:T(8,128)(2,1)S(1)}, bf16[1152,128]{1,0:T(8,128)(2,1)S(1)}, u32[]{:S(2)}, u32[]{:S(2)}) collective-permute-start(bf16[1152,128]{1,0:T(8,128)(2,1)S(1)} %convolution_convert_fusion.3), channel_id=1, source_target_pairs={{0,1},{1,0},{2,3},{3,2},{4,5},{5,4},{6,7},{7,6},{8,9},{9,8},{10,11... | collective-permute-start | bytes 884744 | tf_op jit(solution)/shard_map/ppermute | solution.py:18
  54.7 5.0 %collective-permute-start.8 = (bf16[1152,128]{1,0:T(8,128)(2,1)S(1)}, bf16[1152,128]{1,0:T(8,128)(2,1)S(1)}, u32[]{:S(2)}, u32[]{:S(2)}) collective-permute-start(bf16[1152,128]{1,0:T(8,128)(2,1)S(1)} %convolution_convert_fusion.2), channel_id=1, source_target_pairs={{0,1},{1,0},{2,3},{3,2},{4,5},{5,4},{6,7},{7,6},{8,9},{9,8},{10,11... | collective-permute-start | bytes 884744 | tf_op jit(solution)/shard_map/ppermute | solution.py:18
  55.8 8.4 %collective-permute-start.5 = (bf16[1152,128]{1,0:T(8,128)(2,1)S(1)}, bf16[1152,128]{1,0:T(8,128)(2,1)S(1)}, u32[]{:S(2)}, u32[]{:S(2)}) collective-permute-start(bf16[1152,128]{1,0:T(8,128)(2,1)S(1)} %convolution_convert_fusion.4), channel_id=1, source_target_pairs={{0,1},{1,0},{2,3},{3,2},{4,5},{5,4},{6,7},{7,6},{8,9},{9,8},{10,11... | collective-permute-start | bytes 884744 | tf_op jit(solution)/shard_map/ppermute | solution.py:18
  55.9 4.5 %collective-permute-start.10 = (bf16[1152,128]{1,0:T(8,128)(2,1)S(1)}, bf16[1152,128]{1,0:T(8,128)(2,1)S(1)}, u32[]{:S(2)}, u32[]{:S(2)}) collective-permute-start(bf16[1152,128]{1,0:T(8,128)(2,1)S(1)} %convolution_convert_fusion.1), channel_id=1, source_target_pairs={{0,1},{1,0},{2,3},{3,2},{4,5},{5,4},{6,7},{7,6},{8,9},{9,8},{10,11... | collective-permute-start | bytes 884744 | tf_op jit(solution)/shard_map/ppermute | solution.py:18
  56.8 10.0 %collective-permute-start.7 = (bf16[1152,128]{1,0:T(8,128)(2,1)S(1)}, bf16[1152,128]{1,0:T(8,128)(2,1)S(1)}, u32[]{:S(2)}, u32[]{:S(2)}) collective-permute-start(bf16[1152,128]{1,0:T(8,128)(2,1)S(1)} %add_convert_fusion.3), channel_id=1, source_target_pairs={{0,4},{2,6},{4,0},{6,2},{1,5},{3,7},{5,1},{7,3},{8,12},{10,14},{12... | collective-permute-start | bytes 884744 | tf_op jit(solution)/shard_map/ppermute | solution.py:23
  60.2 13.4 %collective-permute-start.9 = (bf16[1152,128]{1,0:T(8,128)(2,1)S(1)}, bf16[1152,128]{1,0:T(8,128)(2,1)S(1)}, u32[]{:S(2)}, u32[]{:S(2)}) collective-permute-start(bf16[1152,128]{1,0:T(8,128)(2,1)S(1)} %add_convert_fusion.2), channel_id=1, source_target_pairs={{0,2},{2,4},{4,6},{6,0},{1,3},{3,5},{5,7},{7,1},{8,10},{10,12},{12... | collective-permute-start | bytes 884744 | tf_op jit(solution)/shard_map/ppermute | solution.py:23
  60.9 12.8 %collective-permute-start.11 = (bf16[1152,128]{1,0:T(8,128)(2,1)S(1)}, bf16[1152,128]{1,0:T(8,128)(2,1)S(1)}, u32[]{:S(2)}, u32[]{:S(2)}) collective-permute-start(bf16[1152,128]{1,0:T(8,128)(2,1)S(1)} %add_convert_fusion.1), channel_id=1, source_target_pairs={{0,6},{2,0},{4,2},{6,4},{1,7},{3,1},{5,3},{7,5},{8,14},{10,8},{12,... | collective-permute-start | bytes 884744 | tf_op jit(solution)/shard_map/ppermute | solution.py:23
  63.7 10.8 %collective-permute-start.12 = (bf16[3,288,256]{2,1,0:T(8,128)(2,1)S(1)}, bf16[3,288,256]{2,1,0:T(8,128)(2,1)S(1)}, u32[]{:S(2)}, u32[]{:S(2)}) collective-permute-start(bf16[3,288,256]{2,1,0:T(8,128)(2,1)S(1)} %pad_maximum_fusion), channel_id=1, source_target_pairs={{0,128},{128,0},{1,129},{129,1},{2,130},{130,2},{3,131},{131,3},{4... | collective-permute-start | bytes 1327112 | tf_op jit(solution)/shard_map/ppermute | solution.py:18
  74.6 15.1 %all-to-all-start.1 = ((bf16[16,72,128]{2,1,0:T(8,128)(2,1)}), bf16[16,72,128]{2,1,0:T(8,128)(2,1)S(1)}, u32[]{:S(2)}, u32[]{:S(2)}) async-start(bf16[16,72,128]{2,1,0:T(8,128)(2,1)} %bitcast.16), calls=%async_computation.1 | async-start | bytes 589824 | tf_op jit(solution)/shard_map/all_to_all | solution.py:143
  91.1 15.3 %all-to-all-start.2 = ((bf16[16,72,128]{2,1,0:T(8,128)(2,1)}), bf16[16,72,128]{2,1,0:T(8,128)(2,1)S(1)}, u32[]{:S(2)}, u32[]{:S(2)}) async-start(bf16[16,72,128]{2,1,0:T(8,128)(2,1)} %broadcast_in_dim.53), calls=%async_computation.2 | async-start | bytes 589824 | tf_op jit(solution)/shard_map/all_to_all | solution.py:50
  94.9 23.5 %collective-permute-start.23 = (bf16[2304,128]{1,0:T(8,128)(2,1)}, bf16[2304,128]{1,0:T(8,128)(2,1)}, u32[]{:S(2)}, u32[]{:S(2)}) collective-permute-start(bf16[2304,128]{1,0:T(8,128)(2,1)} %constant_dynamic-slice_fusion.3), channel_id=1, source_target_pairs={{0,128},{128,0},{1,129},{129,1},{2,130},{130,2},{3,131},{131,3},{4... | collective-permute-start | bytes 1769480 | tf_op jit(solution)/shard_map/ppermute | solution.py:18
  106.4 14.6 %collective-permute-start.19 = (bf16[16,72,128]{2,1,0:T(8,128)(2,1)S(1)}, bf16[16,72,128]{2,1,0:T(8,128)(2,1)S(1)}, u32[]{:S(2)}, u32[]{:S(2)}) collective-permute-start(bf16[16,72,128]{2,1,0:T(8,128)(2,1)S(1)} %all-to-all-done.2), channel_id=1, source_target_pairs={{0,2},{2,4},{4,6},{6,0},{1,3},{3,5},{5,7},{7,1},{8,10},{10,12},{12... | collective-permute-start | bytes 884744 | tf_op jit(solution)/shard_map/ppermute | solution.py:23
  109.3 12.8 %collective-permute-start.17 = (bf16[16,72,128]{2,1,0:T(8,128)(2,1)S(1)}, bf16[16,72,128]{2,1,0:T(8,128)(2,1)S(1)}, u32[]{:S(2)}, u32[]{:S(2)}) collective-permute-start(bf16[16,72,128]{2,1,0:T(8,128)(2,1)S(1)} %all-to-all-done.2), channel_id=1, source_target_pairs={{0,6},{2,0},{4,2},{6,4},{1,7},{3,1},{5,3},{7,5},{8,14},{10,8},{12,... | collective-permute-start | bytes 884744 | tf_op jit(solution)/shard_map/ppermute | solution.py:23
  110.3 11.9 %collective-permute-start.15 = (bf16[16,72,128]{2,1,0:T(8,128)(2,1)S(1)}, bf16[16,72,128]{2,1,0:T(8,128)(2,1)S(1)}, u32[]{:S(2)}, u32[]{:S(2)}) collective-permute-start(bf16[16,72,128]{2,1,0:T(8,128)(2,1)S(1)} %all-to-all-done.2), channel_id=1, source_target_pairs={{0,4},{2,6},{4,0},{6,2},{1,5},{3,7},{5,1},{7,3},{8,12},{10,14},{12... | collective-permute-start | bytes 884744 | tf_op jit(solution)/shard_map/ppermute | solution.py:23
  112.2 5.2 %collective-permute-start.14 = (bf16[36,128]{1,0:T(8,128)(2,1)S(1)}, bf16[36,128]{1,0:T(8,128)(2,1)S(1)}, u32[]{:S(2)}, u32[]{:S(2)}) collective-permute-start(bf16[36,128]{1,0:T(8,128)(2,1)S(1)} %broadcast_select_fusion.2), channel_id=1, source_target_pairs={{0,1},{1,0},{2,3},{3,2},{4,5},{5,4},{6,7},{7,6},{8,9},{9,8},{10,11... | collective-permute-start | bytes 27656 | tf_op jit(solution)/shard_map/ppermute | solution.py:18
  117.5 10.4 %collective-permute-start.22 = (bf16[8,72,128]{2,1,0:T(8,128)(2,1)S(1)}, bf16[8,72,128]{2,1,0:T(8,128)(2,1)S(1)}, u32[]{:S(2)}, u32[]{:S(2)}) collective-permute-start(bf16[8,72,128]{2,1,0:T(8,128)(2,1)S(1)} %constant_dynamic-slice_fusion), channel_id=1, source_target_pairs={{0,128},{128,0},{1,129},{129,1},{2,130},{130,2},{3,131},{131,3},{4... | collective-permute-start | bytes 442376 | tf_op jit(solution)/shard_map/ppermute | solution.py:18
  120.3 11.5 %collective-permute-start.24 = (bf16[2304,128]{1,0:T(8,128)(2,1)}, bf16[2304,128]{1,0:T(8,128)(2,1)S(1)}, u32[]{:S(2)}, u32[]{:S(2)}) collective-permute-start(bf16[2304,128]{1,0:T(8,128)(2,1)} %collective-permute-done.23), channel_id=1, source_target_pairs={{0,1},{1,0},{2,3},{3,2},{4,5},{5,4},{6,7},{7,6},{8,9},{9,8},{10,11... | collective-permute-start | bytes 1769480 | tf_op jit(solution)/shard_map/ppermute | solution.py:18
  121.0 4.9 %collective-permute-start.21 = (bf16[1152,128]{1,0:T(8,128)(2,1)S(1)}, bf16[1152,128]{1,0:T(8,128)(2,1)S(1)}, u32[]{:S(2)}, u32[]{:S(2)}) collective-permute-start(bf16[1152,128]{1,0:T(8,128)(2,1)S(1)} %bitcast.138), channel_id=1, source_target_pairs={{0,1},{1,0},{2,3},{3,2},{4,5},{5,4},{6,7},{7,6},{8,9},{9,8},{10,11... | collective-permute-start | bytes 884744 | tf_op jit(solution)/shard_map/ppermute | solution.py:18
  122.2 4.2 %collective-permute-start.18 = (bf16[1152,128]{1,0:T(8,128)(2,1)S(1)}, bf16[1152,128]{1,0:T(8,128)(2,1)S(1)}, u32[]{:S(2)}, u32[]{:S(2)}) collective-permute-start(bf16[1152,128]{1,0:T(8,128)(2,1)S(1)} %bitcast.142), channel_id=1, source_target_pairs={{0,1},{1,0},{2,3},{3,2},{4,5},{5,4},{6,7},{7,6},{8,9},{9,8},{10,11... | collective-permute-start | bytes 884744 | tf_op jit(solution)/shard_map/ppermute | solution.py:18
  122.2 4.8 %collective-permute-start.16 = (bf16[1152,128]{1,0:T(8,128)(2,1)S(1)}, bf16[1152,128]{1,0:T(8,128)(2,1)S(1)}, u32[]{:S(2)}, u32[]{:S(2)}) collective-permute-start(bf16[1152,128]{1,0:T(8,128)(2,1)S(1)} %bitcast.140), channel_id=1, source_target_pairs={{0,1},{1,0},{2,3},{3,2},{4,5},{5,4},{6,7},{7,6},{8,9},{9,8},{10,11... | collective-permute-start | bytes 884744 | tf_op jit(solution)/shard_map/ppermute | solution.py:18
  127.9 9.2 %collective-permute-start.28 = (bf16[8,72,128]{2,1,0:T(8,128)(2,1)S(1)}, bf16[8,72,128]{2,1,0:T(8,128)(2,1)S(1)}, u32[]{:S(2)}, u32[]{:S(2)}) collective-permute-start(bf16[8,72,128]{2,1,0:T(8,128)(2,1)S(1)} %collective-permute-done.22), channel_id=1, source_target_pairs={{0,6},{2,0},{4,2},{6,4},{1,7},{3,1},{5,3},{7,5},{8,14},{10,8},{12,... | collective-permute-start | bytes 442376 | tf_op jit(solution)/shard_map/ppermute | solution.py:23
  129.7 7.4 %collective-permute-start.27 = (bf16[8,72,128]{2,1,0:T(8,128)(2,1)S(1)}, bf16[8,72,128]{2,1,0:T(8,128)(2,1)S(1)}, u32[]{:S(2)}, u32[]{:S(2)}) collective-permute-start(bf16[8,72,128]{2,1,0:T(8,128)(2,1)S(1)} %collective-permute-done.22), channel_id=1, source_target_pairs={{0,4},{2,6},{4,0},{6,2},{1,5},{3,7},{5,1},{7,3},{8,12},{10,14},{12... | collective-permute-start | bytes 442376 | tf_op jit(solution)/shard_map/ppermute | solution.py:23
  130.6 9.5 %collective-permute-start.26 = (bf16[8,72,128]{2,1,0:T(8,128)(2,1)S(1)}, bf16[8,72,128]{2,1,0:T(8,128)(2,1)S(1)}, u32[]{:S(2)}, u32[]{:S(2)}) collective-permute-start(bf16[8,72,128]{2,1,0:T(8,128)(2,1)S(1)} %collective-permute-done.22), channel_id=1, source_target_pairs={{0,2},{2,4},{4,6},{6,0},{1,3},{3,5},{5,7},{7,1},{8,10},{10,12},{12... | collective-permute-start | bytes 442376 | tf_op jit(solution)/shard_map/ppermute | solution.py:23
  130.6 4.8 %collective-permute-start.25 = (bf16[288,256]{1,0:T(8,128)(2,1)S(1)}, bf16[288,256]{1,0:T(8,128)(2,1)S(1)}, u32[]{:S(2)}, u32[]{:S(2)}) collective-permute-start(bf16[288,256]{1,0:T(8,128)(2,1)S(1)} %get-tuple-element.68), channel_id=1, source_target_pairs={{0,128},{128,0},{1,129},{129,1},{2,130},{130,2},{3,131},{131,3},{4... | collective-permute-start | bytes 442376 | tf_op jit(solution)/shard_map/ppermute | solution.py:18
  140.3 2.8 %collective-permute-start.29 = (bf16[2304,128]{1,0:T(8,128)(2,1)S(1)}, bf16[2304,128]{1,0:T(8,128)(2,1)S(1)}, u32[]{:S(2)}, u32[]{:S(2)}) collective-permute-start(bf16[2304,128]{1,0:T(8,128)(2,1)S(1)} %bitcast.135), channel_id=1, source_target_pairs={{0,1},{1,0},{2,3},{3,2},{4,5},{5,4},{6,7},{7,6},{8,9},{9,8},{10,11... | collective-permute-start | bytes 1769480 | tf_op jit(solution)/shard_map/ppermute | solution.py:18
  (26 other events, 196.5 us)
